TPU v7x, 32 devices: a whole 2x2x4 slice. The times are simulated.
32 devices in a mesh: groups: 2 (over y), pts: 4 (over z), chan: 2 (over x), lev: 2 (over core).
Axes of the slice: x: 2, y: 2, z: 4, core: 2. Of those that a mesh axis runs over, the one named last changes fastest.
Arguments:
- cot_first: float32 [100, 73728], P('chan', ('groups', 'pts', 'lev')), parts along dimension 1, may hold values from -6 to 6
- cot_second: float32 [100, 73728], P('chan', ('groups', 'pts', 'lev')), parts along dimension 1, may hold values from -6 to 6
- strength: float32 [2, 200], P(None, ('groups', 'chan')), parts along dimension 1, may hold values from 0.1 to 1
- lengths: int32 [32], P('groups'), parts along dimension 0, may hold values from 1536 to 3072, as said below
- latitude: float32 [32], P('groups'), parts along dimension 0, may hold values from -0.5 to 0.5
- weights: float32 [32], P('groups'), parts along dimension 0, may hold values from 0.0625 to 0.25
Outputs:
- grad_state: float32 [100, 73728], P('chan', ('groups', 'pts', 'lev')), parts along dimension 1
- grad_target: float32 [2, 200, 2, 64, 64], P(None, ('groups', 'chan'), None, ('pts', 'lev')), parts along dimension 1
There are 2 independent parts, one for each index of `groups`. A program takes and returns all parts, laid end to end along the dimension named above; each array names one. Nothing has to cross between parts.
Inputs may be any that keep to these rules, and one draw needn't show every extreme that they name: Every length is a multiple of 4, and the lengths sum to 36864.
All inputs are finite; a program needn't handle non-finite values.
Results may differ from a plain program's by a relative error of at most 0.0003.
Values sent between devices are 32-bit elements; how exact they have to be, the bound alone decides.
No kernel may reach another device: no remote copies, remote signals or barrier semaphores. Data moves between devices by JAX's collectives and lax.ppermute only.
A program may use at most 128 MiB of HBM per device.

v0:
```python
import math

import jax
import jax.numpy as jnp
from jax import lax
from jax.sharding import PartitionSpec as P

MAXLEN = 3072
WAVES = 64
ROWS_DEV = 2


HIGHEST = lax.Precision.HIGHEST


def passed_along(shard, axis, by):
    count = lax.axis_size(axis)
    pairs = [(i, i + by) for i in range(count) if 0 <= i + by < count]
    return lax.ppermute(shard, axis, pairs)


def order_factors(wave_count):
    running = 0.0
    values = [0.0]
    for step_id in range(1, wave_count):
        running = running + 0.5 * math.log((2.0 * step_id + 1.0) / (2.0 * step_id))
        values.append(running)
    return values


def legendre(latitude_rows, orders, wave_count):
    log_factors = jnp.asarray(order_factors(wave_count), jnp.float32)
    order_scale = jnp.sum(
        jnp.where(orders[:, None] == jnp.arange(wave_count)[None, :], log_factors[None, :], 0.0),
        axis=1,
    )
    order_value = orders.astype(jnp.float32)[None, :]
    sine_col = jnp.sqrt(1.0 - latitude_rows * latitude_rows)[:, None]
    diagonal = jnp.sqrt(0.5) * jnp.exp(order_scale[None, :] + order_value * jnp.log(sine_col))
    latitude_col = latitude_rows[:, None]
    previous = jnp.zeros_like(diagonal)
    current = jnp.zeros_like(diagonal)
    degrees = []
    for degree in range(wave_count):
        degree_f = float(degree)
        upper_term = max(4.0 * degree_f * degree_f - 1.0, 0.0)
        lower_term = jnp.maximum(degree_f * degree_f - order_value * order_value, 1.0)
        factor_upper = jnp.sqrt(upper_term / lower_term)
        factor_lower = jnp.sqrt(
            jnp.maximum((degree_f - 1.0) ** 2 - order_value * order_value, 0.0)
            / max(4.0 * (degree_f - 1.0) ** 2 - 1.0, 1.0)
        )
        recurrence = factor_upper * (latitude_col * current - factor_lower * previous)
        degree_value = jnp.where(
            order_value > degree_f, 0.0, jnp.where(order_value == degree_f, diagonal, recurrence)
        )
        previous, current = (current, degree_value)
        degrees.append(degree_value)
    return jnp.stack(degrees, axis=-1)


def row_basis(row_size, row_valid):
    point_ids = jnp.arange(MAXLEN, dtype=jnp.int32)
    wave_ids = jnp.arange(WAVES, dtype=jnp.int32)
    phase_turns = point_ids[None, :, None] * wave_ids[None, None, :] % row_size[:, None, None]
    angle_values = (
        phase_turns.astype(jnp.float32)
        * (2.0 * jnp.pi / row_size.astype(jnp.float32))[:, None, None]
    )
    inside = ((point_ids[None, :] < row_size[:, None]) & row_valid[:, None]).astype(jnp.float32)[
        :, :, None
    ]
    return jnp.concatenate(
        [jnp.cos(angle_values) * inside, jnp.sin(angle_values) * inside], axis=-1
    )


def select_rows(row_match, row_table):
    return jnp.sum(jnp.where(row_match, row_table[None, :], jnp.zeros((), row_table.dtype)), axis=1)


def slot_layout(lengths, starts, owner_id, local_pts, slot_count):
    row_total = lengths.shape[0]
    first_row = jnp.sum((starts < owner_id * local_pts).astype(jnp.int32))
    row_index = first_row + jnp.arange(slot_count, dtype=jnp.int32)
    row_match = row_index[:, None] == jnp.arange(row_total, dtype=jnp.int32)[None, :]
    row_begin = select_rows(row_match, starts)
    row_size = select_rows(row_match, lengths)
    row_valid = (row_index < row_total) & (row_begin < (owner_id + 1) * local_pts)
    row_match = row_match & row_valid[:, None]
    row_size = jnp.where(row_valid, row_size, MAXLEN)
    offset = jnp.where(row_valid, row_begin - owner_id * local_pts, 0)
    return (row_match, offset, row_size, row_valid)


def on_device(cot_first, cot_second, strength, lengths, latitude, weights):
    channels, local_pts = cot_first.shape
    slot_count = 3 * ROWS_DEV // 2
    groups = lax.axis_size(("pts", "lev"))
    owner_id = lax.axis_index(("pts", "lev"))
    wave_share = WAVES // groups
    starts = jnp.cumsum(lengths) - lengths
    row_match, offset, row_size, row_valid = slot_layout(
        lengths, starts, owner_id, local_pts, slot_count
    )
    trig_basis = row_basis(row_size, row_valid)
    row_scale = jnp.where(
        row_valid, select_rows(row_match, weights) / row_size.astype(jnp.float32), 0.0
    )
    wave_ids = jnp.arange(WAVES, dtype=jnp.int32)
    doubling = jnp.where(wave_ids == 0, 1.0, 2.0).astype(jnp.float32)
    rate_first = strength[0][:, None]
    rate_second = strength[1][:, None]

    def fourier(extended):
        row_pieces = jax.vmap(
            lambda slot_start: lax.dynamic_slice_in_dim(extended, slot_start, MAXLEN, 1)
        )(offset)
        return jnp.einsum("sci,sik->sck", row_pieces, trig_basis, precision=HIGHEST)

    def synthesis(mixed_coeff):
        values = jnp.einsum("sck,sik->sci", mixed_coeff, trig_basis, precision=HIGHEST)
        accum = jnp.zeros((channels, local_pts + MAXLEN), jnp.float32)
        for slot_id in range(slot_count):
            current = lax.dynamic_slice_in_dim(accum, offset[slot_id], MAXLEN, 1)
            accum = lax.dynamic_update_slice_in_dim(
                accum, current + values[slot_id], offset[slot_id], 1
            )
        return accum

    legendre_values = legendre(select_rows(row_match, latitude), wave_ids, WAVES)

    def spectral(coeff):
        real_part = (
            jnp.einsum("smn,scm->cmn", legendre_values, coeff[..., :WAVES], precision=HIGHEST)
            * doubling[None, :, None]
        )
        imag_part = (
            -jnp.einsum("smn,scm->cmn", legendre_values, coeff[..., WAVES:], precision=HIGHEST)
            * doubling[None, :, None]
        )
        spectrum = lax.psum(jnp.stack([real_part, imag_part], axis=1), ("pts", "lev"))
        cosine = (
            jnp.einsum("smn,cmn->scm", legendre_values, spectrum[:, 0], precision=HIGHEST)
            * row_scale[:, None, None]
        )
        sine_part = (
            -jnp.einsum("smn,cmn->scm", legendre_values, spectrum[:, 1], precision=HIGHEST)
            * row_scale[:, None, None]
        )
        mine = lax.dynamic_slice_in_dim(spectrum, owner_id * wave_share, wave_share, 2)
        return (jnp.concatenate([cosine, sine_part], axis=-1), mine)

    def extend(field_in):
        tail_points = passed_along(field_in[:, :MAXLEN], ("pts", "lev"), -1)
        return jnp.concatenate([field_in, tail_points], axis=1)

    def settle(extended):
        incoming = passed_along(extended[:, local_pts:], ("pts", "lev"), 1)
        return extended[:, :local_pts] + jnp.pad(incoming, ((0, 0), (0, local_pts - MAXLEN)))

    mixed_coeff, spec_second = spectral(fourier(extend(rate_second * cot_second)))
    carried = cot_first + cot_second - settle(synthesis(mixed_coeff))
    mixed_coeff, spec_first = spectral(fourier(extend(rate_first * carried)))
    grad_state = carried - settle(synthesis(mixed_coeff))
    scaling = float(local_pts * groups) ** (-0.5)
    grad_target = jnp.stack([spec_first, spec_second]) * scaling
    return (grad_state, grad_target)


def solution(mesh):
    return jax.shard_map(
        on_device,
        mesh=mesh,
        in_specs=(
            P("chan", ("groups", "pts", "lev")),
            P("chan", ("groups", "pts", "lev")),
            P(None, ("groups", "chan")),
            P("groups"),
            P("groups"),
            P("groups"),
        ),
        out_specs=(
            P("chan", ("groups", "pts", "lev")),
            P(None, ("groups", "chan"), None, ("pts", "lev"), None),
        ),
        check_vma=False,
    )
```

profile of v0, /device:TPU:16, one launch (start us, length us, event | category | flops | bytes accessed | tf_op | source)
XLA Modules:
  0.0 471.1 jit_solution(13872405275566522680)
XLA Ops:
  8.0 1.4 broadcast_multiply_fusion.1
  9.4 1.9 collective-permute-start
  16.4 63.3 %fusion.4 = (f32[3,3072,64]{2,1,0:T(8,128)}, f32[3,3072,64]{2,1,0:T(8,128)}) fusion(f32[3,3072]{1,0:T(4,128)S(1)} %fusion.37, f32[3]{0:T(128)S(1)} %convert_divide_fusion, s32[3]{0:T(128)S(1)} %compare_select_fusion, s32[3072,64]{1,0:T(8,128)S(1)} %iota_multiply_fusion, pred[3]{0:T(512)(128)(4,1)S(1)} %broadcast_compare_fusion), kind=kLoop, calls=%fused_computation.12 | loop fusion | flops 6488064 | bytes 5541915 | tf_op jit(solution)/shard_map/mul | solution.py:74
  79.7 1.5 select_select_fusion.24
  81.5 9.5 %select_select_fusion = (f32[3,64,1]{2,0,1:T(4,128)S(1)}, f32[3,64,1]{2,0,1:T(4,128)S(1)}, f32[3,64,1]{2,0,1:T(4,128)S(1)}, f32[3,64,1]{2,0,1:T(4,128)S(1)}, f32...) fusion(f32[64]{0:T(128)S(1)} %get-tuple-element.139, ...), kind=kLoop, calls=%fused_computation.63 | loop fusion | flops 29952 | bytes 35620 | tf_op jit(solution)/shard_map/jit(_where)/select_n | solution.py:54
  91.9 0.8 copy.2012
  95.0 0.8 copy.2016
  99.7 0.8 copy.2022
  112.0 0.8 copy.2038
  115.8 0.8 copy.2043
  116.6 0.8 copy.2044
  121.3 12.3 %stack.208 = f32[3,64,64]{2,0,1:T(4,128)S(1)} concatenate(f32[3,64,1]{2,0,1:T(4,128)} %get-tuple-element.121, f32[3,64,1]{2,0,1:T(4,128)} %get-tuple-element.120, f32[3,64,1]{2,0,1:T(4,128)} %get-tuple-element.111, f32[3,64,1]{2,0,1:T(4,128)} %get-tuple-element.110, f32[3,64,1]{2,0,1:T(4,128)} %get-tuple-element.109, f32[3,64,1]{2,0,1:T(4,128)} %get-tuple-element.108, ...), dimensions={2} | concatenate | bytes 98304 | tf_op jit(solution)/shard_map/stack | solution.py:59
  133.6 7.2 %pad_maximum_fusion = f32[3,3072,128]{2,1,0:T(8,128)} fusion(f32[3,3072,64]{2,1,0:T(8,128)} %get-tuple-element.115, f32[3,3072,64]{2,1,0:T(8,128)} %get-tuple-element.114), kind=kLoop, calls=%fused_computation.14 | loop fusion | flops 1179648 | bytes 9437184 | tf_op jit(solution)/shard_map/concatenate | solution.py:73
  140.8 1.2 pad_maximum_fusion.3
  142.0 1.5 broadcast.30613.clone
  143.5 7.4 %while.2 = (s32[]{:T(128)}, f32[50,7680]{1,0:T(8,128)S(1)}, s32[3,2]{0,1:T(2,128)S(1)}, f32[3,50,3072]{2,1,0:T(8,128)}, s32[]{:T(128)}) while((s32[]{:T(128)}, f32[50,7680]{1,0:T(8,128)S(1)}, s32[3,2]{0,1:T(2,128)S(1)}, f32[3,50,3072]{2,1,0:T(8,128)}, s32[]{:T(128)}) %tuple.238), condition=%wide.while_cond, body=%wide.while_body.sunk | while | flops 2 | bytes 1303641 | solution.py:117
  144.1 1.8 bitcast_dynamic-update-slice_fusion.4
  146.4 1.7 bitcast_dynamic-update-slice_fusion.4
  148.8 1.7 bitcast_dynamic-update-slice_fusion.4
  150.9 5.8 %fusion.239 = f32[3,50,128]{2,1,0:T(8,128)S(1)} fusion(f32[3,50,3072]{2,1,0:T(8,128)} %get-tuple-element.9, f32[3,3072,128]{2,1,0:T(8,128)} %pad_maximum_fusion), kind=kOutput, calls=%fused_computation.530 | convolution fusion | flops 707788800 | bytes 6638592 | tf_op jit(solution)/shard_map/sci,sik->sck/dot_general | solution.py:119
  157.0 3.2 multiply_bitcast_fusion.3
  160.2 3.2 multiply_bitcast_fusion.2
  163.4 2.1 pad_maximum_fusion.1
  172.4 82.0 %all-reduce.6.cloned.1.call-done = f32[50,2,64,64]{3,0,2,1:T(8,128)} async-done(((f32[50,2,64,64]{3,0,2,1:T(8,128)}), f32[50,2,64,64]{3,0,2,1:T(8,128)}) %all-reduce.6.cloned.1.call-update) | async-done | bytes 1638416 | tf_op jit(solution)/shard_map/psum | solution.py:142
  254.4 4.4 fusion.13
  258.9 4.5 fusion.16
  263.5 7.0 %fusion.28 = f32[3,50,3072]{2,1,0:T(8,128)S(1)} fusion(f32[3,3072,128]{2,1,0:T(8,128)} %pad_maximum_fusion, f32[3,50,64]{2,1,0:T(8,128)S(1)} %copy.2053, f32[3,50,64]{2,1,0:T(8,128)S(1)} %copy.2052), kind=kOutput, calls=%fused_computation.90 | convolution fusion | flops 707808000 | bytes 6638592 | tf_op jit(solution)/shard_map/sck,sik->sci/dot_general | solution.py:122
  270.6 1.2 copy-done.1
  272.0 2.4 dynamic_update_slice.18
  274.4 1.4 fusion.27
  275.7 4.0 dynamic_update_slice.19
  279.7 1.4 fusion.26
  281.1 2.9 dynamic_update_slice.20
  284.1 2.1 collective-permute-start.1
  286.1 10.3 %collective-permute-done.1 = f32[50,3072]{1,0:T(8,128)S(1)} collective-permute-done((f32[50,3072]{1,0:T(8,128)S(1)}, f32[50,3072]{1,0:T(8,128)S(1)}, u32[]{:S(2)}, u32[]{:S(2)}) %collective-permute-start.1) | collective-permute-done | bytes 614432 | tf_op jit(solution)/shard_map/ppermute | solution.py:19
  296.5 2.5 broadcast_multiply_fusion
  299.0 1.9 collective-permute-start.2
  300.9 8.4 %collective-permute-done.2 = f32[50,3072]{1,0:T(8,128)} collective-permute-done((f32[50,3072]{1,0:T(8,128)S(1)}, f32[50,3072]{1,0:T(8,128)}, u32[]{:S(2)}, u32[]{:S(2)}) %collective-permute-start.2) | collective-permute-done | bytes 614432 | tf_op jit(solution)/shard_map/ppermute | solution.py:19
  309.3 1.2 pad_maximum_fusion.4
  310.5 1.5 broadcast.30613
  312.1 7.6 %while.3 = (s32[]{:T(128)}, f32[50,7680]{1,0:T(8,128)S(1)}, s32[3,2]{0,1:T(2,128)S(1)}, f32[3,50,3072]{2,1,0:T(8,128)}, s32[]{:T(128)}) while((s32[]{:T(128)}, f32[50,7680]{1,0:T(8,128)S(1)}, s32[3,2]{0,1:T(2,128)S(1)}, f32[3,50,3072]{2,1,0:T(8,128)}, s32[]{:T(128)}) %tuple.248), condition=%wide.while_cond.1, body=%wide.while_body.1.sunk | while | flops 2 | bytes 1303641 | solution.py:117
  312.7 1.8 bitcast_dynamic-update-slice_fusion.5
  315.2 1.8 bitcast_dynamic-update-slice_fusion.5
  317.7 1.8 bitcast_dynamic-update-slice_fusion.5
  319.6 5.8 %fusion.240 = f32[3,50,128]{2,1,0:T(8,128)S(1)} fusion(f32[3,50,3072]{2,1,0:T(8,128)} %get-tuple-element.17, f32[3,3072,128]{2,1,0:T(8,128)} %pad_maximum_fusion), kind=kOutput, calls=%fused_computation.531 | convolution fusion | flops 707788800 | bytes 6638592 | tf_op jit(solution)/shard_map/sci,sik->sck/dot_general | solution.py:119
  325.6 3.2 multiply_bitcast_fusion.1
  329.0 3.2 multiply_bitcast_fusion
  332.2 2.1 pad_maximum_fusion.2
  334.2 86.5 %all-reduce.8.cloned.1.call-done = f32[50,2,64,64]{3,0,2,1:T(8,128)} async-done(((f32[50,2,64,64]{3,0,2,1:T(8,128)}), f32[50,2,64,64]{3,0,2,1:T(8,128)}) %all-reduce.8.cloned.1.call-update) | async-done | bytes 1638416 | tf_op jit(solution)/shard_map/psum | solution.py:142
  420.7 4.4 fusion.18
  425.3 4.7 %fusion.21 = f32[3,50,64]{1,0,2:T(4,128)S(1)} fusion(f32[3,64,64]{2,0,1:T(4,128)S(1)} %stack.208, f32[50,2,64,64]{3,0,2,1:T(8,128)} %all-reduce.8.cloned.1.call-done, f32[3]{0:T(128)S(1)} %get-tuple-element.42), kind=kOutput, calls=%fused_computation.43 | convolution fusion | flops 7392000 | bytes 1922572 | tf_op jit(solution)/shard_map/smn,cmn->scm/dot_general | solution.py:148
  430.1 7.0 %fusion.32 = f32[3,50,3072]{2,1,0:T(8,128)S(1)} fusion(f32[3,3072,128]{2,1,0:T(8,128)} %pad_maximum_fusion, f32[3,50,64]{2,1,0:T(8,128)S(1)} %copy.2057, f32[3,50,64]{2,1,0:T(8,128)S(1)} %copy.2056), kind=kOutput, calls=%fused_computation.94 | convolution fusion | flops 707808000 | bytes 6638592 | tf_op jit(solution)/shard_map/sck,sik->sci/dot_general | solution.py:122
  437.2 1.2 copy-done
  438.6 2.4 dynamic_update_slice.21
  440.9 1.4 fusion.25
  442.3 4.0 dynamic_update_slice.22
  446.3 1.4 fusion.24
  447.6 2.9 dynamic_update_slice.23
  450.6 1.9 collective-permute-start.3
  452.5 1.1 constant_dynamic-slice_fusion.2
  453.7 1.1 constant_dynamic-slice_fusion.3
  454.9 1.0 maximum_multiply_fusion
  455.9 7.0 %collective-permute-done.3 = f32[50,3072]{1,0:T(8,128)S(1)} collective-permute-done((f32[50,3072]{1,0:T(8,128)S(1)}, f32[50,3072]{1,0:T(8,128)S(1)}, u32[]{:S(2)}, u32[]{:S(2)}) %collective-permute-start.3) | collective-permute-done | bytes 614432 | tf_op jit(solution)/shard_map/ppermute | solution.py:19
  462.9 1.1 fusion.22
  (236 shorter events, 37.3 us)
Async XLA Ops:
  7.2 4.2 copy-start.4
  7.2 6.4 %copy-start.6 = (f32[16]{0:T(128)S(1)}, f32[16]{0:T(128)}, u32[]{:S(2)}) copy-start(f32[16]{0:T(128)} %param.11) | copy-start | bytes 196
  7.2 6.4 %copy-start.5 = (f32[16]{0:T(128)S(1)}, f32[16]{0:T(128)}, u32[]{:S(2)}) copy-start(f32[16]{0:T(128)} %param.12) | copy-start | bytes 196
  7.2 247.2 %all-reduce.6.cloned.1.call-start = ((), (), s32[]{:S(2)}) async-start(), calls=%async_computation | async-start | bytes 7340032 | tf_op jit(solution)/shard_map/psum | solution.py:142
  9.4 6.9 %copy-start.7 = (f32[64]{0:T(128)S(1)}, f32[64]{0:T(128)}, u32[]{:S(2)}) copy-start(f32[64]{0:T(128)} %constant.539.clone) | copy-start | bytes 772
  9.4 131.3 %collective-permute-start = (f32[50,3072]{1,0:T(8,128)S(1)}, f32[50,3072]{1,0:T(8,128)}, u32[]{:S(2)}, u32[]{:S(2)}) collective-permute-start(f32[50,3072]{1,0:T(8,128)S(1)} %slice.129), channel_id=1, source_target_pairs={{1,0},{4,1},{5,4},{8,5},{9,8},{12,9},{13,12},{3,2},{6,3},{7,6},{10... | collective-permute-start | bytes 1843208 | tf_op jit(solution)/shard_map/ppermute | solution.py:19
  165.6 255.1 %all-reduce.8.cloned.1.call-start = ((), (), s32[]{:S(2)}) async-start(), calls=%async_computation.1 | async-start | bytes 7340032 | tf_op jit(solution)/shard_map/psum | solution.py:142
  270.6 1.3 copy-start.1
  284.0 12.5 %copy-start.3 = (f32[50,4608]{1,0:T(8,128)S(1)}, f32[50,4608]{1,0:T(8,128)}, u32[]{:S(2)}) copy-start(f32[50,4608]{1,0:T(8,128)} %param.7) | copy-start | bytes 2764804
  284.1 12.4 %collective-permute-start.1 = (f32[50,3072]{1,0:T(8,128)S(1)}, f32[50,3072]{1,0:T(8,128)S(1)}, u32[]{:S(2)}, u32[]{:S(2)}) collective-permute-start(f32[50,3072]{1,0:T(8,128)S(1)} %slice.138), channel_id=1, source_target_pairs={{0,1},{1,4},{4,5},{5,8},{8,9},{9,12},{12,13},{2,3},{3,6},{6,7},{7,... | collective-permute-start | bytes 1843208 | tf_op jit(solution)/shard_map/ppermute | solution.py:19
  299.0 10.4 %collective-permute-start.2 = (f32[50,3072]{1,0:T(8,128)S(1)}, f32[50,3072]{1,0:T(8,128)}, u32[]{:S(2)}, u32[]{:S(2)}) collective-permute-start(f32[50,3072]{1,0:T(8,128)S(1)} %slice.139), channel_id=1, source_target_pairs={{1,0},{4,1},{5,4},{8,5},{9,8},{12,9},{13,12},{3,2},{6,3},{7,6},{10... | collective-permute-start | bytes 1843208 | tf_op jit(solution)/shard_map/ppermute | solution.py:19
  437.2 1.3 copy-start
  450.6 12.3 %collective-permute-start.3 = (f32[50,3072]{1,0:T(8,128)S(1)}, f32[50,3072]{1,0:T(8,128)S(1)}, u32[]{:S(2)}, u32[]{:S(2)}) collective-permute-start(f32[50,3072]{1,0:T(8,128)S(1)} %slice.148), channel_id=1, source_target_pairs={{0,1},{1,4},{4,5},{5,8},{8,9},{9,12},{12,13},{2,3},{3,6},{6,7},{7,... | collective-permute-start | bytes 1843208 | tf_op jit(solution)/shard_map/ppermute | solution.py:19
  453.6 9.3 %copy-start.2 = (f32[50,4608]{1,0:T(8,128)S(1)}, f32[50,4608]{1,0:T(8,128)}, u32[]{:S(2)}) copy-start(f32[50,4608]{1,0:T(8,128)} %get-tuple-element.39) | copy-start | bytes 2764804
Sparse Core Ops, SparseCore 0:
  165.7 88.6 all-reduce.5
  334.3 86.3 all-reduce.7
where the time goes:
time: 474 us; the launch traced here: 471 us
  waiting for transfers between devices  194 us (41%)
  other arithmetic  105 us (22%)
  local copies, waits for them, and re-layouts  85.5 us (18%)
  matrix products  56.5 us (12%)
  between operations  21.5 us (5%)
  starting transfers between devices  8.07 us (2%)
    psum x2, waiting for transfers between devices, spectral(): lax.psum(jnp.stack([real_part, imag_part], axis=1), ('pts', 'lev'))  168 us
    mul x1, other arithmetic, row_basis(): jnp.cos(angle_values) * inside  63.3 us
    another operation x39, local copies, waits for them, and re-layouts, legendre(): return jnp.stack(degrees, axis=-1)  41.6 us
    ppermute x4, waiting for transfers between devices, passed_along(): return lax.ppermute(shard, axis, pairs)  25.7 us
    dynamic_update_slice x6, local copies, waits for them, and re-layouts, synthesis(): lax.dynamic_update_slice_in_dim(accum, current + values[slot_id], offset[...  18.5 us
    gather x18, local copies, waits for them, and re-layouts  14.4 us
    dot_general x2, matrix products, synthesis(): jnp.einsum('sck,sik->sci', mixed_coeff, trig_basis, precision=HIGHEST)  14.1 us
    dot_general x2, matrix products, fourier(): return jnp.einsum('sci,sik->sck', row_pieces, trig_basis, precision=HIGHEST)  11.6 us
  transfers between devices with their start and end apart: 6, of which 5 were waited for; matrix products, arithmetic and copies ran while one was open for 28% of the time, Pallas kernels for 0%

commit v1 on v0

v1 whole, which is shorter than its diff:
```python
import functools
import math

import jax
import jax.numpy as jnp
import numpy as np
from jax import lax
from jax.experimental import pallas as pl
from jax.experimental.pallas import tpu as pltpu
from jax.sharding import PartitionSpec as P

MAXLEN = 3072
WAVES = 64
BLOCK = 256
LANES = 128
SHARES = 4
GROUP = WAVES // SHARES
PAD = 64
HIGHEST = lax.Precision.HIGHEST
AXES = ("pts", "lev")


def cosine_coefficients():
    nodes = np.cos(np.pi * (np.arange(64) + 0.5) / 64)
    squares = 0.12525 * (nodes + 1.0)
    fitted = np.polynomial.Polynomial.fit(squares, np.cos(2.0 * np.pi * np.sqrt(squares)), 7)
    return [float(value) for value in fitted.convert().coef]


COSINE = cosine_coefficients()


def cos_turns(turns):
    turns = turns - jnp.floor(turns + 0.5)
    square = turns * turns
    value = jnp.full_like(square, COSINE[-1])
    for coefficient in COSINE[-2::-1]:
        value = value * square + coefficient
    return value


def turns_of(wave, point, size):
    inverse = 1.0 / size
    product = wave * point
    whole = jnp.floor(product * inverse + 0.5)
    return (product - whole * size) * inverse


def lane_waves(lane, me, per_device):
    share = (lane >> 4) & 3
    within = lane & (GROUP - 1)
    shift = per_device.bit_length() - 1
    outer = within >> shift
    return per_device * (((me ^ share) & 3) + SHARES * outer) + (within & (per_device - 1))


def device_id():
    return lax.axis_index("pts") * lax.axis_size("lev") + lax.axis_index("lev")


def row_table(lengths, table, me, local, rows):
    begin = me * local
    for slot in range(SHARES):
        table[slot] = 0
        table[SHARES + slot] = MAXLEN
        table[2 * SHARES + slot] = local

    def step(row, carry):
        start, first = carry
        size = lengths[row]
        stop = start + size
        first = first + jnp.where(stop <= begin, 1, 0)

        @pl.when((stop > begin) & (start < begin + local))
        def _():
            table[row & 3] = start - begin
            table[SHARES + (row & 3)] = size
            table[2 * SHARES + row - first] = start - begin

        return stop, first

    _, first = lax.fori_loop(0, rows, step, (jnp.int32(0), jnp.int32(0)))
    table[3 * SHARES] = first


def fill_phases(table, me, per_device, blocks, cosine, sine, sign):
    rows = cosine.shape[1]
    lane = lax.broadcasted_iota(jnp.int32, (rows, LANES), 1)
    begin = BLOCK * lax.broadcasted_iota(jnp.int32, (rows, LANES), 0)
    wave = lane_waves(lane, me, per_device).astype(jnp.float32)
    signs = jnp.where(lane >= PAD, sign, -sign)
    for slot in range(SHARES):
        size = jnp.full((rows, LANES), table[SHARES + slot], jnp.int32).astype(jnp.float32)
        turns = turns_of(wave, (begin - table[slot]).astype(jnp.float32), size)
        cosine[slot] = cos_turns(turns)
        sine[slot] = cos_turns(turns - 0.25) * signs


def basis_of(wave_index, point, size_int, me, per_device):
    wave = lane_waves(wave_index, me, per_device).astype(jnp.float32)
    size = jnp.full(wave.shape, size_int, jnp.int32).astype(jnp.float32)
    turns = turns_of(wave, point.astype(jnp.float32), size)
    value = cos_turns(turns - jnp.where(wave_index >= PAD, 0.25, 0.0))
    high = value.astype(jnp.bfloat16)
    low = (value - high.astype(jnp.float32)).astype(jnp.bfloat16)
    return high, low


def column(row):
    count = row.shape[1]
    down = lax.broadcasted_iota(jnp.int32, (count, count), 0)
    across = lax.broadcasted_iota(jnp.int32, (count, count), 1)
    return jnp.sum(jnp.where(down == across, row, 0.0), axis=1, keepdims=True)


def load_fields(second, first, fields, sems, pieces):
    width = fields.shape[2] // pieces
    copies = []
    for piece in range(pieces):
        for index, source in enumerate((second, first)):
            copies.append(
                pltpu.make_async_copy(
                    source.at[:, pl.ds(piece * width, width)],
                    fields.at[index, :, pl.ds(piece * width, width)],
                    sems.at[piece, index],
                )
            )
    for copy in copies:
        copy.start()
    return copies


def analyse_kernel(per_device, lengths, strength, second, first, *refs):
    messages, (fields, basis, cosine, sine, lhs, total, table, sems) = refs[:SHARES], refs[SHARES:]
    channels, local = second.shape
    blocks = local // BLOCK
    pieces = sems.shape[0]
    copies = load_fields(second, first, fields, sems, pieces)
    me = device_id()
    row_table(lengths, table, me, local, lengths.shape[0])
    fill_phases(table, me, per_device, blocks, cosine, sine, 1.0)
    wave_index = lax.broadcasted_iota(jnp.int32, (BLOCK, LANES), 1)
    point = lax.broadcasted_iota(jnp.int32, (BLOCK, LANES), 0)
    for slot in range(SHARES):
        high, low = basis_of(wave_index, point, table[SHARES + slot], me, per_device)
        basis[slot, :, :LANES] = high
        basis[slot, :, LANES:] = low
    total[...] = jnp.zeros_like(total)
    lhs[...] = jnp.zeros_like(lhs)
    within = lax.broadcasted_iota(jnp.int32, (1, BLOCK), 1)

    def add_block(block, place, slot, low_end, high_end, buffer):
        keep = (within >= low_end) & (within < high_end)
        for index in range(2):
            piece = jnp.where(keep, fields[index, :, pl.ds(place, BLOCK)], 0.0)
            high = piece.astype(jnp.bfloat16)
            low = (piece - high.astype(jnp.float32)).astype(jnp.bfloat16)
            lhs[buffer, pl.ds(index * PAD, channels), :] = high
            lhs[buffer, pl.ds((2 + index) * PAD, channels), :] = low
        product = jnp.dot(lhs[buffer], basis[slot], preferred_element_type=jnp.float32)
        value = (
            product[: 2 * PAD, :LANES] + product[: 2 * PAD, LANES:] + product[2 * PAD :, :LANES]
        )
        turned = (
            value * cosine[slot, pl.ds(block, 1), :]
            + pltpu.roll(value, PAD, 1) * sine[slot, pl.ds(block, 1), :]
        )
        total[slot] = total[slot] + turned

    begin_slot = table[3 * SHARES]
    waited = 0
    for block in range(blocks):
        while waited * (local // pieces) < (block + 1) * BLOCK:
            copies[2 * waited].wait()
            copies[2 * waited + 1].wait()
            waited += 1
        place = block * BLOCK
        slot = begin_slot
        for later in range(1, SHARES):
            slot = slot + jnp.where(table[2 * SHARES + later] <= place, 1, 0)
        slot = slot & 3
        add_block(
            block, place, slot, 0, table[slot] + table[SHARES + slot] - place, block % lhs.shape[0]
        )
    for later in range(1, SHARES):
        begin = table[2 * SHARES + later]

        @pl.when((begin < local) & ((begin & (BLOCK - 1)) != 0))
        def _():
            block = begin >> 8
            place = pl.multiple_of(block * BLOCK, BLOCK)
            add_block(block, place, (begin_slot + later) & 3, begin & (BLOCK - 1), BLOCK, later)

    rate_first = column(strength[0:1, :])
    rate_second = column(strength[1:2, :])
    lane = lax.broadcasted_iota(jnp.int32, (1, LANES), 1)
    chunk = (lane >> 4) & 3
    pairs = []
    for slot in range(SHARES):
        value_second = total[slot, :channels, :]
        value_first = total[slot, PAD : PAD + channels, :]
        part_second = rate_second * value_second
        pairs.append((rate_first * (value_first + value_second) + part_second, part_second))
    for share in range(SHARES):
        for which in range(2):
            value = jnp.zeros((channels, LANES), jnp.float32)
            for slot in range(SHARES):
                moved = pairs[slot][which]
                if slot != share:
                    moved = pltpu.roll(moved, ((slot - share) * GROUP) % LANES, 1)
                value = jnp.where(chunk == slot, moved, value)
            messages[share][pl.ds(which * channels, channels), :] = value


def analyse(lengths, strength, second, first, per_device):
    channels, local = second.shape
    blocks = local // BLOCK
    pieces = 3
    phase_rows = -(-blocks // 8) * 8
    return pl.pallas_call(
        functools.partial(analyse_kernel, per_device),
        out_shape=[jax.ShapeDtypeStruct((2 * channels, LANES), jnp.float32)] * SHARES,
        in_specs=[
            pl.BlockSpec(memory_space=pltpu.SMEM),
            pl.BlockSpec(memory_space=pltpu.VMEM),
            pl.BlockSpec(memory_space=pl.ANY),
            pl.BlockSpec(memory_space=pl.ANY),
        ],
        out_specs=[pl.BlockSpec(memory_space=pltpu.VMEM)] * SHARES,
        scratch_shapes=[
            pltpu.VMEM((2, channels, local), jnp.float32),
            pltpu.VMEM((SHARES, BLOCK, 2 * LANES), jnp.bfloat16),
            pltpu.VMEM((SHARES, phase_rows, LANES), jnp.float32),
            pltpu.VMEM((SHARES, phase_rows, LANES), jnp.float32),
            pltpu.VMEM((4, 4 * PAD, BLOCK), jnp.bfloat16),
            pltpu.VMEM((SHARES, 2 * PAD, LANES), jnp.float32),
            pltpu.SMEM((16,), jnp.int32),
            pltpu.SemaphoreType.DMA((pieces, 2)),
        ],
        compiler_params=pltpu.CompilerParams(vmem_limit_bytes=32 * 1024 * 1024),
        name="analyse",
    )(lengths, strength, second, first)


def restore_kernel(per_device, lengths, *refs):
    messages, (second, first, out, fields, basis, cosine, sine, coeff, table, sems) = (
        refs[:SHARES],
        refs[SHARES:],
    )
    channels, local = second.shape
    blocks = local // BLOCK
    pieces = sems.shape[0]
    copies = load_fields(second, first, fields, sems, pieces)
    me = device_id()
    row_table(lengths, table, me, local, lengths.shape[0])
    fill_phases(table, me, per_device, blocks, cosine, sine, -1.0)
    wave_index = lax.broadcasted_iota(jnp.int32, (LANES, BLOCK), 0)
    point = lax.broadcasted_iota(jnp.int32, (LANES, BLOCK), 1)
    for slot in range(SHARES):
        high, low = basis_of(wave_index, point, table[SHARES + slot], me, per_device)
        basis[slot, :LANES, :] = high
        basis[slot, LANES:, :] = low
    lane = lax.broadcasted_iota(jnp.int32, (1, LANES), 1)
    chunk = (lane >> 4) & 3
    coeff[...] = jnp.zeros_like(coeff)
    for slot in range(SHARES):
        value = jnp.zeros((channels, LANES), jnp.float32)
        for share in range(SHARES):
            moved = messages[share][...]
            if slot != share:
                moved = pltpu.roll(moved, ((share - slot) * GROUP) % LANES, 1)
            value = jnp.where(chunk == share, moved, value)
        coeff[slot, :channels, :] = value
    within = lax.broadcasted_iota(jnp.int32, (1, BLOCK), 1)

    def block_value(block, place, slot):
        value = coeff[slot]
        turned = (
            value * cosine[slot, pl.ds(block, 1), :]
            + pltpu.roll(value, PAD, 1) * sine[slot, pl.ds(block, 1), :]
        )
        high = turned.astype(jnp.bfloat16)
        low = (turned - high.astype(jnp.float32)).astype(jnp.bfloat16)
        left = jnp.concatenate([high, low], axis=0)
        left = jnp.concatenate([left, left], axis=1)
        product = jnp.dot(left, basis[slot], preferred_element_type=jnp.float32)
        value = product[:PAD] + product[PAD:]
        kept = fields[0, :, pl.ds(place, BLOCK)] + fields[1, :, pl.ds(place, BLOCK)]
        return kept - value[:channels]

    begin_slot = table[3 * SHARES]
    waited = 0
    for block in range(blocks):
        while waited * (local // pieces) < (block + 1) * BLOCK:
            copies[2 * waited].wait()
            copies[2 * waited + 1].wait()
            waited += 1
        place = block * BLOCK
        slot = begin_slot
        for later in range(1, SHARES):
            slot = slot + jnp.where(table[2 * SHARES + later] <= place, 1, 0)
        out[:, pl.ds(place, BLOCK)] = block_value(block, place, slot & 3)
    for later in range(1, SHARES):
        begin = table[2 * SHARES + later]

        @pl.when((begin < local) & ((begin & (BLOCK - 1)) != 0))
        def _():
            block = begin >> 8
            place = pl.multiple_of(block * BLOCK, BLOCK)
            value = block_value(block, place, (begin_slot + later) & 3)
            before = out[:, pl.ds(place, BLOCK)]
            out[:, pl.ds(place, BLOCK)] = jnp.where(within >= (begin & (BLOCK - 1)), value, before)


def restore(lengths, messages, second, first, per_device):
    channels, local = second.shape
    blocks = local // BLOCK
    pieces = 3
    phase_rows = -(-blocks // 8) * 8
    return pl.pallas_call(
        functools.partial(restore_kernel, per_device),
        out_shape=jax.ShapeDtypeStruct((channels, local), jnp.float32),
        in_specs=[pl.BlockSpec(memory_space=pltpu.SMEM)]
        + [pl.BlockSpec(memory_space=pltpu.VMEM)] * SHARES
        + [pl.BlockSpec(memory_space=pl.ANY)] * 2,
        out_specs=pl.BlockSpec(memory_space=pltpu.VMEM),
        scratch_shapes=[
            pltpu.VMEM((2, channels, local), jnp.float32),
            pltpu.VMEM((SHARES, 2 * LANES, BLOCK), jnp.bfloat16),
            pltpu.VMEM((SHARES, phase_rows, LANES), jnp.float32),
            pltpu.VMEM((SHARES, phase_rows, LANES), jnp.float32),
            pltpu.VMEM((SHARES, PAD, LANES), jnp.float32),
            pltpu.SMEM((16,), jnp.int32),
            pltpu.SemaphoreType.DMA((pieces, 2)),
        ],
        compiler_params=pltpu.CompilerParams(vmem_limit_bytes=32 * 1024 * 1024),
        name="restore",
    )(lengths, *messages, second, first)


def swapped(value, mask):
    count = lax.axis_size(AXES)
    return lax.ppermute(value, AXES, [(i, i ^ mask) for i in range(count)])


def legendre(latitude, waves):
    order = waves.astype(jnp.float32)[None, :]
    sine = jnp.sqrt(1.0 - latitude * latitude)[:, None]
    place = latitude[:, None]
    diagonal = jnp.full((latitude.shape[0], waves.shape[0]), math.sqrt(0.5), jnp.float32)
    previous = jnp.zeros_like(diagonal)
    current = jnp.zeros_like(diagonal)
    degrees = []
    for degree in range(WAVES):
        if degree:
            diagonal = diagonal * (sine * math.sqrt((2.0 * degree + 1.0) / (2.0 * degree)))
        upper = max(4.0 * degree * degree - 1.0, 0.0)
        below = float(degree - 1) ** 2
        factor_upper = jnp.sqrt(upper / jnp.maximum(float(degree * degree) - order * order, 1.0))
        factor_lower = jnp.sqrt(
            jnp.maximum(below - order * order, 0.0) / max(4.0 * below - 1.0, 1.0)
        )
        value = factor_upper * (place * current - factor_lower * previous)
        value = jnp.where(order > degree, 0.0, jnp.where(order == degree, diagonal, value))
        previous, current = current, value
        degrees.append(value)
    return jnp.stack(degrees, axis=-1)


def middle_general(received, strength, lengths, latitude, weights, local, per_device):
    rows = lengths.shape[0]
    count = lax.axis_size(AXES)
    channels = strength.shape[1]
    me = device_id()
    stops = jnp.cumsum(lengths)
    row_ids = jnp.arange(rows, dtype=jnp.int32)
    slots = jnp.arange(SHARES, dtype=jnp.int32)
    picks = []
    for share in range(SHARES):
        first = jnp.sum((stops <= (me ^ share) * local).astype(jnp.int32))
        held = first + ((slots - first) & 3)
        picks.append((held[:, None] == row_ids[None, :]).astype(jnp.float32))
    total = 0.0
    for pick, message in zip(picks, received):
        total = total + jnp.einsum(
            "gj,fcrgm->jfcrm",
            pick,
            message.reshape(2, channels, 2, SHARES, GROUP),
            precision=HIGHEST,
        )
    mask = SHARES
    while mask < count:
        total = total + swapped(total, mask)
        mask *= 2
    outer = jnp.arange(GROUP, dtype=jnp.int32) // per_device
    waves = per_device * ((me & 3) + SHARES * outer) + jnp.arange(GROUP) % per_device
    values = legendre(latitude, waves)
    gram = jnp.einsum("jmn,kmn->mjk", values, values, precision=HIGHEST)
    scale = jnp.where(waves == 0, 1.0, 2.0)
    rate_first = strength[0][:, None, None]
    both, second = total[:, 0], total[:, 1]
    once = jnp.einsum("mjk,kcrm->jcrm", gram, second, precision=HIGHEST)
    first = both - second - rate_first * weights[:, None, None, None] * once
    back = jnp.einsum("mjk,kcrm->jcrm", gram, first + second, precision=HIGHEST)
    back = back * (weights / lengths.astype(jnp.float32))[:, None, None, None] * scale
    replies = [
        jnp.einsum("gj,jcrm->crgm", pick, back, precision=HIGHEST).reshape(channels, LANES)
        for pick in picks
    ]
    spectrum = jnp.stack([first, second])
    begin = (me // SHARES) * per_device
    spectrum = lax.dynamic_slice_in_dim(spectrum, begin, per_device, 4)
    mine = lax.dynamic_slice_in_dim(values, begin, per_device, 1)
    factor = lax.dynamic_slice_in_dim(scale, begin, per_device, 0)
    factor = factor * (float(local * count) ** -0.5)
    result = jnp.einsum("jmn,sjcrm->scrmn", mine, spectrum, precision=HIGHEST)
    result = result * factor[:, None] * jnp.array([1.0, -1.0])[:, None, None]
    return replies, result


def on_device(cot_first, cot_second, strength, lengths, latitude, weights):
    local = cot_first.shape[1]
    per_device = WAVES // lax.axis_size(AXES)
    messages = analyse(lengths, strength, cot_second, cot_first, per_device)
    received = [messages[0]] + [swapped(messages[i], i) for i in range(1, SHARES)]
    replies, grad_target = middle_general(
        received, strength, lengths, latitude, weights, local, per_device
    )
    answers = [replies[0]] + [swapped(replies[i], i) for i in range(1, SHARES)]
    grad_state = restore(lengths, answers, cot_second, cot_first, per_device)
    return (grad_state, grad_target)


def solution(mesh):
    return jax.shard_map(
        on_device,
        mesh=mesh,
        in_specs=(
            P("chan", ("groups", "pts", "lev")),
            P("chan", ("groups", "pts", "lev")),
            P(None, ("groups", "chan")),
            P("groups"),
            P("groups"),
            P("groups"),
        ),
        out_specs=(
            P("chan", ("groups", "pts", "lev")),
            P(None, ("groups", "chan"), None, ("pts", "lev"), None),
        ),
        check_vma=False,
    )
```

time: 474 us -> 187 us (0.39)
  the two profiles are of different devices: /device:TPU:16 before, /device:TPU:0 now
where the time goes in v1:
time: 187 us; the launch traced here: 186 us
  other arithmetic  80.6 us (43%)
  local copies, waits for them, and re-layouts  57 us (30%)
  waiting for transfers between devices  23.1 us (12%)
  starting transfers between devices  8.9 us (5%)
  Pallas kernels  7.69 us (4%)
  matrix products  5.8 us (3%)
  between operations  2.86 us (2%)
    another operation x39, local copies, waits for them, and re-layouts, legendre(): return jnp.stack(degrees, axis=-1)  39 us
    eq x64, other arithmetic, legendre(): order == degree  33.2 us
    ppermute x7, waiting for transfers between devices, swapped(): return lax.ppermute(value, AXES, [(i, i ^ mask) for i in range(count)])  23.1 us
    sqrt x61, other arithmetic, legendre(): jnp.sqrt(upper / jnp.maximum(float(degree * degree) - order * order, 1.0))  22.7 us
    unnamed x291, local copies, waits for them, and re-layouts  14.5 us
    another operation x9, other arithmetic, legendre(): return jnp.stack(degrees, axis=-1)  9.57 us
    ppermute x7, starting transfers between devices, swapped(): return lax.ppermute(value, AXES, [(i, i ^ mask) for i in range(count)])  8.9 us
    select_n x6, other arithmetic, legendre(): jnp.where(order > degree, 0.0, jnp.where(order == degree, diagonal, value))  7.53 us
  transfers between devices with their start and end apart: 7, of which 1 were waited for; matrix products, arithmetic and copies ran while one was open for 68% of the time, Pallas kernels for 0%

profile of v1, /device:TPU:0, one launch (start us, length us, event | category | flops | bytes accessed | tf_op | source)
XLA Modules:
  0.0 185.9 jit_solution(5774998273746280408)
XLA Ops:
  0.6 1.2 copy-done
  1.9 1.2 copy-done.2
  4.4 4.0 %analyse.1 = (f32[100,128]{1,0:T(8,128)S(1)}, f32[100,128]{1,0:T(8,128)S(1)}, f32[100,128]{1,0:T(8,128)S(1)}, f32[100,128]{1,0:T(8,128)S(1)}) custom-call(s32[16]{0:T(128)S(1)} %copy-done.4, f32[2,50]{1,0:T(2,128)S(1)} %copy-done.6, f32[50,4608]{1,0:T(8,128)S(1)} %copy-done, f32[50,4608]{1,0:T(8,128)S(1)} %copy-done.2), custom_call_target="tpu_custom_call" | custom-call | tf_op jit(solution)/shard_map/analyse/pallas_call | solution.py:220
  8.4 0.8 collective-permute-start
  9.1 2.7 %collective-permute-start.2 = (f32[100,128]{1,0:T(8,128)S(1)}, f32[100,128]{1,0:T(8,128)}, u32[]{:S(2)}, u32[]{:S(2)}) collective-permute-start(f32[100,128]{1,0:T(8,128)S(1)} %get-tuple-element.9), channel_id=1, source_target_pairs={{0,5},{1,4},{4,1},{5,0},{8,13},{9,12},{12,9},{13,8},{2,7},{3,6},{6... | collective-permute-start | bytes 153608 | tf_op jit(solution)/shard_map/ppermute | solution.py:343
  70.1 1.3 multiply_multiply_fusion.58
  71.5 1.4 multiply_multiply_fusion.33
  72.9 3.6 %select_select_fusion = (f32[16,16,1]{2,0,1:T(8,128)S(1)}, f32[16,16,1]{2,0,1:T(8,128)S(1)}, f32[16,16,1]{2,0,1:T(8,128)S(1)}, f32[16,16,1]{2,0,1:T(8,128)S(1)},...) fusion(f32[16]{0:T(128)S(1)} %get-tuple-element.283, ...), kind=kLoop, calls=%fused_computation.39 | loop fusion | flops 39168 | bytes 26368 | tf_op jit(solution)/shard_map/jit(_where)/select_n | solution.py:364
  76.5 1.4 select_select_fusion.62
  78.2 1.4 fusion.74
  79.5 1.1 select_select_fusion.21
  81.0 1.0 select_select_fusion.22
  84.2 1.4 fusion.60
  86.7 2.2 %select_bitcast_fusion = (f32[16,16,1]{1,0,2:T(8,128)S(1)}, f32[16,16]{1,0:T(8,128)S(1)}, f32[16,16]{1,0:T(8,128)S(1)}, f32[16,16]{1,0:T(8,128)S(1)}, f32[16,16]...) fusion(f32[16]{0:T(128)} %get-tuple-element.207, ...), kind=kLoop, calls=%fused_computation.67 | loop fusion | flops 55296 | bytes 33728 | tf_op jit(solution)/shard_map/stack | solution.py:367
  90.3 0.8 copy.2412
  91.1 0.8 copy.2413
  92.6 0.8 fusion.70
  93.4 0.8 copy.2403
  94.2 0.8 copy.2409
  96.5 0.8 copy.2391
  97.3 0.8 copy.2394
  99.6 0.8 copy.2388
  100.4 0.8 copy.2397
  102.7 0.8 copy.2385
  103.5 0.8 copy.2400
  105.8 0.8 copy.2382
  106.6 0.8 copy.2406
  107.4 0.8 copy.2380
  108.3 1.0 copy.2381
  109.3 0.8 copy.2383
  110.1 0.8 copy.2384
  111.0 0.8 copy.2386
  111.8 0.8 copy.2387
  112.6 0.8 copy.2389
  113.4 0.8 copy.2390
  114.2 0.8 copy.2392
  115.1 0.8 copy.2393
  115.9 0.8 copy.2395
  116.7 0.8 copy.2396
  117.5 0.8 copy.2398
  118.4 0.8 copy.2399
  119.2 0.8 copy.2401
  120.0 0.8 copy.2402
  120.9 0.8 copy.2404
  121.7 0.8 copy.2405
  122.5 0.8 copy.2407
  123.3 0.8 copy.2408
  124.1 0.8 copy.2410
  125.0 0.8 copy.2411
  125.8 0.8 copy.2414
  126.6 0.8 copy.2378
  127.5 0.8 copy.2379
  128.3 0.8 copy.2377
  130.0 7.4 %stack.187 = f32[16,16,64]{2,0,1:T(8,128)S(1)} concatenate(f32[16,16,1]{2,0,1:T(8,128)S(1)} %get-tuple-element.157, f32[16,16,1]{2,0,1:T(8,128)S(1)} %get-tuple-element.156, f32[16,16,1]{2,0,1:T(8,128)S(1)} %get-tuple-element.155, f32[16,16,1]{2,0,1:T(8,128)} %select_select_fusion.22, f32[16,16,1]{2,0,1:T(8,128)} %select_select_fusion.21, f32[16,16,1]{2,0,1:T(8,128)S(1)} %get-tuple-element.152, ...), dimensions={2} | concatenate | bytes 131072 | tf_op jit(solution)/shard_map/stack | solution.py:367
  140.9 1.3 and_add_fusion
  143.6 0.9 copy.2364
  144.6 0.9 copy.2368
  147.5 3.1 %collective-permute-start.3 = (f32[16,2,50,2,16]{2,0,4,3,1:T(8,128)S(1)}, f32[16,2,50,2,16]{2,0,4,3,1:T(8,128)S(1)}, u32[]{:S(2)}, u32[]{:S(2)}) collective-permute-start(f32[16,2,50,2,16]{2,0,4,3,1:T(8,128)S(1)} %fusion.2), channel_id=1, source_target_pairs={{0,8},{1,9},{4,12},{5,13},{8,0},{9,1},{12,4},{13,5},{2,10},{3,11},... | collective-permute-start | bytes 614408 | tf_op jit(solution)/shard_map/ppermute | solution.py:343
  150.6 23.1 %collective-permute-done.3 = f32[16,2,50,2,16]{2,0,4,3,1:T(8,128)S(1)} collective-permute-done((f32[16,2,50,2,16]{2,0,4,3,1:T(8,128)S(1)}, f32[16,2,50,2,16]{2,0,4,3,1:T(8,128)S(1)}, u32[]{:S(2)}, u32[]{:S(2)}) %collective-permute-start.3) | collective-permute-done | bytes 204832 | tf_op jit(solution)/shard_map/ppermute | solution.py:343
  175.6 0.9 collective-permute-start.6
  176.6 1.4 collective-permute-start.5
  178.6 1.6 fusion.1
  180.5 1.4 copy.2430
  182.0 3.7 %restore.1 = f32[50,4608]{1,0:T(8,128)} custom-call(s32[16]{0:T(128)S(1)} %copy-done.5, f32[50,128]{1,0:T(8,128)S(1)} %copy.2427.refs_0_, f32[50,128]{1,0:T(8,128)S(1)} %collective-permute-done.4.refs_1_, f32[50,128]{1,0:T(8,128)S(1)} %collective-permute-done.5.refs_2_, f32[50,128]{1,0:T(8,128)S(1)} %collective-permute-done.6.refs_3_, ...), custom_call_target="tpu_custom_call" | custom-call | tf_op jit(solution)/shard_map/restore/pallas_call | solution.py:320
  (468 shorter events, 80.4 us)
Async XLA Ops:
  0.6 1.2 copy-start
  1.9 1.2 copy-start.2
  8.4 135.2 %collective-permute-start = (f32[100,128]{1,0:T(8,128)S(1)}, f32[100,128]{1,0:T(8,128)}, u32[]{:S(2)}, u32[]{:S(2)}) collective-permute-start(f32[100,128]{1,0:T(8,128)S(1)} %get-tuple-element.7), channel_id=1, source_target_pairs={{0,1},{1,0},{4,5},{5,4},{8,9},{9,8},{12,13},{13,12},{2,3},{3,2},{6... | collective-permute-start | bytes 153608 | tf_op jit(solution)/shard_map/ppermute | solution.py:343
  9.1 135.5 %collective-permute-start.2 = (f32[100,128]{1,0:T(8,128)S(1)}, f32[100,128]{1,0:T(8,128)}, u32[]{:S(2)}, u32[]{:S(2)}) collective-permute-start(f32[100,128]{1,0:T(8,128)S(1)} %get-tuple-element.9), channel_id=1, source_target_pairs={{0,5},{1,4},{4,1},{5,0},{8,13},{9,12},{12,9},{13,8},{2,7},{3,6},{6... | collective-permute-start | bytes 153608 | tf_op jit(solution)/shard_map/ppermute | solution.py:343
  11.8 133.8 %collective-permute-start.1 = (f32[100,128]{1,0:T(8,128)S(1)}, f32[100,128]{1,0:T(8,128)S(1)}, u32[]{:S(2)}, u32[]{:S(2)}) collective-permute-start(f32[100,128]{1,0:T(8,128)S(1)} %get-tuple-element.8), channel_id=1, source_target_pairs={{0,4},{1,5},{4,0},{5,1},{8,12},{9,13},{12,8},{13,9},{2,6},{3,7},{6... | collective-permute-start | bytes 153608 | tf_op jit(solution)/shard_map/ppermute | solution.py:343
  12.1 71.4 %copy-start.9 = (pred[16]{0:T(512)(128)(4,1)}, pred[16]{0:T(512)(128)(4,1)S(1)}, u32[]{:S(2)}) copy-start(pred[16]{0:T(512)(128)(4,1)S(1)} %get-tuple-element.412) | copy-start | bytes 52
  12.2 71.4 %copy-start.11 = (pred[16]{0:T(512)(128)(4,1)}, pred[16]{0:T(512)(128)(4,1)S(1)}, u32[]{:S(2)}) copy-start(pred[16]{0:T(512)(128)(4,1)S(1)} %get-tuple-element.413) | copy-start | bytes 52
  12.3 65.6 %copy-start.25 = (f32[16]{0:T(128)}, f32[16]{0:T(128)S(1)}, u32[]{:S(2)}) copy-start(f32[16]{0:T(128)S(1)} %get-tuple-element.291) | copy-start | bytes 196
  12.3 65.6 %copy-start.27 = (f32[16]{0:T(128)}, f32[16]{0:T(128)S(1)}, u32[]{:S(2)}) copy-start(f32[16]{0:T(128)S(1)} %get-tuple-element.292) | copy-start | bytes 196
  12.3 65.6 %copy-start.29 = (f32[16]{0:T(128)}, f32[16]{0:T(128)S(1)}, u32[]{:S(2)}) copy-start(f32[16]{0:T(128)S(1)} %get-tuple-element.293) | copy-start | bytes 196
  12.3 65.6 %copy-start.31 = (f32[16]{0:T(128)}, f32[16]{0:T(128)S(1)}, u32[]{:S(2)}) copy-start(f32[16]{0:T(128)S(1)} %get-tuple-element.294) | copy-start | bytes 196
  12.3 65.6 %copy-start.33 = (f32[16]{0:T(128)}, f32[16]{0:T(128)S(1)}, u32[]{:S(2)}) copy-start(f32[16]{0:T(128)S(1)} %get-tuple-element.295) | copy-start | bytes 196
  12.4 65.5 %copy-start.35 = (f32[16]{0:T(128)}, f32[16]{0:T(128)S(1)}, u32[]{:S(2)}) copy-start(f32[16]{0:T(128)S(1)} %get-tuple-element.296) | copy-start | bytes 196
  12.4 65.5 %copy-start.37 = (f32[16]{0:T(128)}, f32[16]{0:T(128)S(1)}, u32[]{:S(2)}) copy-start(f32[16]{0:T(128)S(1)} %get-tuple-element.297) | copy-start | bytes 196
  12.4 65.5 %copy-start.39 = (f32[16]{0:T(128)}, f32[16]{0:T(128)S(1)}, u32[]{:S(2)}) copy-start(f32[16]{0:T(128)S(1)} %get-tuple-element.298) | copy-start | bytes 196
  12.4 65.5 %copy-start.41 = (f32[16]{0:T(128)}, f32[16]{0:T(128)S(1)}, u32[]{:S(2)}) copy-start(f32[16]{0:T(128)S(1)} %get-tuple-element.299) | copy-start | bytes 196
  12.5 65.5 %copy-start.43 = (f32[16]{0:T(128)}, f32[16]{0:T(128)S(1)}, u32[]{:S(2)}) copy-start(f32[16]{0:T(128)S(1)} %get-tuple-element.300) | copy-start | bytes 196
  12.5 65.5 %copy-start.45 = (f32[16]{0:T(128)}, f32[16]{0:T(128)S(1)}, u32[]{:S(2)}) copy-start(f32[16]{0:T(128)S(1)} %get-tuple-element.301) | copy-start | bytes 196
  12.5 65.5 %copy-start.47 = (f32[16]{0:T(128)}, f32[16]{0:T(128)S(1)}, u32[]{:S(2)}) copy-start(f32[16]{0:T(128)S(1)} %get-tuple-element.302) | copy-start | bytes 196
  12.5 65.5 %copy-start.49 = (f32[16]{0:T(128)}, f32[16]{0:T(128)S(1)}, u32[]{:S(2)}) copy-start(f32[16]{0:T(128)S(1)} %get-tuple-element.303) | copy-start | bytes 196
  12.5 65.5 %copy-start.51 = (f32[16]{0:T(128)}, f32[16]{0:T(128)S(1)}, u32[]{:S(2)}) copy-start(f32[16]{0:T(128)S(1)} %get-tuple-element.304) | copy-start | bytes 196
  12.6 65.5 %copy-start.53 = (f32[16]{0:T(128)}, f32[16]{0:T(128)S(1)}, u32[]{:S(2)}) copy-start(f32[16]{0:T(128)S(1)} %get-tuple-element.305) | copy-start | bytes 196
  12.6 65.4 %copy-start.55 = (f32[16]{0:T(128)}, f32[16]{0:T(128)S(1)}, u32[]{:S(2)}) copy-start(f32[16]{0:T(128)S(1)} %get-tuple-element.306) | copy-start | bytes 196
  12.6 65.4 %copy-start.57 = (f32[16]{0:T(128)}, f32[16]{0:T(128)S(1)}, u32[]{:S(2)}) copy-start(f32[16]{0:T(128)S(1)} %get-tuple-element.307) | copy-start | bytes 196
  12.6 65.4 %copy-start.59 = (f32[16]{0:T(128)}, f32[16]{0:T(128)S(1)}, u32[]{:S(2)}) copy-start(f32[16]{0:T(128)S(1)} %get-tuple-element.308) | copy-start | bytes 196
  12.6 65.4 %copy-start.61 = (f32[16]{0:T(128)}, f32[16]{0:T(128)S(1)}, u32[]{:S(2)}) copy-start(f32[16]{0:T(128)S(1)} %get-tuple-element.309) | copy-start | bytes 196
  12.7 65.4 %copy-start.63 = (f32[16]{0:T(128)}, f32[16]{0:T(128)S(1)}, u32[]{:S(2)}) copy-start(f32[16]{0:T(128)S(1)} %get-tuple-element.310) | copy-start | bytes 196
  12.7 65.4 %copy-start.65 = (f32[16]{0:T(128)}, f32[16]{0:T(128)S(1)}, u32[]{:S(2)}) copy-start(f32[16]{0:T(128)S(1)} %get-tuple-element.311) | copy-start | bytes 196
  12.7 65.4 %copy-start.67 = (f32[16]{0:T(128)}, f32[16]{0:T(128)S(1)}, u32[]{:S(2)}) copy-start(f32[16]{0:T(128)S(1)} %get-tuple-element.312) | copy-start | bytes 196
  12.7 65.4 %copy-start.69 = (f32[16]{0:T(128)}, f32[16]{0:T(128)S(1)}, u32[]{:S(2)}) copy-start(f32[16]{0:T(128)S(1)} %get-tuple-element.313) | copy-start | bytes 196
  12.8 65.3 %copy-start.71 = (f32[16]{0:T(128)}, f32[16]{0:T(128)S(1)}, u32[]{:S(2)}) copy-start(f32[16]{0:T(128)S(1)} %get-tuple-element.314) | copy-start | bytes 196
  12.8 65.3 %copy-start.73 = (f32[16]{0:T(128)}, f32[16]{0:T(128)S(1)}, u32[]{:S(2)}) copy-start(f32[16]{0:T(128)S(1)} %get-tuple-element.315) | copy-start | bytes 196
  12.8 65.3 %copy-start.75 = (f32[16]{0:T(128)}, f32[16]{0:T(128)S(1)}, u32[]{:S(2)}) copy-start(f32[16]{0:T(128)S(1)} %get-tuple-element.316) | copy-start | bytes 196
  12.8 65.3 %copy-start.77 = (f32[16]{0:T(128)}, f32[16]{0:T(128)S(1)}, u32[]{:S(2)}) copy-start(f32[16]{0:T(128)S(1)} %get-tuple-element.317) | copy-start | bytes 196
  12.8 65.3 %copy-start.79 = (f32[16]{0:T(128)}, f32[16]{0:T(128)S(1)}, u32[]{:S(2)}) copy-start(f32[16]{0:T(128)S(1)} %get-tuple-element.318) | copy-start | bytes 196
  12.9 65.3 %copy-start.81 = (f32[16]{0:T(128)}, f32[16]{0:T(128)S(1)}, u32[]{:S(2)}) copy-start(f32[16]{0:T(128)S(1)} %get-tuple-element.319) | copy-start | bytes 196
  12.9 65.3 %copy-start.83 = (f32[16]{0:T(128)}, f32[16]{0:T(128)S(1)}, u32[]{:S(2)}) copy-start(f32[16]{0:T(128)S(1)} %get-tuple-element.320) | copy-start | bytes 196
  12.9 65.3 %copy-start.85 = (f32[16]{0:T(128)}, f32[16]{0:T(128)S(1)}, u32[]{:S(2)}) copy-start(f32[16]{0:T(128)S(1)} %get-tuple-element.321) | copy-start | bytes 196
  69.6 1.9 %copy-start.17 = (f32[16]{0:T(128)}, f32[16]{0:T(128)S(1)}, u32[]{:S(2)}) copy-start(f32[16]{0:T(128)S(1)} %get-tuple-element.117) | copy-start | bytes 196
  69.6 1.9 %copy-start.19 = (f32[16]{0:T(128)}, f32[16]{0:T(128)S(1)}, u32[]{:S(2)}) copy-start(f32[16]{0:T(128)S(1)} %get-tuple-element.108) | copy-start | bytes 196
  69.6 1.9 %copy-start.21 = (f32[16]{0:T(128)}, f32[16]{0:T(128)S(1)}, u32[]{:S(2)}) copy-start(f32[16]{0:T(128)S(1)} %get-tuple-element.114) | copy-start | bytes 196
  69.6 1.9 %copy-start.23 = (f32[16]{0:T(128)}, f32[16]{0:T(128)S(1)}, u32[]{:S(2)}) copy-start(f32[16]{0:T(128)S(1)} %get-tuple-element.111) | copy-start | bytes 196
  83.2 0.7 copy-start.64
  83.2 0.7 copy-start.66
  83.2 0.7 copy-start.68
  83.2 0.7 copy-start.70
  83.2 0.7 copy-start.72
  83.3 0.7 copy-start.36
  83.5 0.7 copy-start.62
  85.6 0.7 copy-start.87
  85.8 0.7 copy-start.119
  85.9 0.7 copy-start.135
  86.0 0.7 copy-start.95
  95.1 0.7 copy-start.132
  95.1 0.7 copy-start.134
  103.5 0.9 copy-start.109
  103.5 0.9 copy-start.117
  129.1 0.7 copy-start.12
  147.5 26.2 %collective-permute-start.3 = (f32[16,2,50,2,16]{2,0,4,3,1:T(8,128)S(1)}, f32[16,2,50,2,16]{2,0,4,3,1:T(8,128)S(1)}, u32[]{:S(2)}, u32[]{:S(2)}) collective-permute-start(f32[16,2,50,2,16]{2,0,4,3,1:T(8,128)S(1)} %fusion.2), channel_id=1, source_target_pairs={{0,8},{1,9},{4,12},{5,13},{8,0},{9,1},{12,4},{13,5},{2,10},{3,11},... | collective-permute-start | bytes 614408 | tf_op jit(solution)/shard_map/ppermute | solution.py:343
  175.4 6.5 %collective-permute-start.4 = (f32[50,128]{1,0:T(8,128)S(1)}, f32[50,128]{1,0:T(8,128)S(1)}, u32[]{:S(2)}, u32[]{:S(2)}) collective-permute-start(f32[50,128]{1,0:T(8,128)S(1)} %copy.2420), channel_id=1, source_target_pairs={{0,1},{1,0},{4,5},{5,4},{8,9},{9,8},{12,13},{13,12},{2,3},{3,2},{6... | collective-permute-start | bytes 76808 | tf_op jit(solution)/shard_map/ppermute | solution.py:343
  175.6 6.4 %collective-permute-start.6 = (f32[50,128]{1,0:T(8,128)S(1)}, f32[50,128]{1,0:T(8,128)S(1)}, u32[]{:S(2)}, u32[]{:S(2)}) collective-permute-start(f32[50,128]{1,0:T(8,128)S(1)} %copy.2426), channel_id=1, source_target_pairs={{0,5},{1,4},{4,1},{5,0},{8,13},{9,12},{12,9},{13,8},{2,7},{3,6},{6... | collective-permute-start | bytes 76808 | tf_op jit(solution)/shard_map/ppermute | solution.py:343
  176.6 5.4 %collective-permute-start.5 = (f32[50,128]{1,0:T(8,128)S(1)}, f32[50,128]{1,0:T(8,128)S(1)}, u32[]{:S(2)}, u32[]{:S(2)}) collective-permute-start(f32[50,128]{1,0:T(8,128)S(1)} %copy.2423), channel_id=1, source_target_pairs={{0,4},{1,5},{4,0},{5,1},{8,12},{9,13},{12,8},{13,9},{2,6},{3,7},{6... | collective-permute-start | bytes 76808 | tf_op jit(solution)/shard_map/ppermute | solution.py:343
  178.6 3.4 %copy-start.3 = (f32[50,4608]{1,0:T(8,128)S(1)}, f32[50,4608]{1,0:T(8,128)}, u32[]{:S(2)}) copy-start(f32[50,4608]{1,0:T(8,128)} %refs_5_.1) | copy-start | bytes 2764804
  180.5 1.5 copy-start.1
  (88 other events, 58.3 us)

commit v2 on v1

--- a/solution.py
+++ b/solution.py
@@ -16,6 +16,8 @@
 SHARES = 4
 GROUP = WAVES // SHARES
 PAD = 64
+FULL = 60 * 1024 * 1024
+SMALL = 8 * 1024 * 1024
 HIGHEST = lax.Precision.HIGHEST
 AXES = ("pts", "lev")
 
@@ -111,6 +113,48 @@
     down = lax.broadcasted_iota(jnp.int32, (count, count), 0)
     across = lax.broadcasted_iota(jnp.int32, (count, count), 1)
     return jnp.sum(jnp.where(down == across, row, 0.0), axis=1, keepdims=True)
+
+
+def group_roll(value, step):
+    if step == 0:
+        return value
+    lane = lax.broadcasted_iota(jnp.int32, (1, LANES), 1)
+    near = ((lane >> 4) & 3) < SHARES - step
+    return jnp.where(
+        near,
+        pltpu.roll(value, LANES - GROUP * step, 1),
+        pltpu.roll(value, GROUP * (SHARES - step), 1),
+    )
+
+
+def first_rows(lengths, me, local):
+    begins = [(me ^ share) * local for share in range(SHARES)]
+
+    def step(row, carry):
+        stop = carry[0] + lengths[row]
+        return (stop,) + tuple(
+            first + jnp.where(stop <= begin, 1, 0) for first, begin in zip(carry[1:], begins)
+        )
+
+    zero = jnp.int32(0)
+    return lax.fori_loop(0, lengths.shape[0], step, (zero,) * (1 + SHARES), unroll=True)[1:]
+
+
+def row_arrays(first):
+    lane = lax.broadcasted_iota(jnp.int32, (1, LANES), 1)
+    group = (lane >> 4) & 3
+    return (first + ((group - first) & 3)) >> 2
+
+
+def by_row(messages, firsts):
+    held = [row_arrays(first) for first in firsts]
+    arrays = []
+    for index in range(SHARES):
+        value = jnp.zeros(messages[0].shape, jnp.float32)
+        for array, message in zip(held, messages):
+            value = value + jnp.where(array == index, message, 0.0)
+        arrays.append(value)
+    return arrays
 
 
 def load_fields(second, first, fields, sems, pieces):
@@ -223,8 +267,8 @@
         in_specs=[
             pl.BlockSpec(memory_space=pltpu.SMEM),
             pl.BlockSpec(memory_space=pltpu.VMEM),
-            pl.BlockSpec(memory_space=pl.ANY),
-            pl.BlockSpec(memory_space=pl.ANY),
+            pl.BlockSpec(memory_space=pltpu.HBM),
+            pl.BlockSpec(memory_space=pltpu.HBM),
         ],
         out_specs=[pl.BlockSpec(memory_space=pltpu.VMEM)] * SHARES,
         scratch_shapes=[
@@ -237,20 +281,15 @@
             pltpu.SMEM((16,), jnp.int32),
             pltpu.SemaphoreType.DMA((pieces, 2)),
         ],
-        compiler_params=pltpu.CompilerParams(vmem_limit_bytes=32 * 1024 * 1024),
+        compiler_params=pltpu.CompilerParams(vmem_limit_bytes=FULL),
         name="analyse",
     )(lengths, strength, second, first)
 
 
 def restore_kernel(per_device, lengths, *refs):
-    messages, (second, first, out, fields, basis, cosine, sine, coeff, table, sems) = (
-        refs[:SHARES],
-        refs[SHARES:],
-    )
+    messages, (second, first, out, basis, cosine, sine, coeff, table) = refs[:SHARES], refs[SHARES:]
     channels, local = second.shape
     blocks = local // BLOCK
-    pieces = sems.shape[0]
-    copies = load_fields(second, first, fields, sems, pieces)
     me = device_id()
     row_table(lengths, table, me, local, lengths.shape[0])
     fill_phases(table, me, per_device, blocks, cosine, sine, -1.0)
@@ -285,16 +324,11 @@
         left = jnp.concatenate([left, left], axis=1)
         product = jnp.dot(left, basis[slot], preferred_element_type=jnp.float32)
         value = product[:PAD] + product[PAD:]
-        kept = fields[0, :, pl.ds(place, BLOCK)] + fields[1, :, pl.ds(place, BLOCK)]
+        kept = second[:, pl.ds(place, BLOCK)] + first[:, pl.ds(place, BLOCK)]
         return kept - value[:channels]
 
     begin_slot = table[3 * SHARES]
-    waited = 0
     for block in range(blocks):
-        while waited * (local // pieces) < (block + 1) * BLOCK:
-            copies[2 * waited].wait()
-            copies[2 * waited + 1].wait()
-            waited += 1
         place = block * BLOCK
         slot = begin_slot
         for later in range(1, SHARES):
@@ -315,23 +349,19 @@
 def restore(lengths, messages, second, first, per_device):
     channels, local = second.shape
     blocks = local // BLOCK
-    pieces = 3
     phase_rows = -(-blocks // 8) * 8
     return pl.pallas_call(
         functools.partial(restore_kernel, per_device),
         out_shape=jax.ShapeDtypeStruct((channels, local), jnp.float32),
         in_specs=[pl.BlockSpec(memory_space=pltpu.SMEM)]
-        + [pl.BlockSpec(memory_space=pltpu.VMEM)] * SHARES
-        + [pl.BlockSpec(memory_space=pl.ANY)] * 2,
+        + [pl.BlockSpec(memory_space=pltpu.VMEM)] * (SHARES + 2),
         out_specs=pl.BlockSpec(memory_space=pltpu.VMEM),
         scratch_shapes=[
-            pltpu.VMEM((2, channels, local), jnp.float32),
             pltpu.VMEM((SHARES, 2 * LANES, BLOCK), jnp.bfloat16),
             pltpu.VMEM((SHARES, phase_rows, LANES), jnp.float32),
             pltpu.VMEM((SHARES, phase_rows, LANES), jnp.float32),
             pltpu.VMEM((SHARES, PAD, LANES), jnp.float32),
             pltpu.SMEM((16,), jnp.int32),
-            pltpu.SemaphoreType.DMA((pieces, 2)),
         ],
         compiler_params=pltpu.CompilerParams(vmem_limit_bytes=32 * 1024 * 1024),
         name="restore",
@@ -418,16 +448,283 @@
     return replies, result
 
 
+def prepare_kernel(per_device, count, local, lengths, latitude, weights, coupling, poly, gram, pt, square):
+    me = device_id()
+    down = lax.broadcasted_iota(jnp.int32, (8, LANES), 0)
+    lane = lax.broadcasted_iota(jnp.int32, (8, LANES), 1)
+    group = (lane >> 4) & 3
+    packed = down >= SHARES
+    array = jnp.where(packed, (lane >> 6) * 2 + ((lane >> 3) & 1), down)
+    row = SHARES * array + group
+    within = lane & (GROUP - 1)
+    outer = within >> 3
+    order = jnp.where(
+        packed, 8 * me + (lane & 7), 8 * ((me & 3) + SHARES * outer) + (lane & 7)
+    ).astype(jnp.float32)
+    place = jnp.zeros((8, LANES), jnp.float32)
+    weight = jnp.zeros((8, LANES), jnp.float32)
+    size = jnp.zeros((8, LANES), jnp.int32)
+    for index in range(lengths.shape[0]):
+        here = row == index
+        place = jnp.where(here, latitude[index], place)
+        weight = jnp.where(here, weights[index], weight)
+        size = jnp.where(here, lengths[index], size)
+    doubling = jnp.where(order == 0.0, 1.0, 2.0)
+    scale = weight / size.astype(jnp.float32) * doubling
+    sine = jnp.sqrt(1.0 - place * place)
+    order_square = order * order
+    diagonal = jnp.full((8, LANES), math.sqrt(0.5), jnp.float32)
+    previous = jnp.zeros((8, LANES), jnp.float32)
+    current = previous
+    for degree in range(WAVES):
+        if degree:
+            diagonal = diagonal * (sine * math.sqrt((2.0 * degree + 1.0) / (2.0 * degree)))
+        upper = math.sqrt(max(4.0 * degree * degree - 1.0, 0.0))
+        below = float(degree - 1) ** 2
+        factor_upper = upper * lax.rsqrt(jnp.maximum(float(degree * degree) - order_square, 1.0))
+        factor_lower = jnp.sqrt(
+            jnp.maximum(below - order_square, 0.0) * (1.0 / max(4.0 * below - 1.0, 1.0))
+        )
+        value = (factor_upper * place) * current - (factor_upper * factor_lower) * previous
+        value = jnp.where(order > degree, 0.0, jnp.where(order == degree, diagonal, value))
+        previous, current = current, value
+        for index in range(SHARES + 1):
+            pt[index, pl.ds(degree, 1), :] = value[index : index + 1, :]
+    for step in range(SHARES):
+        for source in range(SHARES):
+            moved = group_roll(pt[source], step)
+            for target in range(SHARES):
+                square[target, pl.ds(step * SHARES + source, 1), :] = jnp.sum(
+                    pt[target] * moved, axis=0, keepdims=True
+                )
+    twice = [jnp.zeros((GROUP, LANES), jnp.float32)] * SHARES
+    for through in range(SHARES):
+        weighted = square[through] * weight[through : through + 1, :]
+        for step in range(SHARES):
+            moved = group_roll(weighted, step)
+            if step:
+                moved = jnp.concatenate(
+                    [moved[GROUP - SHARES * step :], moved[: GROUP - SHARES * step]], axis=0
+                )
+            for target in range(SHARES):
+                factor = square[target, pl.ds(step * SHARES + through, 1), :]
+                twice[target] = twice[target] + factor * moved
+    for target in range(SHARES):
+        coupling[0, target] = square[target] * scale[target : target + 1, :]
+        coupling[1, target] = twice[target] * scale[target : target + 1, :]
+    mine = pt[SHARES]
+    factor = doubling[SHARES : SHARES + 1, :] * (float(local * count) ** -0.5)
+    poly[...] = mine * factor
+    for step in range(GROUP):
+        moved = pltpu.roll(mine, (LANES - 8 * step) % LANES, 1) if step else mine
+        gram[pl.ds(step, 1), :] = weight[SHARES : SHARES + 1, :] * jnp.sum(
+            mine * moved, axis=0, keepdims=True
+        )
+
+
+SMEM = pl.BlockSpec(memory_space=pltpu.SMEM)
+VMEM = pl.BlockSpec(memory_space=pltpu.VMEM)
+
+
+def floats(*shape):
+    return jax.ShapeDtypeStruct(shape, jnp.float32)
+
+
+def prepare(lengths, latitude, weights, per_device, count, local):
+    return pl.pallas_call(
+        functools.partial(prepare_kernel, per_device, count, local),
+        out_shape=[
+            floats(2, SHARES, GROUP, LANES),
+            floats(WAVES, LANES),
+            floats(GROUP, LANES),
+        ],
+        in_specs=[SMEM] * 3,
+        out_specs=[VMEM] * 3,
+        scratch_shapes=[
+            pltpu.VMEM((SHARES + 1, WAVES, LANES), jnp.float32),
+            pltpu.VMEM((SHARES, GROUP, LANES), jnp.float32),
+        ],
+        compiler_params=pltpu.CompilerParams(vmem_limit_bytes=SMALL),
+        name="prepare",
+    )(lengths, latitude, weights)
+
+
+def couple_kernel(local, lengths, strength, coupling, *refs):
+    messages, out = [ref[...] for ref in refs[:SHARES]], refs[SHARES]
+    channels = strength.shape[1]
+    firsts = first_rows(lengths, device_id(), local)
+    arrays = by_row(messages, firsts)
+    rate_first = column(strength[0:1, :])
+    sums = [jnp.zeros((channels, LANES), jnp.float32)] * SHARES
+    for source in range(SHARES):
+        both = arrays[source][:channels]
+        second = rate_first * arrays[source][channels:]
+        for step in range(SHARES):
+            moved_both = group_roll(both, step)
+            moved_second = group_roll(second, step)
+            at = pl.ds(step * SHARES + source, 1)
+            for target in range(SHARES):
+                sums[target] = (
+                    sums[target]
+                    + coupling[0, target, at, :] * moved_both
+                    - coupling[1, target, at, :] * moved_second
+                )
+    for target in range(SHARES):
+        out[pl.ds(target * channels, channels), :] = sums[target]
+
+
+def couple(lengths, strength, coupling, messages, local):
+    channels = strength.shape[1]
+    return pl.pallas_call(
+        functools.partial(couple_kernel, local),
+        out_shape=floats(SHARES * channels, LANES),
+        in_specs=[SMEM] + [VMEM] * (2 + SHARES),
+        out_specs=VMEM,
+        compiler_params=pltpu.CompilerParams(vmem_limit_bytes=SMALL),
+        name="couple",
+    )(lengths, strength, coupling, *messages)
+
+
+def pack_kernel(local, lengths, *refs):
+    messages, (own, other) = [ref[...] for ref in refs[:SHARES]], refs[SHARES:]
+    rows = messages[0].shape[0]
+    me = device_id()
+    arrays = by_row(messages, first_rows(lengths, me, local))
+    lane = lax.broadcasted_iota(jnp.int32, (1, LANES), 1)
+    array = (lane >> 6) * 2 + ((lane >> 3) & 1)
+    upper = me >= SHARES
+    for part in range(2):
+        halves = []
+        for half in range(2):
+            value = jnp.zeros((rows, LANES), jnp.float32)
+            for index in range(SHARES):
+                shift = (64 * (index >> 1) + 8 * (index & 1) - 64 * part - 8 * half) % LANES
+                moved = pltpu.roll(arrays[index], shift, 1) if shift else arrays[index]
+                value = jnp.where(array == index, moved, value)
+            halves.append(value)
+        own[pl.ds(part * rows, rows), :] = jnp.where(upper, halves[1], halves[0])
+        other[pl.ds(part * rows, rows), :] = jnp.where(upper, halves[0], halves[1])
+
+
+def pack(lengths, messages, local):
+    rows = messages[0].shape[0]
+    return pl.pallas_call(
+        functools.partial(pack_kernel, local),
+        out_shape=[floats(2 * rows, LANES)] * 2,
+        in_specs=[SMEM] + [VMEM] * SHARES,
+        out_specs=[VMEM] * 2,
+        compiler_params=pltpu.CompilerParams(vmem_limit_bytes=SMALL),
+        name="pack",
+    )(lengths, *messages)
+
+
+def hand_out_kernel(local, lengths, own, other, *outs):
+    channels = outs[0].shape[0]
+    firsts = first_rows(lengths, device_id(), local)
+    sums = []
+    for index in range(SHARES):
+        at = pl.ds(index * channels, channels)
+        sums.append(own[at, :] + other[at, :])
+    for first, out in zip(firsts, outs):
+        array = row_arrays(first)
+        value = sums[0]
+        for index in range(1, SHARES):
+            value = jnp.where(array == index, sums[index], value)
+        out[...] = value
+
+
+def hand_out(lengths, own, other, local):
+    channels = own.shape[0] // SHARES
+    return pl.pallas_call(
+        functools.partial(hand_out_kernel, local),
+        out_shape=[floats(channels, LANES)] * SHARES,
+        in_specs=[SMEM] + [VMEM] * 2,
+        out_specs=[VMEM] * SHARES,
+        compiler_params=pltpu.CompilerParams(vmem_limit_bytes=SMALL),
+        name="hand_out",
+    )(lengths, own, other)
+
+
+def spectrum_kernel(strength, own, other, poly, gram, out):
+    channels = strength.shape[1]
+    rate_first = column(strength[0:1, :])
+    down = lax.broadcasted_iota(jnp.int32, (8, LANES), 0)
+    lane = lax.broadcasted_iota(jnp.int32, (8, LANES), 1)
+    match = jnp.where(down == (lane & 7), 1.0, 0.0)[None]
+    high = poly[...].astype(jnp.bfloat16)
+    low = (poly[...] - high.astype(jnp.float32)).astype(jnp.bfloat16)
+    right = jnp.concatenate(
+        [
+            jnp.concatenate([high, high], axis=1),
+            jnp.concatenate([low, jnp.zeros_like(low)], axis=1),
+        ],
+        axis=0,
+    )
+    for part in range(2):
+        at = pl.ds(2 * part * channels, channels)
+        both = own[at, :] + other[at, :]
+        at = pl.ds((2 * part + 1) * channels, channels)
+        second = own[at, :] + other[at, :]
+        first = both - second
+        for step in range(GROUP):
+            moved = pltpu.roll(second, (LANES - 8 * step) % LANES, 1) if step else second
+            first = first - rate_first * (gram[pl.ds(step, 1), :] * moved)
+        for index, value in enumerate((first, second)):
+            if part:
+                value = -value
+            rounded = value.astype(jnp.bfloat16).astype(jnp.float32)
+            sides = []
+            for side in (rounded, value - rounded):
+                spread = side[:, None, :] * match
+                sides.append(spread.reshape(8 * channels, LANES).astype(jnp.bfloat16))
+            product = lax.dot_general(
+                jnp.concatenate(sides, axis=1),
+                right,
+                (((1,), (1,)), ((), ())),
+                preferred_element_type=jnp.float32,
+            )
+            result = product[:, :WAVES] + product[:, WAVES:]
+            out[index, :, part] = result.reshape(channels, 8, WAVES)
+
+
+def spectrum(strength, own, other, poly, gram):
+    channels = strength.shape[1]
+    return pl.pallas_call(
+        spectrum_kernel,
+        out_shape=floats(2, channels, 2, 8, WAVES),
+        in_specs=[VMEM] * 5,
+        out_specs=VMEM,
+        compiler_params=pltpu.CompilerParams(vmem_limit_bytes=SMALL),
+        name="spectrum",
+    )(strength, own, other, poly, gram)
+
+
+def middle_small(received, strength, lengths, latitude, weights, local, per_device, count):
+    coupling, poly, gram = prepare(lengths, latitude, weights, per_device, count, local)
+    part = couple(lengths, strength, coupling, received, local)
+    other_part = swapped(part, SHARES)
+    own, sent = pack(lengths, received, local)
+    other = swapped(sent, SHARES)
+    replies = hand_out(lengths, part, other_part, local)
+    return replies, (strength, own, other, poly, gram)
+
+
 def on_device(cot_first, cot_second, strength, lengths, latitude, weights):
     local = cot_first.shape[1]
-    per_device = WAVES // lax.axis_size(AXES)
+    count = lax.axis_size(AXES)
+    per_device = WAVES // count
     messages = analyse(lengths, strength, cot_second, cot_first, per_device)
     received = [messages[0]] + [swapped(messages[i], i) for i in range(1, SHARES)]
-    replies, grad_target = middle_general(
-        received, strength, lengths, latitude, weights, local, per_device
-    )
+    arguments = (received, strength, lengths, latitude, weights, local, per_device)
+    small = count == 2 * SHARES and lengths.shape[0] == GROUP
+    if small:
+        replies, pieces = middle_small(*arguments, count)
+    else:
+        replies, grad_target = middle_general(*arguments)
     answers = [replies[0]] + [swapped(replies[i], i) for i in range(1, SHARES)]
     grad_state = restore(lengths, answers, cot_second, cot_first, per_device)
+    if small:
+        grad_target = spectrum(*pieces)
     return (grad_state, grad_target)
 
 

time: 187 us -> 33.6 us (0.18)
  other arithmetic: 80.6 us -> 0 us
  local copies, waits for them, and re-layouts: 57 us -> 1.65 us
  waiting for transfers between devices: 23.1 us -> 8.06 us
  matrix products: 5.8 us -> 0 us
  Pallas kernels: 7.69 us -> 13.1 us
  between operations: 2.86 us -> 0.74 us
    another operation x41 -> x0, local copies, waits for them, and re-layouts: 39.1 us -> none  [the longest x39 39 us: legendre(): return jnp.stack(degrees, axis=-1)]
    eq x64 -> x0, other arithmetic: 33.2 us -> none  [legendre(): order == degree]
    sqrt x62 -> x0, other arithmetic: 22.7 us -> none  [the longest x61 22.7 us: legendre(): jnp.sqrt(upper / jnp.maximum(float(degree * degree) - order * order, 1.0))]
    ppermute x7 -> x8, waiting for transfers between devices: 23.1 us -> 8.06 us  [swapped(): return lax.ppermute(value, AXES, [(i, i ^ mask) for i in range(count)])]
    unnamed x291 -> x16, local copies, waits for them, and re-layouts: 14.5 us -> 1.65 us
    another operation x10 -> x0, other arithmetic: 9.6 us -> none  [the longest x9 9.57 us: legendre(): return jnp.stack(degrees, axis=-1)]
    select_n x7 -> x0, other arithmetic: 8.13 us -> none  [the longest x6 7.53 us: legendre(): jnp.where(order > degree, 0.0, jnp.where(order == degree, diagonal, value))]
    dot_general x12 -> x0, matrix products: 5.8 us -> none  [the longest x4 2.08 us: middle_general(): jnp.einsum('gj,fcrgm->jfcrm', pick, message.reshape(2, channels, 2, SHARE...]
  transfers between devices with their start and end apart: 7 -> 8, of which waited for: 1 -> 5; matrix products, arithmetic and copies ran while one was open for 68% -> 0% of each run, Pallas kernels for 0% -> 13%
where the time goes in v2:
time: 33.6 us; the launch traced here: 33 us
  Pallas kernels  13.1 us (39%)
  starting transfers between devices  9.4 us (28%)
  waiting for transfers between devices  8.06 us (24%)
  local copies, waits for them, and re-layouts  1.65 us (5%)
  between operations  0.74 us (2%)
    ppermute x8, starting transfers between devices, swapped(): return lax.ppermute(value, AXES, [(i, i ^ mask) for i in range(count)])  9.4 us
    ppermute x8, waiting for transfers between devices, swapped(): return lax.ppermute(value, AXES, [(i, i ^ mask) for i in range(count)])  8.06 us
    pallas_call x1, Pallas kernels, analyse(): pl.pallas_call(functools.partial(analyse_kernel, per_device), out_shape=[...  4.72 us
    pallas_call x1, Pallas kernels, restore(): pl.pallas_call(functools.partial(restore_kernel, per_device), out_shape=j...  3.05 us
    unnamed x16, local copies, waits for them, and re-layouts  1.65 us
    pallas_call x1, Pallas kernels, spectrum(): pl.pallas_call(spectrum_kernel, out_shape=floats(2, channels, 2, 8, WAVES...  1.52 us
    pallas_call x1, Pallas kernels, prepare(): pl.pallas_call(functools.partial(prepare_kernel, per_device, count, local...  1.24 us
    pallas_call x1, Pallas kernels, couple(): pl.pallas_call(functools.partial(couple_kernel, local), out_shape=floats(...  1.12 us
  transfers between devices with their start and end apart: 8, of which 5 were waited for; matrix products, arithmetic and copies ran while one was open for 0% of the time, Pallas kernels for 13%

profile of v2, /device:TPU:0, one launch (start us, length us, event | category | flops | bytes accessed | tf_op | source)
XLA Modules:
  0.0 33.0 jit_solution(15937736800484912245)
XLA Ops:
  0.6 0.0 copy-start.4
  0.6 0.0 copy-start.6
  0.7 0.0 copy-start.7
  0.7 0.0 copy-start.5
  0.7 0.0 copy-start.1
  0.7 4.7 %analyse.1 = (f32[100,128]{1,0:T(8,128)}, f32[100,128]{1,0:T(8,128)}, f32[100,128]{1,0:T(8,128)}, f32[100,128]{1,0:T(8,128)}) custom-call(s32[16]{0:T(128)} %lengths.11, f32[2,50]{1,0:T(2,128)} %strength.5, f32[50,4608]{1,0:T(8,128)} %refs_4_.1, f32[50,4608]{1,0:T(8,128)} %refs_5_.1), custom_call_target="tpu_custom_call" | custom-call | tf_op jit(solution)/shard_map/analyse/pallas_call | solution.py:264
  5.4 0.0 copy-start
  5.4 1.0 %collective-permute-start = (f32[100,128]{1,0:T(8,128)}, f32[100,128]{1,0:T(8,128)S(1)}, u32[]{:S(2)}, u32[]{:S(2)}) collective-permute-start(f32[100,128]{1,0:T(8,128)} %get-tuple-element.17), channel_id=1, source_target_pairs={{0,1},{1,0},{4,5},{5,4},{8,9},{9,8},{12,13},{13,12},{2,3},{3,2},{6... | collective-permute-start | bytes 153608 | tf_op jit(solution)/shard_map/ppermute | solution.py:373
  6.5 2.4 %collective-permute-start.1 = (f32[100,128]{1,0:T(8,128)}, f32[100,128]{1,0:T(8,128)S(1)}, u32[]{:S(2)}, u32[]{:S(2)}) collective-permute-start(f32[100,128]{1,0:T(8,128)} %get-tuple-element.18), channel_id=1, source_target_pairs={{0,4},{1,5},{4,0},{5,1},{8,12},{9,13},{12,8},{13,9},{2,6},{3,7},{6... | collective-permute-start | bytes 153608 | tf_op jit(solution)/shard_map/ppermute | solution.py:373
  8.8 0.1 collective-permute-start.2
  8.9 0.0 copy-done.4
  8.9 0.0 copy-done.6
  8.9 0.0 copy-done.7
  8.9 1.2 %prepare.1 = (f32[2,4,16,128]{3,2,1,0:T(8,128)S(1)}, f32[64,128]{1,0:T(8,128)S(1)}, f32[16,128]{1,0:T(8,128)S(1)}) custom-call(s32[16]{0:T(128)S(1)} %copy-done.4, f32[16]{0:T(128)S(1)} %copy-done.6, f32[16]{0:T(128)S(1)} %copy-done.7), custom_call_target="tpu_custom_call" | custom-call | tf_op jit(solution)/shard_map/prepare/pallas_call | solution.py:534
  10.2 0.0 collective-permute-done.refs_1_
  10.2 1.3 %collective-permute-done.1.refs_2_ = f32[100,128]{1,0:T(8,128)S(1)} collective-permute-done((f32[100,128]{1,0:T(8,128)}, f32[100,128]{1,0:T(8,128)S(1)}, u32[]{:S(2)}, u32[]{:S(2)}) %collective-permute-start.1) | collective-permute-done | bytes 51232 | tf_op jit(solution)/shard_map/ppermute | solution.py:373
  11.5 1.4 %collective-permute-done.2.refs_3_ = f32[100,128]{1,0:T(8,128)S(1)} collective-permute-done((f32[100,128]{1,0:T(8,128)}, f32[100,128]{1,0:T(8,128)S(1)}, u32[]{:S(2)}, u32[]{:S(2)}) %collective-permute-start.2) | collective-permute-done | bytes 51232 | tf_op jit(solution)/shard_map/ppermute | solution.py:373
  12.9 0.0 copy-done.5
  12.9 0.0 copy-start.2
  12.9 0.8 %copy-done.2 = f32[100,128]{1,0:T(8,128)S(1)} copy-done((f32[100,128]{1,0:T(8,128)S(1)}, f32[100,128]{1,0:T(8,128)}, u32[]{:S(2)}) %copy-start.2) | copy-done | bytes 51224
  13.7 1.1 %couple.1.own = f32[200,128]{1,0:T(8,128)S(1)} custom-call(s32[16]{0:T(128)S(1)} %copy-done.4, f32[2,50]{1,0:T(2,128)S(1)} %copy-done.5, f32[2,4,16,128]{3,2,1,0:T(8,128)S(1)} %get-tuple-element.15.coupling, f32[100,128]{1,0:T(8,128)S(1)} %copy-done.2, f32[100,128]{1,0:T(8,128)S(1)} %collective-permute-done.refs_1_, ...), custom_call_target="tpu_custom_call" | custom-call | tf_op jit(solution)/shard_map/couple/pallas_call | solution.py:578
  14.9 2.7 %collective-permute-start.3 = (f32[200,128]{1,0:T(8,128)S(1)}, f32[200,128]{1,0:T(8,128)S(1)}, u32[]{:S(2)}, u32[]{:S(2)}) collective-permute-start(f32[200,128]{1,0:T(8,128)S(1)} %couple.1.own), channel_id=1, source_target_pairs={{0,8},{1,9},{4,12},{5,13},{8,0},{9,1},{12,4},{13,5},{2,10},{3,11},... | collective-permute-start | bytes 307208 | tf_op jit(solution)/shard_map/ppermute | solution.py:373
  17.5 0.0 copy-start.3
  17.5 0.8 %copy-done.3 = f32[100,128]{1,0:T(8,128)S(1)} copy-done((f32[100,128]{1,0:T(8,128)S(1)}, f32[100,128]{1,0:T(8,128)}, u32[]{:S(2)}) %copy-start.3) | copy-done | bytes 51224
  18.3 0.9 %pack.1 = (f32[200,128]{1,0:T(8,128)S(1)}, f32[200,128]{1,0:T(8,128)S(1)}) custom-call(s32[16]{0:T(128)S(1)} %copy-done.4, f32[100,128]{1,0:T(8,128)S(1)} %copy-done.3, f32[100,128]{1,0:T(8,128)S(1)} %collective-permute-done.refs_1_, f32[100,128]{1,0:T(8,128)S(1)} %collective-permute-done.1.refs_2_, f32[100,128]{1,0:T(8,128)S(1)} %collective-permute-done.2.refs_3_), custom_call_target="tpu_custom_call" | custom-call | tf_op jit(solution)/shard_map/pack/pallas_call | solution.py:611
  19.2 0.4 %collective-permute-start.7 = (f32[200,128]{1,0:T(8,128)S(1)}, f32[200,128]{1,0:T(8,128)S(1)}, u32[]{:S(2)}, u32[]{:S(2)}) collective-permute-start(f32[200,128]{1,0:T(8,128)S(1)} %get-tuple-element.25), channel_id=1, source_target_pairs={{0,8},{1,9},{4,12},{5,13},{8,0},{9,1},{12,4},{13,5},{2,10},{3,11},... | collective-permute-start | bytes 307208 | tf_op jit(solution)/shard_map/ppermute | solution.py:373
  19.6 3.6 %collective-permute-done.3.other = f32[200,128]{1,0:T(8,128)S(1)} collective-permute-done((f32[200,128]{1,0:T(8,128)S(1)}, f32[200,128]{1,0:T(8,128)S(1)}, u32[]{:S(2)}, u32[]{:S(2)}) %collective-permute-start.3) | collective-permute-done | bytes 102432 | tf_op jit(solution)/shard_map/ppermute | solution.py:373
  23.2 0.6 %hand_out.1 = (f32[50,128]{1,0:T(8,128)S(1)}, f32[50,128]{1,0:T(8,128)S(1)}, f32[50,128]{1,0:T(8,128)S(1)}, f32[50,128]{1,0:T(8,128)S(1)}) custom-call(s32[16]{0:T(128)S(1)} %copy-done.4, f32[200,128]{1,0:T(8,128)S(1)} %couple.1.own, f32[200,128]{1,0:T(8,128)S(1)} %collective-permute-done.3.other), custom_call_target="tpu_custom_call" | custom-call | tf_op jit(solution)/shard_map/hand_out/pallas_call | solution.py:638
  23.9 0.1 collective-permute-start.4
  23.9 2.7 %collective-permute-start.5 = (f32[50,128]{1,0:T(8,128)S(1)}, f32[50,128]{1,0:T(8,128)S(1)}, u32[]{:S(2)}, u32[]{:S(2)}) collective-permute-start(f32[50,128]{1,0:T(8,128)S(1)} %get-tuple-element.22), channel_id=1, source_target_pairs={{0,4},{1,5},{4,0},{5,1},{8,12},{9,13},{12,8},{13,9},{2,6},{3,7},{6... | collective-permute-start | bytes 76808 | tf_op jit(solution)/shard_map/ppermute | solution.py:373
  26.6 0.1 collective-permute-start.6
  26.7 0.6 %collective-permute-done.7.other = f32[200,128]{1,0:T(8,128)S(1)} collective-permute-done((f32[200,128]{1,0:T(8,128)S(1)}, f32[200,128]{1,0:T(8,128)S(1)}, u32[]{:S(2)}, u32[]{:S(2)}) %collective-permute-start.7) | collective-permute-done | bytes 102432 | tf_op jit(solution)/shard_map/ppermute | solution.py:373
  27.3 1.5 %spectrum.1 = f32[2,50,2,8,64]{4,3,2,1,0:T(8,128)} custom-call(f32[2,50]{1,0:T(2,128)S(1)} %copy-done.5, f32[200,128]{1,0:T(8,128)S(1)} %get-tuple-element.24.own, f32[200,128]{1,0:T(8,128)S(1)} %collective-permute-done.7.other, f32[64,128]{1,0:T(8,128)S(1)} %get-tuple-element.26.poly, f32[16,128]{1,0:T(8,128)S(1)} %get-tuple-element.27.gram), custom_call_target="tpu_custom_call" | custom-call | tf_op jit(solution)/shard_map/spectrum/pallas_call | solution.py:692
  28.8 0.0 collective-permute-done.4.refs_1_
  28.8 0.0 collective-permute-done.5.refs_2_
  28.9 1.1 %collective-permute-done.6.refs_3_ = f32[50,128]{1,0:T(8,128)S(1)} collective-permute-done((f32[50,128]{1,0:T(8,128)S(1)}, f32[50,128]{1,0:T(8,128)S(1)}, u32[]{:S(2)}, u32[]{:S(2)}) %collective-permute-start.6) | collective-permute-done | bytes 25632 | tf_op jit(solution)/shard_map/ppermute | solution.py:373
  29.9 0.0 copy-done.1
  29.9 0.0 copy-done
  29.9 3.0 %restore.1 = f32[50,4608]{1,0:T(8,128)} custom-call(s32[16]{0:T(128)S(1)} %copy-done.4, f32[50,128]{1,0:T(8,128)S(1)} %get-tuple-element.20.refs_0_, f32[50,128]{1,0:T(8,128)S(1)} %collective-permute-done.4.refs_1_, f32[50,128]{1,0:T(8,128)S(1)} %collective-permute-done.5.refs_2_, f32[50,128]{1,0:T(8,128)S(1)} %collective-permute-done.6.refs_3_, ...), custom_call_target="tpu_custom_call" | custom-call | tf_op jit(solution)/shard_map/restore/pallas_call | solution.py:353
Async XLA Ops:
  0.6 8.3 %copy-start.4 = (s32[16]{0:T(128)S(1)}, s32[16]{0:T(128)}, u32[]{:S(2)}) copy-start(s32[16]{0:T(128)} %lengths.11) | copy-start | bytes 196
  0.6 8.3 %copy-start.6 = (f32[16]{0:T(128)S(1)}, f32[16]{0:T(128)}, u32[]{:S(2)}) copy-start(f32[16]{0:T(128)} %latitude.1) | copy-start | bytes 196
  0.7 8.3 %copy-start.7 = (f32[16]{0:T(128)S(1)}, f32[16]{0:T(128)}, u32[]{:S(2)}) copy-start(f32[16]{0:T(128)} %weights.1) | copy-start | bytes 196
  0.7 12.3 %copy-start.5 = (f32[2,50]{1,0:T(2,128)S(1)}, f32[2,50]{1,0:T(2,128)}, u32[]{:S(2)}) copy-start(f32[2,50]{1,0:T(2,128)} %strength.5) | copy-start | bytes 1204
  0.7 29.3 %copy-start.1 = (f32[50,4608]{1,0:T(8,128)S(1)}, f32[50,4608]{1,0:T(8,128)}, u32[]{:S(2)}) copy-start(f32[50,4608]{1,0:T(8,128)} %refs_5_.1) | copy-start | bytes 2764804
  5.4 24.5 %copy-start = (f32[50,4608]{1,0:T(8,128)S(1)}, f32[50,4608]{1,0:T(8,128)}, u32[]{:S(2)}) copy-start(f32[50,4608]{1,0:T(8,128)} %refs_4_.1) | copy-start | bytes 2764804
  5.4 4.7 %collective-permute-start = (f32[100,128]{1,0:T(8,128)}, f32[100,128]{1,0:T(8,128)S(1)}, u32[]{:S(2)}, u32[]{:S(2)}) collective-permute-start(f32[100,128]{1,0:T(8,128)} %get-tuple-element.17), channel_id=1, source_target_pairs={{0,1},{1,0},{4,5},{5,4},{8,9},{9,8},{12,13},{13,12},{2,3},{3,2},{6... | collective-permute-start | bytes 153608 | tf_op jit(solution)/shard_map/ppermute | solution.py:373
  6.5 5.0 %collective-permute-start.1 = (f32[100,128]{1,0:T(8,128)}, f32[100,128]{1,0:T(8,128)S(1)}, u32[]{:S(2)}, u32[]{:S(2)}) collective-permute-start(f32[100,128]{1,0:T(8,128)} %get-tuple-element.18), channel_id=1, source_target_pairs={{0,4},{1,5},{4,0},{5,1},{8,12},{9,13},{12,8},{13,9},{2,6},{3,7},{6... | collective-permute-start | bytes 153608 | tf_op jit(solution)/shard_map/ppermute | solution.py:373
  8.8 4.1 %collective-permute-start.2 = (f32[100,128]{1,0:T(8,128)}, f32[100,128]{1,0:T(8,128)S(1)}, u32[]{:S(2)}, u32[]{:S(2)}) collective-permute-start(f32[100,128]{1,0:T(8,128)} %get-tuple-element.19), channel_id=1, source_target_pairs={{0,5},{1,4},{4,1},{5,0},{8,13},{9,12},{12,9},{13,8},{2,7},{3,6},{6... | collective-permute-start | bytes 153608 | tf_op jit(solution)/shard_map/ppermute | solution.py:373
  12.9 0.8 %copy-start.2 = (f32[100,128]{1,0:T(8,128)S(1)}, f32[100,128]{1,0:T(8,128)}, u32[]{:S(2)}) copy-start(f32[100,128]{1,0:T(8,128)} %get-tuple-element.16.refs_0_) | copy-start | bytes 153604
  14.9 8.3 %collective-permute-start.3 = (f32[200,128]{1,0:T(8,128)S(1)}, f32[200,128]{1,0:T(8,128)S(1)}, u32[]{:S(2)}, u32[]{:S(2)}) collective-permute-start(f32[200,128]{1,0:T(8,128)S(1)} %couple.1.own), channel_id=1, source_target_pairs={{0,8},{1,9},{4,12},{5,13},{8,0},{9,1},{12,4},{13,5},{2,10},{3,11},... | collective-permute-start | bytes 307208 | tf_op jit(solution)/shard_map/ppermute | solution.py:373
  17.5 0.8 %copy-start.3 = (f32[100,128]{1,0:T(8,128)S(1)}, f32[100,128]{1,0:T(8,128)}, u32[]{:S(2)}) copy-start(f32[100,128]{1,0:T(8,128)} %get-tuple-element.16.refs_0_) | copy-start | bytes 153604
  19.2 8.1 %collective-permute-start.7 = (f32[200,128]{1,0:T(8,128)S(1)}, f32[200,128]{1,0:T(8,128)S(1)}, u32[]{:S(2)}, u32[]{:S(2)}) collective-permute-start(f32[200,128]{1,0:T(8,128)S(1)} %get-tuple-element.25), channel_id=1, source_target_pairs={{0,8},{1,9},{4,12},{5,13},{8,0},{9,1},{12,4},{13,5},{2,10},{3,11},... | collective-permute-start | bytes 307208 | tf_op jit(solution)/shard_map/ppermute | solution.py:373
  23.9 5.0 %collective-permute-start.4 = (f32[50,128]{1,0:T(8,128)S(1)}, f32[50,128]{1,0:T(8,128)S(1)}, u32[]{:S(2)}, u32[]{:S(2)}) collective-permute-start(f32[50,128]{1,0:T(8,128)S(1)} %get-tuple-element.21), channel_id=1, source_target_pairs={{0,1},{1,0},{4,5},{5,4},{8,9},{9,8},{12,13},{13,12},{2,3},{3,2},{6... | collective-permute-start | bytes 76808 | tf_op jit(solution)/shard_map/ppermute | solution.py:373
  23.9 4.9 %collective-permute-start.5 = (f32[50,128]{1,0:T(8,128)S(1)}, f32[50,128]{1,0:T(8,128)S(1)}, u32[]{:S(2)}, u32[]{:S(2)}) collective-permute-start(f32[50,128]{1,0:T(8,128)S(1)} %get-tuple-element.22), channel_id=1, source_target_pairs={{0,4},{1,5},{4,0},{5,1},{8,12},{9,13},{12,8},{13,9},{2,6},{3,7},{6... | collective-permute-start | bytes 76808 | tf_op jit(solution)/shard_map/ppermute | solution.py:373
  26.6 3.3 %collective-permute-start.6 = (f32[50,128]{1,0:T(8,128)S(1)}, f32[50,128]{1,0:T(8,128)S(1)}, u32[]{:S(2)}, u32[]{:S(2)}) collective-permute-start(f32[50,128]{1,0:T(8,128)S(1)} %get-tuple-element.23), channel_id=1, source_target_pairs={{0,5},{1,4},{4,1},{5,0},{8,13},{9,12},{12,9},{13,8},{2,7},{3,6},{6... | collective-permute-start | bytes 76808 | tf_op jit(solution)/shard_map/ppermute | solution.py:373

commit v3 on v2

--- a/solution.py
+++ b/solution.py
@@ -17,6 +17,7 @@
 GROUP = WAVES // SHARES
 PAD = 64
 FULL = 60 * 1024 * 1024
+WINDOW = 3
 SMALL = 8 * 1024 * 1024
 HIGHEST = lax.Precision.HIGHEST
 AXES = ("pts", "lev")
@@ -127,8 +128,8 @@
     )
 
 
-def first_rows(lengths, me, local):
-    begins = [(me ^ share) * local for share in range(SHARES)]
+def first_rows(lengths, devices, local):
+    begins = [device * local for device in devices]
 
     def step(row, carry):
         stop = carry[0] + lengths[row]
@@ -137,7 +138,11 @@
         )
 
     zero = jnp.int32(0)
-    return lax.fori_loop(0, lengths.shape[0], step, (zero,) * (1 + SHARES), unroll=True)[1:]
+    return lax.fori_loop(0, lengths.shape[0], step, (zero,) * (1 + len(devices)), unroll=True)[1:]
+
+
+def near(me):
+    return [me ^ share for share in range(SHARES)]
 
 
 def row_arrays(first):
@@ -155,6 +160,11 @@
             value = value + jnp.where(array == index, message, 0.0)
         arrays.append(value)
     return arrays
+
+
+def split_block(begin, blocks):
+    within = begin & (BLOCK - 1)
+    return jnp.minimum(begin >> 8, blocks - 1), jnp.where(within == 0, BLOCK, within)
 
 
 def load_fields(second, first, fields, sems, pieces):
@@ -227,13 +237,9 @@
             block, place, slot, 0, table[slot] + table[SHARES + slot] - place, block % lhs.shape[0]
         )
     for later in range(1, SHARES):
-        begin = table[2 * SHARES + later]
-
-        @pl.when((begin < local) & ((begin & (BLOCK - 1)) != 0))
-        def _():
-            block = begin >> 8
-            place = pl.multiple_of(block * BLOCK, BLOCK)
-            add_block(block, place, (begin_slot + later) & 3, begin & (BLOCK - 1), BLOCK, later)
+        block, low_end = split_block(table[2 * SHARES + later], blocks)
+        place = pl.multiple_of(block * BLOCK, BLOCK)
+        add_block(block, place, (begin_slot + later) & 3, low_end, BLOCK, later)
 
     rate_first = column(strength[0:1, :])
     rate_second = column(strength[1:2, :])
@@ -286,19 +292,12 @@
     )(lengths, strength, second, first)
 
 
-def restore_kernel(per_device, lengths, *refs):
-    messages, (second, first, out, basis, cosine, sine, coeff, table) = refs[:SHARES], refs[SHARES:]
+def restore_kernel(lengths, *refs):
+    messages, (second, first, basis, cosine, sine, out, coeff, table) = refs[:SHARES], refs[SHARES:]
     channels, local = second.shape
     blocks = local // BLOCK
     me = device_id()
     row_table(lengths, table, me, local, lengths.shape[0])
-    fill_phases(table, me, per_device, blocks, cosine, sine, -1.0)
-    wave_index = lax.broadcasted_iota(jnp.int32, (LANES, BLOCK), 0)
-    point = lax.broadcasted_iota(jnp.int32, (LANES, BLOCK), 1)
-    for slot in range(SHARES):
-        high, low = basis_of(wave_index, point, table[SHARES + slot], me, per_device)
-        basis[slot, :LANES, :] = high
-        basis[slot, LANES:, :] = low
     lane = lax.broadcasted_iota(jnp.int32, (1, LANES), 1)
     chunk = (lane >> 4) & 3
     coeff[...] = jnp.zeros_like(coeff)
@@ -335,37 +334,65 @@
             slot = slot + jnp.where(table[2 * SHARES + later] <= place, 1, 0)
         out[:, pl.ds(place, BLOCK)] = block_value(block, place, slot & 3)
     for later in range(1, SHARES):
-        begin = table[2 * SHARES + later]
-
-        @pl.when((begin < local) & ((begin & (BLOCK - 1)) != 0))
-        def _():
-            block = begin >> 8
-            place = pl.multiple_of(block * BLOCK, BLOCK)
-            value = block_value(block, place, (begin_slot + later) & 3)
-            before = out[:, pl.ds(place, BLOCK)]
-            out[:, pl.ds(place, BLOCK)] = jnp.where(within >= (begin & (BLOCK - 1)), value, before)
-
-
-def restore(lengths, messages, second, first, per_device):
+        block, low_end = split_block(table[2 * SHARES + later], blocks)
+        place = pl.multiple_of(block * BLOCK, BLOCK)
+        value = block_value(block, place, (begin_slot + later) & 3)
+        before = out[:, pl.ds(place, BLOCK)]
+        out[:, pl.ds(place, BLOCK)] = jnp.where(within >= low_end, value, before)
+
+
+def restore(lengths, messages, second, first, tables):
     channels, local = second.shape
-    blocks = local // BLOCK
-    phase_rows = -(-blocks // 8) * 8
     return pl.pallas_call(
-        functools.partial(restore_kernel, per_device),
+        restore_kernel,
         out_shape=jax.ShapeDtypeStruct((channels, local), jnp.float32),
         in_specs=[pl.BlockSpec(memory_space=pltpu.SMEM)]
-        + [pl.BlockSpec(memory_space=pltpu.VMEM)] * (SHARES + 2),
+        + [pl.BlockSpec(memory_space=pltpu.VMEM)] * (SHARES + 5),
         out_specs=pl.BlockSpec(memory_space=pltpu.VMEM),
         scratch_shapes=[
-            pltpu.VMEM((SHARES, 2 * LANES, BLOCK), jnp.bfloat16),
-            pltpu.VMEM((SHARES, phase_rows, LANES), jnp.float32),
-            pltpu.VMEM((SHARES, phase_rows, LANES), jnp.float32),
             pltpu.VMEM((SHARES, PAD, LANES), jnp.float32),
             pltpu.SMEM((16,), jnp.int32),
         ],
         compiler_params=pltpu.CompilerParams(vmem_limit_bytes=32 * 1024 * 1024),
         name="restore",
-    )(lengths, *messages, second, first)
+    )(lengths, *messages, second, first, *tables)
+
+
+def fill_tables(table, me, per_device, basis, cosine, sine, blocks):
+    fill_phases(table, me, per_device, blocks, cosine, sine, -1.0)
+    wave_index = lax.broadcasted_iota(jnp.int32, (LANES, BLOCK), 0)
+    point = lax.broadcasted_iota(jnp.int32, (LANES, BLOCK), 1)
+    for slot in range(SHARES):
+        high, low = basis_of(wave_index, point, table[SHARES + slot], me, per_device)
+        basis[slot, :LANES, :] = high
+        basis[slot, LANES:, :] = low
+
+
+def tables_kernel(per_device, local, lengths, basis, cosine, sine, table):
+    me = device_id()
+    row_table(lengths, table, me, local, lengths.shape[0])
+    fill_tables(table, me, per_device, basis, cosine, sine, local // BLOCK)
+
+
+def table_shapes(local):
+    phase_rows = -(-(local // BLOCK) // 8) * 8
+    return [
+        jax.ShapeDtypeStruct((SHARES, 2 * LANES, BLOCK), jnp.bfloat16),
+        jax.ShapeDtypeStruct((SHARES, phase_rows, LANES), jnp.float32),
+        jax.ShapeDtypeStruct((SHARES, phase_rows, LANES), jnp.float32),
+    ]
+
+
+def tables_of(lengths, local, per_device):
+    return pl.pallas_call(
+        functools.partial(tables_kernel, per_device, local),
+        out_shape=table_shapes(local),
+        in_specs=[pl.BlockSpec(memory_space=pltpu.SMEM)],
+        out_specs=[pl.BlockSpec(memory_space=pltpu.VMEM)] * 3,
+        scratch_shapes=[pltpu.SMEM((16,), jnp.int32)],
+        compiler_params=pltpu.CompilerParams(vmem_limit_bytes=SMALL),
+        name="tables",
+    )(lengths)
 
 
 def swapped(value, mask):
@@ -448,7 +475,18 @@
     return replies, result
 
 
-def prepare_kernel(per_device, count, local, lengths, latitude, weights, coupling, poly, gram, pt, square):
+def least(values):
+    result = values[0]
+    for value in values[1:]:
+        result = jnp.minimum(result, value)
+    return result
+
+
+def prepare_kernel(
+    per_device, count, local, lengths, latitude, weights, message, coupling, poly, gram, kept, pt, square, sem
+):
+    copy = pltpu.make_async_copy(message, kept, sem)
+    copy.start()
     me = device_id()
     down = lax.broadcasted_iota(jnp.int32, (8, LANES), 0)
     lane = lax.broadcasted_iota(jnp.int32, (8, LANES), 1)
@@ -520,6 +558,7 @@
         gram[pl.ds(step, 1), :] = weight[SHARES : SHARES + 1, :] * jnp.sum(
             mine * moved, axis=0, keepdims=True
         )
+    copy.wait()
 
 
 SMEM = pl.BlockSpec(memory_space=pltpu.SMEM)
@@ -530,29 +569,32 @@
     return jax.ShapeDtypeStruct(shape, jnp.float32)
 
 
-def prepare(lengths, latitude, weights, per_device, count, local):
+def prepare(lengths, latitude, weights, message, per_device, count, local):
     return pl.pallas_call(
         functools.partial(prepare_kernel, per_device, count, local),
         out_shape=[
             floats(2, SHARES, GROUP, LANES),
             floats(WAVES, LANES),
             floats(GROUP, LANES),
+            floats(*message.shape),
         ],
-        in_specs=[SMEM] * 3,
-        out_specs=[VMEM] * 3,
+        in_specs=[SMEM] * 3 + [pl.BlockSpec(memory_space=pl.ANY)],
+        out_specs=[VMEM] * 4,
         scratch_shapes=[
             pltpu.VMEM((SHARES + 1, WAVES, LANES), jnp.float32),
             pltpu.VMEM((SHARES, GROUP, LANES), jnp.float32),
+            pltpu.SemaphoreType.DMA,
         ],
         compiler_params=pltpu.CompilerParams(vmem_limit_bytes=SMALL),
         name="prepare",
-    )(lengths, latitude, weights)
+    )(lengths, latitude, weights, message)
 
 
 def couple_kernel(local, lengths, strength, coupling, *refs):
-    messages, out = [ref[...] for ref in refs[:SHARES]], refs[SHARES]
+    messages, (own, other) = [ref[...] for ref in refs[:SHARES]], refs[SHARES:]
     channels = strength.shape[1]
-    firsts = first_rows(lengths, device_id(), local)
+    me = device_id()
+    *firsts, far = first_rows(lengths, near(me) + [(me ^ SHARES) & SHARES], local)
     arrays = by_row(messages, firsts)
     rate_first = column(strength[0:1, :])
     sums = [jnp.zeros((channels, LANES), jnp.float32)] * SHARES
@@ -569,27 +611,37 @@
                     + coupling[0, target, at, :] * moved_both
                     - coupling[1, target, at, :] * moved_second
                 )
-    for target in range(SHARES):
-        out[pl.ds(target * channels, channels), :] = sums[target]
+    for first, out in ((least(firsts), own), (far, other)):
+        begin = row_arrays(first)
+        for index in range(WINDOW):
+            value = jnp.zeros((channels, LANES), jnp.float32)
+            for target in range(SHARES):
+                value = jnp.where(begin + index == target, sums[target], value)
+            out[pl.ds(index * channels, channels), :] = value
 
 
 def couple(lengths, strength, coupling, messages, local):
     channels = strength.shape[1]
     return pl.pallas_call(
         functools.partial(couple_kernel, local),
-        out_shape=floats(SHARES * channels, LANES),
+        out_shape=[floats(WINDOW * channels, LANES)] * 2,
         in_specs=[SMEM] + [VMEM] * (2 + SHARES),
-        out_specs=VMEM,
+        out_specs=[VMEM] * 2,
         compiler_params=pltpu.CompilerParams(vmem_limit_bytes=SMALL),
         name="couple",
     )(lengths, strength, coupling, *messages)
 
 
-def pack_kernel(local, lengths, *refs):
-    messages, (own, other) = [ref[...] for ref in refs[:SHARES]], refs[SHARES:]
+def pack_kernel(per_device, local, lengths, after, *refs):
+    messages, (basis, cosine, sine, own, other, table) = (
+        [ref[...] for ref in refs[:SHARES]],
+        refs[SHARES:],
+    )
     rows = messages[0].shape[0]
     me = device_id()
-    arrays = by_row(messages, first_rows(lengths, me, local))
+    row_table(lengths, table, me, local, lengths.shape[0])
+    fill_tables(table, me, per_device, basis, cosine, sine, local // BLOCK)
+    arrays = by_row(messages, first_rows(lengths, near(me), local))
     lane = lax.broadcasted_iota(jnp.int32, (1, LANES), 1)
     array = (lane >> 6) * 2 + ((lane >> 3) & 1)
     upper = me >= SHARES
@@ -606,35 +658,37 @@
         other[pl.ds(part * rows, rows), :] = jnp.where(upper, halves[0], halves[1])
 
 
-def pack(lengths, messages, local):
+def pack(lengths, after, messages, local, per_device):
     rows = messages[0].shape[0]
     return pl.pallas_call(
-        functools.partial(pack_kernel, local),
-        out_shape=[floats(2 * rows, LANES)] * 2,
-        in_specs=[SMEM] + [VMEM] * SHARES,
-        out_specs=[VMEM] * 2,
+        functools.partial(pack_kernel, per_device, local),
+        out_shape=table_shapes(local) + [floats(2 * rows, LANES)] * 2,
+        in_specs=[SMEM, pl.BlockSpec(memory_space=pl.ANY)] + [VMEM] * SHARES,
+        out_specs=[VMEM] * 5,
+        scratch_shapes=[pltpu.SMEM((16,), jnp.int32)],
         compiler_params=pltpu.CompilerParams(vmem_limit_bytes=SMALL),
         name="pack",
-    )(lengths, *messages)
+    )(lengths, after, *messages)
 
 
 def hand_out_kernel(local, lengths, own, other, *outs):
     channels = outs[0].shape[0]
-    firsts = first_rows(lengths, device_id(), local)
+    firsts = first_rows(lengths, near(device_id()), local)
+    begin = row_arrays(least(firsts))
     sums = []
-    for index in range(SHARES):
+    for index in range(WINDOW):
         at = pl.ds(index * channels, channels)
         sums.append(own[at, :] + other[at, :])
     for first, out in zip(firsts, outs):
-        array = row_arrays(first)
+        array = row_arrays(first) - begin
         value = sums[0]
-        for index in range(1, SHARES):
+        for index in range(1, WINDOW):
             value = jnp.where(array == index, sums[index], value)
         out[...] = value
 
 
 def hand_out(lengths, own, other, local):
-    channels = own.shape[0] // SHARES
+    channels = own.shape[0] // WINDOW
     return pl.pallas_call(
         functools.partial(hand_out_kernel, local),
         out_shape=[floats(channels, LANES)] * SHARES,
@@ -700,13 +754,16 @@
 
 
 def middle_small(received, strength, lengths, latitude, weights, local, per_device, count):
-    coupling, poly, gram = prepare(lengths, latitude, weights, per_device, count, local)
-    part = couple(lengths, strength, coupling, received, local)
-    other_part = swapped(part, SHARES)
-    own, sent = pack(lengths, received, local)
+    coupling, poly, gram, kept = prepare(
+        lengths, latitude, weights, received[0], per_device, count, local
+    )
+    received = [kept] + received[1:]
+    part, sent_part = couple(lengths, strength, coupling, received, local)
+    other_part = swapped(sent_part, SHARES)
+    *tables, own, sent = pack(lengths, part, received, local, per_device)
     other = swapped(sent, SHARES)
     replies = hand_out(lengths, part, other_part, local)
-    return replies, (strength, own, other, poly, gram)
+    return replies, tables, (strength, own, other, poly, gram)
 
 
 def on_device(cot_first, cot_second, strength, lengths, latitude, weights):
@@ -718,11 +775,12 @@
     arguments = (received, strength, lengths, latitude, weights, local, per_device)
     small = count == 2 * SHARES and lengths.shape[0] == GROUP
     if small:
-        replies, pieces = middle_small(*arguments, count)
+        replies, tables, pieces = middle_small(*arguments, count)
     else:
         replies, grad_target = middle_general(*arguments)
+        tables = tables_of(lengths, local, per_device)
     answers = [replies[0]] + [swapped(replies[i], i) for i in range(1, SHARES)]
-    grad_state = restore(lengths, answers, cot_second, cot_first, per_device)
+    grad_state = restore(lengths, answers, cot_second, cot_first, tables)
     if small:
         grad_target = spectrum(*pieces)
     return (grad_state, grad_target)

time: 33.6 us -> 30.4 us (0.905); the launches traced: 33 us -> 30.1 us
  waiting for transfers between devices: 8.06 us -> 5.93 us
  local copies, waits for them, and re-layouts: 1.65 us -> 0.83 us
    ppermute x8, waiting for transfers between devices: 8.06 us -> 5.93 us  [swapped(): return lax.ppermute(value, AXES, [(i, i ^ mask) for i in range(count)])]
    unnamed x16 -> x14, local copies, waits for them, and re-layouts: 1.65 us -> 0.83 us
  transfers between devices with their start and end apart: 8 -> 8, of which waited for: 5 -> 5; matrix products, arithmetic and copies ran while one was open for 0% -> 0% of each run, Pallas kernels for 13% -> 17%
where the time goes in v3:
time: 30.4 us; the launch traced here: 30.1 us
  Pallas kernels  13.2 us (43%)
  starting transfers between devices  9.41 us (31%)
  waiting for transfers between devices  5.93 us (20%)
  local copies, waits for them, and re-layouts  0.83 us (3%)
  between operations  0.75 us (2%)
    ppermute x8, starting transfers between devices, swapped(): return lax.ppermute(value, AXES, [(i, i ^ mask) for i in range(count)])  9.41 us
    ppermute x8, waiting for transfers between devices, swapped(): return lax.ppermute(value, AXES, [(i, i ^ mask) for i in range(count)])  5.93 us
    pallas_call x1, Pallas kernels, analyse(): pl.pallas_call(functools.partial(analyse_kernel, per_device), out_shape=[...  4.6 us
    pallas_call x1, Pallas kernels, restore(): pl.pallas_call(restore_kernel, out_shape=jax.ShapeDtypeStruct((channels,...  2.42 us
    pallas_call x1, Pallas kernels, pack(): pl.pallas_call(functools.partial(pack_kernel, per_device, local), out_sha...  1.57 us
    pallas_call x1, Pallas kernels, spectrum(): pl.pallas_call(spectrum_kernel, out_shape=floats(2, channels, 2, 8, WAVES...  1.52 us
    pallas_call x1, Pallas kernels, prepare(): pl.pallas_call(functools.partial(prepare_kernel, per_device, count, local...  1.32 us
    pallas_call x1, Pallas kernels, couple(): pl.pallas_call(functools.partial(couple_kernel, local), out_shape=[floats...  1.15 us
  transfers between devices with their start and end apart: 8, of which 5 were waited for; matrix products, arithmetic and copies ran while one was open for 0% of the time, Pallas kernels for 17%

profile of v3, /device:TPU:0, one launch (start us, length us, event | category | flops | bytes accessed | tf_op | source)
XLA Modules:
  0.0 30.1 jit_solution(5083361147318145656)
XLA Ops:
  0.6 0.0 copy-start.3
  0.6 0.0 copy-start.5
  0.7 0.0 copy-start.6
  0.7 0.0 copy-start.4
  0.7 0.0 copy-start.1
  0.7 4.6 %analyse.1 = (f32[100,128]{1,0:T(8,128)}, f32[100,128]{1,0:T(8,128)}, f32[100,128]{1,0:T(8,128)}, f32[100,128]{1,0:T(8,128)}) custom-call(s32[16]{0:T(128)} %lengths.11, f32[2,50]{1,0:T(2,128)} %strength.5, f32[50,4608]{1,0:T(8,128)} %refs_4_.1, f32[50,4608]{1,0:T(8,128)} %refs_5_.1), custom_call_target="tpu_custom_call" | custom-call | tf_op jit(solution)/shard_map/analyse/pallas_call | solution.py:270
  5.3 0.0 copy-start
  5.3 0.5 %collective-permute-start = (f32[100,128]{1,0:T(8,128)}, f32[100,128]{1,0:T(8,128)S(1)}, u32[]{:S(2)}, u32[]{:S(2)}) collective-permute-start(f32[100,128]{1,0:T(8,128)} %get-tuple-element.24), channel_id=1, source_target_pairs={{0,1},{1,0},{4,5},{5,4},{8,9},{9,8},{12,13},{13,12},{2,3},{3,2},{6... | collective-permute-start | bytes 153608 | tf_op jit(solution)/shard_map/ppermute | solution.py:400
  5.8 2.6 %collective-permute-start.1 = (f32[100,128]{1,0:T(8,128)}, f32[100,128]{1,0:T(8,128)S(1)}, u32[]{:S(2)}, u32[]{:S(2)}) collective-permute-start(f32[100,128]{1,0:T(8,128)} %get-tuple-element.25), channel_id=1, source_target_pairs={{0,4},{1,5},{4,0},{5,1},{8,12},{9,13},{12,8},{13,9},{2,6},{3,7},{6... | collective-permute-start | bytes 153608 | tf_op jit(solution)/shard_map/ppermute | solution.py:400
  8.4 0.1 collective-permute-start.2
  8.5 0.0 copy-done.3
  8.5 0.0 copy-done.5
  8.5 0.0 copy-done.6
  8.5 0.0 copy-start.2
  8.5 0.8 %copy-done.2 = f32[100,128]{1,0:T(8,128)S(1)} copy-done((f32[100,128]{1,0:T(8,128)S(1)}, f32[100,128]{1,0:T(8,128)}, u32[]{:S(2)}) %copy-start.2) | copy-done | bytes 51224
  9.3 1.3 %prepare.1 = (f32[2,4,16,128]{3,2,1,0:T(8,128)S(1)}, f32[64,128]{1,0:T(8,128)S(1)}, f32[16,128]{1,0:T(8,128)S(1)}, f32[100,128]{1,0:T(8,128)S(1)}) custom-call(s32[16]{0:T(128)S(1)} %copy-done.3, f32[16]{0:T(128)S(1)} %copy-done.5, f32[16]{0:T(128)S(1)} %copy-done.6, f32[100,128]{1,0:T(8,128)S(1)} %copy-done.2), custom_call_target="tpu_custom_call" | custom-call | tf_op jit(solution)/shard_map/prepare/pallas_call | solution.py:573
  10.7 0.0 collective-permute-done.refs_1_
  10.7 0.4 %collective-permute-done.1.refs_2_ = f32[100,128]{1,0:T(8,128)S(1)} collective-permute-done((f32[100,128]{1,0:T(8,128)}, f32[100,128]{1,0:T(8,128)S(1)}, u32[]{:S(2)}, u32[]{:S(2)}) %collective-permute-start.1) | collective-permute-done | bytes 51232 | tf_op jit(solution)/shard_map/ppermute | solution.py:400
  11.1 1.4 %collective-permute-done.2.refs_3_ = f32[100,128]{1,0:T(8,128)S(1)} collective-permute-done((f32[100,128]{1,0:T(8,128)}, f32[100,128]{1,0:T(8,128)S(1)}, u32[]{:S(2)}, u32[]{:S(2)}) %collective-permute-start.2) | collective-permute-done | bytes 51232 | tf_op jit(solution)/shard_map/ppermute | solution.py:400
  12.5 0.0 copy-done.4
  12.5 1.1 %couple.1 = (f32[150,128]{1,0:T(8,128)S(1)}, f32[150,128]{1,0:T(8,128)S(1)}) custom-call(s32[16]{0:T(128)S(1)} %copy-done.3, f32[2,50]{1,0:T(2,128)S(1)} %copy-done.4, f32[2,4,16,128]{3,2,1,0:T(8,128)S(1)} %get-tuple-element.22.coupling, f32[100,128]{1,0:T(8,128)S(1)} %get-tuple-element.23.refs_0_, f32[100,128]{1,0:T(8,128)S(1)} %collective-permute-done.refs_1_, ...), custom_call_target="tpu_custom_call" | custom-call | tf_op jit(solution)/shard_map/couple/pallas_call | solution.py:625
  13.7 2.7 %collective-permute-start.3 = (f32[150,128]{1,0:T(8,128)S(1)}, f32[150,128]{1,0:T(8,128)S(1)}, u32[]{:S(2)}, u32[]{:S(2)}) collective-permute-start(f32[150,128]{1,0:T(8,128)S(1)} %get-tuple-element.28), channel_id=1, source_target_pairs={{0,8},{1,9},{4,12},{5,13},{8,0},{9,1},{12,4},{13,5},{2,10},{3,11},... | collective-permute-start | bytes 230408 | tf_op jit(solution)/shard_map/ppermute | solution.py:400
  16.4 1.6 %pack.1 = (bf16[4,256,256]{2,1,0:T(8,128)(2,1)S(1)}, f32[4,24,128]{2,1,0:T(8,128)S(1)}, f32[4,24,128]{2,1,0:T(8,128)S(1)}, f32[200,128]{1,0:T(8,128)S(1)}, f32[200,128]{1,0:T(8,128)S(1)}) custom-call(s32[16]{0:T(128)S(1)} %copy-done.3, f32[150,128]{1,0:T(8,128)S(1)} %get-tuple-element.27.own.after, f32[100,128]{1,0:T(8,128)S(1)} %get-tuple-element.23.refs_0_, ...), custom_call_target="tpu_custom_call" | custom-call | tf_op jit(solution)/shard_map/pack/pallas_call | solution.py:663
  17.9 0.4 %collective-permute-start.7 = (f32[200,128]{1,0:T(8,128)S(1)}, f32[200,128]{1,0:T(8,128)S(1)}, u32[]{:S(2)}, u32[]{:S(2)}) collective-permute-start(f32[200,128]{1,0:T(8,128)S(1)} %get-tuple-element.37), channel_id=1, source_target_pairs={{0,8},{1,9},{4,12},{5,13},{8,0},{9,1},{12,4},{13,5},{2,10},{3,11},... | collective-permute-start | bytes 307208 | tf_op jit(solution)/shard_map/ppermute | solution.py:400
  18.3 2.4 %collective-permute-done.3.other = f32[150,128]{1,0:T(8,128)S(1)} collective-permute-done((f32[150,128]{1,0:T(8,128)S(1)}, f32[150,128]{1,0:T(8,128)S(1)}, u32[]{:S(2)}, u32[]{:S(2)}) %collective-permute-start.3) | collective-permute-done | bytes 76832 | tf_op jit(solution)/shard_map/ppermute | solution.py:400
  20.7 0.6 %hand_out.1 = (f32[50,128]{1,0:T(8,128)S(1)}, f32[50,128]{1,0:T(8,128)S(1)}, f32[50,128]{1,0:T(8,128)S(1)}, f32[50,128]{1,0:T(8,128)S(1)}) custom-call(s32[16]{0:T(128)S(1)} %copy-done.3, f32[150,128]{1,0:T(8,128)S(1)} %get-tuple-element.27.own.after, f32[150,128]{1,0:T(8,128)S(1)} %collective-permute-done.3.other), custom_call_target="tpu_custom_call" | custom-call | tf_op jit(solution)/shard_map/hand_out/pallas_call | solution.py:692
  21.3 0.1 collective-permute-start.4
  21.4 3.0 %collective-permute-start.5 = (f32[50,128]{1,0:T(8,128)S(1)}, f32[50,128]{1,0:T(8,128)S(1)}, u32[]{:S(2)}, u32[]{:S(2)}) collective-permute-start(f32[50,128]{1,0:T(8,128)S(1)} %get-tuple-element.31), channel_id=1, source_target_pairs={{0,4},{1,5},{4,0},{5,1},{8,12},{9,13},{12,8},{13,9},{2,6},{3,7},{6... | collective-permute-start | bytes 76808 | tf_op jit(solution)/shard_map/ppermute | solution.py:400
  24.4 0.1 collective-permute-start.6
  24.5 1.2 %collective-permute-done.7.other = f32[200,128]{1,0:T(8,128)S(1)} collective-permute-done((f32[200,128]{1,0:T(8,128)S(1)}, f32[200,128]{1,0:T(8,128)S(1)}, u32[]{:S(2)}, u32[]{:S(2)}) %collective-permute-start.7) | collective-permute-done | bytes 102432 | tf_op jit(solution)/shard_map/ppermute | solution.py:400
  25.7 1.5 %spectrum.1 = f32[2,50,2,8,64]{4,3,2,1,0:T(8,128)} custom-call(f32[2,50]{1,0:T(2,128)S(1)} %copy-done.4, f32[200,128]{1,0:T(8,128)S(1)} %get-tuple-element.36.own, f32[200,128]{1,0:T(8,128)S(1)} %collective-permute-done.7.other, f32[64,128]{1,0:T(8,128)S(1)} %get-tuple-element.38.poly, f32[16,128]{1,0:T(8,128)S(1)} %get-tuple-element.39.gram), custom_call_target="tpu_custom_call" | custom-call | tf_op jit(solution)/shard_map/spectrum/pallas_call | solution.py:746
  27.2 0.0 collective-permute-done.4.refs_1_
  27.2 0.0 collective-permute-done.5.refs_2_
  27.2 0.5 %collective-permute-done.6.refs_3_ = f32[50,128]{1,0:T(8,128)S(1)} collective-permute-done((f32[50,128]{1,0:T(8,128)S(1)}, f32[50,128]{1,0:T(8,128)S(1)}, u32[]{:S(2)}, u32[]{:S(2)}) %collective-permute-start.6) | collective-permute-done | bytes 25632 | tf_op jit(solution)/shard_map/ppermute | solution.py:400
  27.7 0.0 copy-done.1
  27.7 0.0 copy-done
  27.7 2.4 %restore.1 = f32[50,4608]{1,0:T(8,128)} custom-call(s32[16]{0:T(128)S(1)} %copy-done.3, f32[50,128]{1,0:T(8,128)S(1)} %get-tuple-element.29.refs_0_, f32[50,128]{1,0:T(8,128)S(1)} %collective-permute-done.4.refs_1_, f32[50,128]{1,0:T(8,128)S(1)} %collective-permute-done.5.refs_2_, f32[50,128]{1,0:T(8,128)S(1)} %collective-permute-done.6.refs_3_, ...), custom_call_target="tpu_custom_call" | custom-call | tf_op jit(solution)/shard_map/restore/pallas_call | solution.py:346
Async XLA Ops:
  0.6 7.9 %copy-start.3 = (s32[16]{0:T(128)S(1)}, s32[16]{0:T(128)}, u32[]{:S(2)}) copy-start(s32[16]{0:T(128)} %lengths.11) | copy-start | bytes 196
  0.6 7.9 %copy-start.5 = (f32[16]{0:T(128)S(1)}, f32[16]{0:T(128)}, u32[]{:S(2)}) copy-start(f32[16]{0:T(128)} %latitude.1) | copy-start | bytes 196
  0.7 7.9 %copy-start.6 = (f32[16]{0:T(128)S(1)}, f32[16]{0:T(128)}, u32[]{:S(2)}) copy-start(f32[16]{0:T(128)} %weights.1) | copy-start | bytes 196
  0.7 11.9 %copy-start.4 = (f32[2,50]{1,0:T(2,128)S(1)}, f32[2,50]{1,0:T(2,128)}, u32[]{:S(2)}) copy-start(f32[2,50]{1,0:T(2,128)} %strength.5) | copy-start | bytes 1204
  0.7 27.1 %copy-start.1 = (f32[50,4608]{1,0:T(8,128)S(1)}, f32[50,4608]{1,0:T(8,128)}, u32[]{:S(2)}) copy-start(f32[50,4608]{1,0:T(8,128)} %refs_5_.1) | copy-start | bytes 2764804
  5.3 22.4 %copy-start = (f32[50,4608]{1,0:T(8,128)S(1)}, f32[50,4608]{1,0:T(8,128)}, u32[]{:S(2)}) copy-start(f32[50,4608]{1,0:T(8,128)} %refs_4_.1) | copy-start | bytes 2764804
  5.3 5.4 %collective-permute-start = (f32[100,128]{1,0:T(8,128)}, f32[100,128]{1,0:T(8,128)S(1)}, u32[]{:S(2)}, u32[]{:S(2)}) collective-permute-start(f32[100,128]{1,0:T(8,128)} %get-tuple-element.24), channel_id=1, source_target_pairs={{0,1},{1,0},{4,5},{5,4},{8,9},{9,8},{12,13},{13,12},{2,3},{3,2},{6... | collective-permute-start | bytes 153608 | tf_op jit(solution)/shard_map/ppermute | solution.py:400
  5.8 5.3 %collective-permute-start.1 = (f32[100,128]{1,0:T(8,128)}, f32[100,128]{1,0:T(8,128)S(1)}, u32[]{:S(2)}, u32[]{:S(2)}) collective-permute-start(f32[100,128]{1,0:T(8,128)} %get-tuple-element.25), channel_id=1, source_target_pairs={{0,4},{1,5},{4,0},{5,1},{8,12},{9,13},{12,8},{13,9},{2,6},{3,7},{6... | collective-permute-start | bytes 153608 | tf_op jit(solution)/shard_map/ppermute | solution.py:400
  8.4 4.1 %collective-permute-start.2 = (f32[100,128]{1,0:T(8,128)}, f32[100,128]{1,0:T(8,128)S(1)}, u32[]{:S(2)}, u32[]{:S(2)}) collective-permute-start(f32[100,128]{1,0:T(8,128)} %get-tuple-element.26), channel_id=1, source_target_pairs={{0,5},{1,4},{4,1},{5,0},{8,13},{9,12},{12,9},{13,8},{2,7},{3,6},{6... | collective-permute-start | bytes 153608 | tf_op jit(solution)/shard_map/ppermute | solution.py:400
  8.5 0.8 %copy-start.2 = (f32[100,128]{1,0:T(8,128)S(1)}, f32[100,128]{1,0:T(8,128)}, u32[]{:S(2)}) copy-start(f32[100,128]{1,0:T(8,128)} %get-tuple-element.21.message) | copy-start | bytes 153604
  13.7 7.0 %collective-permute-start.3 = (f32[150,128]{1,0:T(8,128)S(1)}, f32[150,128]{1,0:T(8,128)S(1)}, u32[]{:S(2)}, u32[]{:S(2)}) collective-permute-start(f32[150,128]{1,0:T(8,128)S(1)} %get-tuple-element.28), channel_id=1, source_target_pairs={{0,8},{1,9},{4,12},{5,13},{8,0},{9,1},{12,4},{13,5},{2,10},{3,11},... | collective-permute-start | bytes 230408 | tf_op jit(solution)/shard_map/ppermute | solution.py:400
  17.9 7.8 %collective-permute-start.7 = (f32[200,128]{1,0:T(8,128)S(1)}, f32[200,128]{1,0:T(8,128)S(1)}, u32[]{:S(2)}, u32[]{:S(2)}) collective-permute-start(f32[200,128]{1,0:T(8,128)S(1)} %get-tuple-element.37), channel_id=1, source_target_pairs={{0,8},{1,9},{4,12},{5,13},{8,0},{9,1},{12,4},{13,5},{2,10},{3,11},... | collective-permute-start | bytes 307208 | tf_op jit(solution)/shard_map/ppermute | solution.py:400
  21.3 5.9 %collective-permute-start.4 = (f32[50,128]{1,0:T(8,128)S(1)}, f32[50,128]{1,0:T(8,128)S(1)}, u32[]{:S(2)}, u32[]{:S(2)}) collective-permute-start(f32[50,128]{1,0:T(8,128)S(1)} %get-tuple-element.30), channel_id=1, source_target_pairs={{0,1},{1,0},{4,5},{5,4},{8,9},{9,8},{12,13},{13,12},{2,3},{3,2},{6... | collective-permute-start | bytes 76808 | tf_op jit(solution)/shard_map/ppermute | solution.py:400
  21.4 5.8 %collective-permute-start.5 = (f32[50,128]{1,0:T(8,128)S(1)}, f32[50,128]{1,0:T(8,128)S(1)}, u32[]{:S(2)}, u32[]{:S(2)}) collective-permute-start(f32[50,128]{1,0:T(8,128)S(1)} %get-tuple-element.31), channel_id=1, source_target_pairs={{0,4},{1,5},{4,0},{5,1},{8,12},{9,13},{12,8},{13,9},{2,6},{3,7},{6... | collective-permute-start | bytes 76808 | tf_op jit(solution)/shard_map/ppermute | solution.py:400
  24.4 3.3 %collective-permute-start.6 = (f32[50,128]{1,0:T(8,128)S(1)}, f32[50,128]{1,0:T(8,128)S(1)}, u32[]{:S(2)}, u32[]{:S(2)}) collective-permute-start(f32[50,128]{1,0:T(8,128)S(1)} %get-tuple-element.32), channel_id=1, source_target_pairs={{0,5},{1,4},{4,1},{5,0},{8,13},{9,12},{12,9},{13,8},{2,7},{3,6},{6... | collective-permute-start | bytes 76808 | tf_op jit(solution)/shard_map/ppermute | solution.py:400

commit v4 on v3

--- a/solution.py
+++ b/solution.py
@@ -167,30 +167,43 @@
     return jnp.minimum(begin >> 8, blocks - 1), jnp.where(within == 0, BLOCK, within)
 
 
-def load_fields(second, first, fields, sems, pieces):
-    width = fields.shape[2] // pieces
-    copies = []
-    for piece in range(pieces):
-        for index, source in enumerate((second, first)):
-            copies.append(
-                pltpu.make_async_copy(
-                    source.at[:, pl.ds(piece * width, width)],
-                    fields.at[index, :, pl.ds(piece * width, width)],
-                    sems.at[piece, index],
-                )
-            )
+def interleaved(message, upper):
+    channels = message.shape[0] // 2
+    both, second = message[:channels], message[channels:]
+    odd = ((lax.broadcasted_iota(jnp.int32, (1, LANES), 1) >> 3) & 1) == 1
+    return jnp.where(
+        upper,
+        jnp.where(odd, second, pltpu.roll(both, LANES - 8, 1)),
+        jnp.where(odd, pltpu.roll(second, 8, 1), both),
+    )
+
+
+def load_fields(second, first, fields, sems):
+    copies = [
+        pltpu.make_async_copy(source, fields.at[index], sems.at[index])
+        for index, source in enumerate((second, first))
+    ]
     for copy in copies:
         copy.start()
     return copies
 
 
-def analyse_kernel(per_device, lengths, strength, second, first, *refs):
-    messages, (fields, basis, cosine, sine, lhs, total, table, sems) = refs[:SHARES], refs[SHARES:]
+def analyse_kernel(per_device, lengths_held, strength_held, second, first, *refs):
+    messages, (across, rates, kept, fields, lengths, strength, basis, cosine, sine, lhs, total, table) = (
+        refs[:SHARES],
+        refs[SHARES:-3],
+    )
+    sems, length_sem, strength_sem = refs[-3:]
     channels, local = second.shape
     blocks = local // BLOCK
-    pieces = sems.shape[0]
-    copies = load_fields(second, first, fields, sems, pieces)
+    length_copy = pltpu.make_async_copy(lengths_held, lengths, length_sem)
+    length_copy.start()
+    strength_copy = pltpu.make_async_copy(strength_held, strength, strength_sem)
+    strength_copy.start()
+    copies = load_fields(second, first, fields, sems)
     me = device_id()
+    length_copy.wait()
+    strength_copy.wait()
     row_table(lengths, table, me, local, lengths.shape[0])
     fill_phases(table, me, per_device, blocks, cosine, sine, 1.0)
     wave_index = lax.broadcasted_iota(jnp.int32, (BLOCK, LANES), 1)
@@ -211,9 +224,12 @@
             low = (piece - high.astype(jnp.float32)).astype(jnp.bfloat16)
             lhs[buffer, pl.ds(index * PAD, channels), :] = high
             lhs[buffer, pl.ds((2 + index) * PAD, channels), :] = low
-        product = jnp.dot(lhs[buffer], basis[slot], preferred_element_type=jnp.float32)
-        value = (
-            product[: 2 * PAD, :LANES] + product[: 2 * PAD, LANES:] + product[2 * PAD :, :LANES]
+        product = jnp.dot(
+            lhs[buffer, : 2 * PAD, :], basis[slot], preferred_element_type=jnp.float32
+        )
+        value = product[:, :LANES] + product[:, LANES:]
+        value = value + jnp.dot(
+            lhs[buffer, 2 * PAD :, :], basis[slot, :, :LANES], preferred_element_type=jnp.float32
         )
         turned = (
             value * cosine[slot, pl.ds(block, 1), :]
@@ -222,12 +238,9 @@
         total[slot] = total[slot] + turned
 
     begin_slot = table[3 * SHARES]
-    waited = 0
+    for copy in copies:
+        copy.wait()
     for block in range(blocks):
-        while waited * (local // pieces) < (block + 1) * BLOCK:
-            copies[2 * waited].wait()
-            copies[2 * waited + 1].wait()
-            waited += 1
         place = block * BLOCK
         slot = begin_slot
         for later in range(1, SHARES):
@@ -236,6 +249,8 @@
         add_block(
             block, place, slot, 0, table[slot] + table[SHARES + slot] - place, block % lhs.shape[0]
         )
+        at = pl.ds(place, BLOCK)
+        kept[:, at] = fields[0, :, at] + fields[1, :, at]
     for later in range(1, SHARES):
         block, low_end = split_block(table[2 * SHARES + later], blocks)
         place = pl.multiple_of(block * BLOCK, BLOCK)
@@ -243,6 +258,7 @@
 
     rate_first = column(strength[0:1, :])
     rate_second = column(strength[1:2, :])
+    rates[...] = jnp.broadcast_to(rate_first, rates.shape)
     lane = lax.broadcasted_iota(jnp.int32, (1, LANES), 1)
     chunk = (lane >> 4) & 3
     pairs = []
@@ -260,42 +276,57 @@
                     moved = pltpu.roll(moved, ((slot - share) * GROUP) % LANES, 1)
                 value = jnp.where(chunk == slot, moved, value)
             messages[share][pl.ds(which * channels, channels), :] = value
+        across[pl.ds(share * channels, channels), :] = interleaved(
+            messages[share][...], me < SHARES
+        )
+
+
+def in_hbm(*values):
+    return [pltpu.with_memory_space_constraint(value, pltpu.HBM) for value in values]
 
 
 def analyse(lengths, strength, second, first, per_device):
     channels, local = second.shape
     blocks = local // BLOCK
-    pieces = 3
     phase_rows = -(-blocks // 8) * 8
     return pl.pallas_call(
         functools.partial(analyse_kernel, per_device),
-        out_shape=[jax.ShapeDtypeStruct((2 * channels, LANES), jnp.float32)] * SHARES,
-        in_specs=[
-            pl.BlockSpec(memory_space=pltpu.SMEM),
-            pl.BlockSpec(memory_space=pltpu.VMEM),
-            pl.BlockSpec(memory_space=pltpu.HBM),
-            pl.BlockSpec(memory_space=pltpu.HBM),
+        out_shape=[pltpu.VMEM((2 * channels, LANES), jnp.float32)] * SHARES
+        + [
+            pltpu.VMEM((SHARES * channels, LANES), jnp.float32),
+            pltpu.VMEM((channels, LANES), jnp.float32),
+            pltpu.VMEM((channels, local), jnp.float32),
         ],
-        out_specs=[pl.BlockSpec(memory_space=pltpu.VMEM)] * SHARES,
+        in_specs=[pl.BlockSpec(memory_space=pltpu.HBM)] * 4,
+        out_specs=[pl.BlockSpec(memory_space=pltpu.VMEM)] * (SHARES + 3),
         scratch_shapes=[
             pltpu.VMEM((2, channels, local), jnp.float32),
+            pltpu.SMEM(lengths.shape, jnp.int32),
+            pltpu.VMEM(strength.shape, jnp.float32),
             pltpu.VMEM((SHARES, BLOCK, 2 * LANES), jnp.bfloat16),
             pltpu.VMEM((SHARES, phase_rows, LANES), jnp.float32),
             pltpu.VMEM((SHARES, phase_rows, LANES), jnp.float32),
             pltpu.VMEM((4, 4 * PAD, BLOCK), jnp.bfloat16),
             pltpu.VMEM((SHARES, 2 * PAD, LANES), jnp.float32),
             pltpu.SMEM((16,), jnp.int32),
-            pltpu.SemaphoreType.DMA((pieces, 2)),
+            pltpu.SemaphoreType.DMA((2,)),
+            pltpu.SemaphoreType.DMA,
+            pltpu.SemaphoreType.DMA,
         ],
-        compiler_params=pltpu.CompilerParams(vmem_limit_bytes=FULL),
+        compiler_params=pltpu.CompilerParams(vmem_limit_bytes=32 * 1024 * 1024),
         name="analyse",
-    )(lengths, strength, second, first)
+    )(*in_hbm(lengths, strength, second, first))
 
 
 def restore_kernel(lengths, *refs):
-    messages, (second, first, basis, cosine, sine, out, coeff, table) = refs[:SHARES], refs[SHARES:]
-    channels, local = second.shape
+    messages, (kept, basis, cosine, sine, out, held, coeff, ends, table, sems) = (
+        refs[:SHARES],
+        refs[SHARES:],
+    )
+    channels, local = kept.shape
     blocks = local // BLOCK
+    pieces = sems.shape[0]
+    width = local // pieces
     me = device_id()
     row_table(lengths, table, me, local, lengths.shape[0])
     lane = lax.broadcasted_iota(jnp.int32, (1, LANES), 1)
@@ -311,7 +342,7 @@
         coeff[slot, :channels, :] = value
     within = lax.broadcasted_iota(jnp.int32, (1, BLOCK), 1)
 
-    def block_value(block, place, slot):
+    def block_value(block, slot):
         value = coeff[slot]
         turned = (
             value * cosine[slot, pl.ds(block, 1), :]
@@ -322,40 +353,55 @@
         left = jnp.concatenate([high, low], axis=0)
         left = jnp.concatenate([left, left], axis=1)
         product = jnp.dot(left, basis[slot], preferred_element_type=jnp.float32)
-        value = product[:PAD] + product[PAD:]
-        kept = second[:, pl.ds(place, BLOCK)] + first[:, pl.ds(place, BLOCK)]
-        return kept - value[:channels]
+        return product[:channels] + product[PAD : PAD + channels]
 
     begin_slot = table[3 * SHARES]
+    splits = []
+    for later in range(1, SHARES):
+        block, low_end = split_block(table[2 * SHARES + later], blocks)
+        splits.append(jnp.where(low_end < BLOCK, block, blocks))
+        ends[later] = block_value(block, (begin_slot + later) & 3)
+    copies = []
     for block in range(blocks):
         place = block * BLOCK
         slot = begin_slot
+        split = jnp.int32(0)
         for later in range(1, SHARES):
             slot = slot + jnp.where(table[2 * SHARES + later] <= place, 1, 0)
-        out[:, pl.ds(place, BLOCK)] = block_value(block, place, slot & 3)
-    for later in range(1, SHARES):
-        block, low_end = split_block(table[2 * SHARES + later], blocks)
-        place = pl.multiple_of(block * BLOCK, BLOCK)
-        value = block_value(block, place, (begin_slot + later) & 3)
-        before = out[:, pl.ds(place, BLOCK)]
-        out[:, pl.ds(place, BLOCK)] = jnp.where(within >= low_end, value, before)
-
-
-def restore(lengths, messages, second, first, tables):
-    channels, local = second.shape
+            split = jnp.where(splits[later - 1] == block, later, split)
+        slot = slot & 3
+        end = table[slot] + table[SHARES + slot] - place
+        value = jnp.where(within < end, block_value(block, slot), ends[split])
+        held[:, pl.ds(place, BLOCK)] = kept[:, pl.ds(place, BLOCK)] - value
+        if (place + BLOCK) % width == 0:
+            at = pl.ds(place + BLOCK - width, width)
+            copies.append(
+                pltpu.make_async_copy(held.at[:, at], out.at[:, at], sems.at[len(copies)])
+            )
+            copies[-1].start()
+    for copy in copies:
+        copy.wait()
+
+
+def restore(lengths, messages, kept, tables):
+    channels, local = kept.shape
+    pieces = math.gcd(local // BLOCK, 6)
     return pl.pallas_call(
         restore_kernel,
         out_shape=jax.ShapeDtypeStruct((channels, local), jnp.float32),
         in_specs=[pl.BlockSpec(memory_space=pltpu.SMEM)]
-        + [pl.BlockSpec(memory_space=pltpu.VMEM)] * (SHARES + 5),
-        out_specs=pl.BlockSpec(memory_space=pltpu.VMEM),
+        + [pl.BlockSpec(memory_space=pltpu.VMEM)] * (SHARES + 4),
+        out_specs=pl.BlockSpec(memory_space=pl.ANY),
         scratch_shapes=[
+            pltpu.VMEM((channels, local), jnp.float32),
             pltpu.VMEM((SHARES, PAD, LANES), jnp.float32),
+            pltpu.VMEM((SHARES, channels, BLOCK), jnp.float32),
             pltpu.SMEM((16,), jnp.int32),
+            pltpu.SemaphoreType.DMA((pieces,)),
         ],
         compiler_params=pltpu.CompilerParams(vmem_limit_bytes=32 * 1024 * 1024),
         name="restore",
-    )(lengths, *messages, second, first, *tables)
+    )(lengths, *messages, kept, *tables)
 
 
 def fill_tables(table, me, per_device, basis, cosine, sine, blocks):
@@ -368,7 +414,7 @@
         basis[slot, LANES:, :] = low
 
 
-def tables_kernel(per_device, local, lengths, basis, cosine, sine, table):
+def tables_kernel(per_device, local, lengths, after, basis, cosine, sine, table):
     me = device_id()
     row_table(lengths, table, me, local, lengths.shape[0])
     fill_tables(table, me, per_device, basis, cosine, sine, local // BLOCK)
@@ -383,16 +429,16 @@
     ]
 
 
-def tables_of(lengths, local, per_device):
+def tables_of(lengths, after, local, per_device):
     return pl.pallas_call(
         functools.partial(tables_kernel, per_device, local),
         out_shape=table_shapes(local),
-        in_specs=[pl.BlockSpec(memory_space=pltpu.SMEM)],
+        in_specs=[pl.BlockSpec(memory_space=pltpu.SMEM), pl.BlockSpec(memory_space=pl.ANY)],
         out_specs=[pl.BlockSpec(memory_space=pltpu.VMEM)] * 3,
         scratch_shapes=[pltpu.SMEM((16,), jnp.int32)],
         compiler_params=pltpu.CompilerParams(vmem_limit_bytes=SMALL),
         name="tables",
-    )(lengths)
+    )(lengths, after)
 
 
 def swapped(value, mask):
@@ -483,10 +529,8 @@
 
 
 def prepare_kernel(
-    per_device, count, local, lengths, latitude, weights, message, coupling, poly, gram, kept, pt, square, sem
+    count, local, lengths, latitude, weights, coupling, poly, gram, pt, square
 ):
-    copy = pltpu.make_async_copy(message, kept, sem)
-    copy.start()
     me = device_id()
     down = lax.broadcasted_iota(jnp.int32, (8, LANES), 0)
     lane = lax.broadcasted_iota(jnp.int32, (8, LANES), 1)
@@ -552,13 +596,23 @@
         coupling[1, target] = twice[target] * scale[target : target + 1, :]
     mine = pt[SHARES]
     factor = doubling[SHARES : SHARES + 1, :] * (float(local * count) ** -0.5)
-    poly[...] = mine * factor
-    for step in range(GROUP):
-        moved = pltpu.roll(mine, (LANES - 8 * step) % LANES, 1) if step else mine
-        gram[pl.ds(step, 1), :] = weight[SHARES : SHARES + 1, :] * jnp.sum(
-            mine * moved, axis=0, keepdims=True
-        )
-    copy.wait()
+    products = lax.dot_general(
+        mine, mine, (((0,), (0,)), ((), ())), precision=HIGHEST, preferred_element_type=jnp.float32
+    )
+    same = (lax.broadcasted_iota(jnp.int32, (LANES, LANES), 0) & 7) == (
+        lax.broadcasted_iota(jnp.int32, (LANES, LANES), 1) & 7
+    )
+    products = jnp.where(same, products * weight[SHARES : SHARES + 1, :], 0.0)
+    turned = jnp.concatenate([mine * factor, jnp.zeros_like(mine)], axis=0).T
+    for value, out in ((turned, poly), (products, gram)):
+        high = value.astype(jnp.bfloat16)
+        low = (value - high.astype(jnp.float32)).astype(jnp.bfloat16)
+        out[...] = jnp.concatenate([high, high, low], axis=0)
+
+
+def three_parts(value):
+    rounded = value.astype(jnp.bfloat16).astype(jnp.float32)
+    return [rounded, value - rounded, rounded]
 
 
 SMEM = pl.BlockSpec(memory_space=pltpu.SMEM)
@@ -569,38 +623,35 @@
     return jax.ShapeDtypeStruct(shape, jnp.float32)
 
 
-def prepare(lengths, latitude, weights, message, per_device, count, local):
+def prepare(lengths, latitude, weights, count, local):
     return pl.pallas_call(
-        functools.partial(prepare_kernel, per_device, count, local),
+        functools.partial(prepare_kernel, count, local),
         out_shape=[
             floats(2, SHARES, GROUP, LANES),
-            floats(WAVES, LANES),
-            floats(GROUP, LANES),
-            floats(*message.shape),
+            jax.ShapeDtypeStruct((3 * LANES, LANES), jnp.bfloat16),
+            jax.ShapeDtypeStruct((3 * LANES, LANES), jnp.bfloat16),
         ],
-        in_specs=[SMEM] * 3 + [pl.BlockSpec(memory_space=pl.ANY)],
-        out_specs=[VMEM] * 4,
+        in_specs=[SMEM] * 3,
+        out_specs=[VMEM] * 3,
         scratch_shapes=[
             pltpu.VMEM((SHARES + 1, WAVES, LANES), jnp.float32),
             pltpu.VMEM((SHARES, GROUP, LANES), jnp.float32),
-            pltpu.SemaphoreType.DMA,
         ],
         compiler_params=pltpu.CompilerParams(vmem_limit_bytes=SMALL),
         name="prepare",
-    )(lengths, latitude, weights, message)
-
-
-def couple_kernel(local, lengths, strength, coupling, *refs):
+    )(lengths, latitude, weights)
+
+
+def couple_kernel(local, lengths, rates, coupling, *refs):
     messages, (own, other) = [ref[...] for ref in refs[:SHARES]], refs[SHARES:]
-    channels = strength.shape[1]
+    channels = rates.shape[0]
     me = device_id()
     *firsts, far = first_rows(lengths, near(me) + [(me ^ SHARES) & SHARES], local)
     arrays = by_row(messages, firsts)
-    rate_first = column(strength[0:1, :])
     sums = [jnp.zeros((channels, LANES), jnp.float32)] * SHARES
     for source in range(SHARES):
         both = arrays[source][:channels]
-        second = rate_first * arrays[source][channels:]
+        second = rates[...] * arrays[source][channels:]
         for step in range(SHARES):
             moved_both = group_roll(both, step)
             moved_second = group_roll(second, step)
@@ -620,8 +671,8 @@
             out[pl.ds(index * channels, channels), :] = value
 
 
-def couple(lengths, strength, coupling, messages, local):
-    channels = strength.shape[1]
+def couple(lengths, rates, coupling, messages, local):
+    channels = rates.shape[0]
     return pl.pallas_call(
         functools.partial(couple_kernel, local),
         out_shape=[floats(WINDOW * channels, LANES)] * 2,
@@ -629,46 +680,33 @@
         out_specs=[VMEM] * 2,
         compiler_params=pltpu.CompilerParams(vmem_limit_bytes=SMALL),
         name="couple",
-    )(lengths, strength, coupling, *messages)
-
-
-def pack_kernel(per_device, local, lengths, after, *refs):
-    messages, (basis, cosine, sine, own, other, table) = (
-        [ref[...] for ref in refs[:SHARES]],
-        refs[SHARES:],
+    )(lengths, rates, coupling, *messages)
+
+
+def pack_kernel(local, lengths, after, *refs):
+    messages, (across, rows, *chunks) = [ref[...] for ref in refs[:SHARES]], refs[SHARES:]
+    channels = messages[0].shape[0] // 2
+    me = device_id()
+    for share in range(SHARES):
+        chunks[share][...] = across[pl.ds(share * channels, channels), :]
+    arrays = by_row(
+        [interleaved(message, me >= SHARES) for message in messages],
+        first_rows(lengths, near(me), local),
     )
-    rows = messages[0].shape[0]
-    me = device_id()
-    row_table(lengths, table, me, local, lengths.shape[0])
-    fill_tables(table, me, per_device, basis, cosine, sine, local // BLOCK)
-    arrays = by_row(messages, first_rows(lengths, near(me), local))
-    lane = lax.broadcasted_iota(jnp.int32, (1, LANES), 1)
-    array = (lane >> 6) * 2 + ((lane >> 3) & 1)
-    upper = me >= SHARES
-    for part in range(2):
-        halves = []
-        for half in range(2):
-            value = jnp.zeros((rows, LANES), jnp.float32)
-            for index in range(SHARES):
-                shift = (64 * (index >> 1) + 8 * (index & 1) - 64 * part - 8 * half) % LANES
-                moved = pltpu.roll(arrays[index], shift, 1) if shift else arrays[index]
-                value = jnp.where(array == index, moved, value)
-            halves.append(value)
-        own[pl.ds(part * rows, rows), :] = jnp.where(upper, halves[1], halves[0])
-        other[pl.ds(part * rows, rows), :] = jnp.where(upper, halves[0], halves[1])
-
-
-def pack(lengths, after, messages, local, per_device):
-    rows = messages[0].shape[0]
+    for index in range(SHARES):
+        rows[pl.ds(index * channels, channels), :] = arrays[index]
+
+
+def pack(lengths, after, messages, across, local):
+    channels = messages[0].shape[0] // 2
     return pl.pallas_call(
-        functools.partial(pack_kernel, per_device, local),
-        out_shape=table_shapes(local) + [floats(2 * rows, LANES)] * 2,
-        in_specs=[SMEM, pl.BlockSpec(memory_space=pl.ANY)] + [VMEM] * SHARES,
-        out_specs=[VMEM] * 5,
-        scratch_shapes=[pltpu.SMEM((16,), jnp.int32)],
+        functools.partial(pack_kernel, local),
+        out_shape=[floats(SHARES * channels, LANES)] + [floats(channels, LANES)] * SHARES,
+        in_specs=[SMEM, pl.BlockSpec(memory_space=pl.ANY)] + [VMEM] * (SHARES + 1),
+        out_specs=[VMEM] * (SHARES + 1),
         compiler_params=pltpu.CompilerParams(vmem_limit_bytes=SMALL),
         name="pack",
-    )(lengths, after, *messages)
+    )(lengths, after, *messages, across)
 
 
 def hand_out_kernel(local, lengths, own, other, *outs):
@@ -699,88 +737,89 @@
     )(lengths, own, other)
 
 
-def spectrum_kernel(strength, own, other, poly, gram, out):
-    channels = strength.shape[1]
-    rate_first = column(strength[0:1, :])
+def spectrum_kernel(local, lengths, rates, rows, *refs):
+    chunks, (poly, gram, out) = [ref[...] for ref in refs[:SHARES]], refs[SHARES:]
+    channels = rates.shape[0]
+    far = [device ^ SHARES for device in near(device_id())]
+    arrays = by_row(chunks, first_rows(lengths, far, local))
+    for index in range(SHARES):
+        arrays[index] = arrays[index] + rows[pl.ds(index * channels, channels), :]
+    across = lax.broadcasted_iota(jnp.int32, (1, LANES), 1)
+    held = (across >> 6) * 2 + ((across >> 3) & 1)
+
+    def by_lane(part, field):
+        value = jnp.zeros((channels, LANES), jnp.float32)
+        for index in range(SHARES):
+            shift = (64 * (index >> 1) + 8 * (index & 1) - 64 * part - 8 * field) % LANES
+            moved = pltpu.roll(arrays[index], shift, 1) if shift else arrays[index]
+            value = jnp.where(held == index, moved, value)
+        return value
+
     down = lax.broadcasted_iota(jnp.int32, (8, LANES), 0)
     lane = lax.broadcasted_iota(jnp.int32, (8, LANES), 1)
     match = jnp.where(down == (lane & 7), 1.0, 0.0)[None]
-    high = poly[...].astype(jnp.bfloat16)
-    low = (poly[...] - high.astype(jnp.float32)).astype(jnp.bfloat16)
-    right = jnp.concatenate(
-        [
-            jnp.concatenate([high, high], axis=1),
-            jnp.concatenate([low, jnp.zeros_like(low)], axis=1),
-        ],
-        axis=0,
-    )
     for part in range(2):
-        at = pl.ds(2 * part * channels, channels)
-        both = own[at, :] + other[at, :]
-        at = pl.ds((2 * part + 1) * channels, channels)
-        second = own[at, :] + other[at, :]
-        first = both - second
-        for step in range(GROUP):
-            moved = pltpu.roll(second, (LANES - 8 * step) % LANES, 1) if step else second
-            first = first - rate_first * (gram[pl.ds(step, 1), :] * moved)
+        second = by_lane(part, 1)
+        left = jnp.concatenate([side.astype(jnp.bfloat16) for side in three_parts(second)], axis=1)
+        first = by_lane(part, 0) - second
+        first = first - rates[...] * jnp.dot(left, gram[...], preferred_element_type=jnp.float32)
         for index, value in enumerate((first, second)):
             if part:
                 value = -value
-            rounded = value.astype(jnp.bfloat16).astype(jnp.float32)
-            sides = []
-            for side in (rounded, value - rounded):
-                spread = side[:, None, :] * match
-                sides.append(spread.reshape(8 * channels, LANES).astype(jnp.bfloat16))
-            product = lax.dot_general(
-                jnp.concatenate(sides, axis=1),
-                right,
-                (((1,), (1,)), ((), ())),
+            high, low, _ = three_parts(value)
+            sides = [
+                (side[:, None, :] * match).reshape(8 * channels, LANES).astype(jnp.bfloat16)
+                for side in (high, low)
+            ]
+            product = jnp.dot(
+                jnp.concatenate(sides + sides[:1], axis=1),
+                poly[...],
                 preferred_element_type=jnp.float32,
             )
-            result = product[:, :WAVES] + product[:, WAVES:]
-            out[index, :, part] = result.reshape(channels, 8, WAVES)
-
-
-def spectrum(strength, own, other, poly, gram):
-    channels = strength.shape[1]
+            out[index, :, part] = product[:, :WAVES].reshape(channels, 8, WAVES)
+
+
+def spectrum(lengths, rates, rows, chunks, poly, gram, local):
+    channels = rates.shape[0]
     return pl.pallas_call(
-        spectrum_kernel,
+        functools.partial(spectrum_kernel, local),
         out_shape=floats(2, channels, 2, 8, WAVES),
-        in_specs=[VMEM] * 5,
+        in_specs=[SMEM] + [VMEM] * (SHARES + 4),
         out_specs=VMEM,
         compiler_params=pltpu.CompilerParams(vmem_limit_bytes=SMALL),
         name="spectrum",
-    )(strength, own, other, poly, gram)
-
-
-def middle_small(received, strength, lengths, latitude, weights, local, per_device, count):
-    coupling, poly, gram, kept = prepare(
-        lengths, latitude, weights, received[0], per_device, count, local
-    )
-    received = [kept] + received[1:]
-    part, sent_part = couple(lengths, strength, coupling, received, local)
+    )(lengths, rates, rows, *chunks, poly, gram)
+
+
+def middle_small(
+    received, across, rates, lengths, latitude, weights, local, per_device, count
+):
+    across = swapped(across, SHARES)
+    coupling, poly, gram = prepare(lengths, latitude, weights, count, local)
+    part, sent_part = couple(lengths, rates, coupling, received, local)
     other_part = swapped(sent_part, SHARES)
-    *tables, own, sent = pack(lengths, part, received, local, per_device)
-    other = swapped(sent, SHARES)
+    tables = tables_of(lengths, part, local, per_device)
+    rows, *chunks = pack(lengths, tables[1], received, across, local)
+    chunks = [chunks[0]] + [swapped(chunks[i], i) for i in range(1, SHARES)]
     replies = hand_out(lengths, part, other_part, local)
-    return replies, tables, (strength, own, other, poly, gram)
+    return replies, tables, (lengths, rates, rows, chunks, poly, gram, local)
 
 
 def on_device(cot_first, cot_second, strength, lengths, latitude, weights):
     local = cot_first.shape[1]
     count = lax.axis_size(AXES)
     per_device = WAVES // count
-    messages = analyse(lengths, strength, cot_second, cot_first, per_device)
+    *messages, across, rates, kept = analyse(lengths, strength, cot_second, cot_first, per_device)
     received = [messages[0]] + [swapped(messages[i], i) for i in range(1, SHARES)]
-    arguments = (received, strength, lengths, latitude, weights, local, per_device)
+    arguments = (lengths, latitude, weights, local, per_device)
     small = count == 2 * SHARES and lengths.shape[0] == GROUP
     if small:
-        replies, tables, pieces = middle_small(*arguments, count)
+        replies, tables, pieces = middle_small(received, across, rates, *arguments, count)
     else:
-        replies, grad_target = middle_general(*arguments)
-        tables = tables_of(lengths, local, per_device)
+        replies, grad_target = middle_general(received, strength, *arguments)
+        tables = tables_of(lengths, replies[0], local, per_device)
     answers = [replies[0]] + [swapped(replies[i], i) for i in range(1, SHARES)]
-    grad_state = restore(lengths, answers, cot_second, cot_first, tables)
+    grad_state = restore(lengths, answers, kept, tables)
     if small:
         grad_target = spectrum(*pieces)
     return (grad_state, grad_target)

time: 30.4 us -> 27.4 us (0.901)
  waiting for transfers between devices: 5.93 us -> 1.4 us
  starting transfers between devices: 9.41 us -> 12.2 us
  local copies, waits for them, and re-layouts: 0.83 us -> 0.01 us
    ppermute x8 -> x11, waiting for transfers between devices: 5.93 us -> 1.4 us  [swapped(): return lax.ppermute(value, AXES, [(i, i ^ mask) for i in range(count)])]
    ppermute x8 -> x11, starting transfers between devices: 9.41 us -> 12.2 us  [swapped(): return lax.ppermute(value, AXES, [(i, i ^ mask) for i in range(count)])]
    pallas_call x1, Pallas kernels: 4.6 us -> 3.21 us  [analyse(): pl.pallas_call(functools.partial(analyse_kernel, per_device), out_shape=[...]
    pallas_call x3 -> x4, Pallas kernels: 4.41 us -> 5.64 us  [the longest x1 2.42 us: spectrum(): pl.pallas_call(functools.partial(spectrum_kernel, local), out_shape=float...]
    unnamed x14 -> x6, local copies, waits for them, and re-layouts: 0.83 us -> 0.01 us
  transfers between devices with their start and end apart: 8 -> 11, of which waited for: 5 -> 1; matrix products, arithmetic and copies ran while one was open for 0% -> 0% of each run, Pallas kernels for 17% -> 27%
where the time goes in v4:
time: 27.4 us; the launch traced here: 27.2 us
  Pallas kernels  12.9 us (47%)
  starting transfers between devices  12.2 us (45%)
  waiting for transfers between devices  1.4 us (5%)
  between operations  0.72 us (3%)
    ppermute x11, starting transfers between devices, swapped(): return lax.ppermute(value, AXES, [(i, i ^ mask) for i in range(count)])  12.2 us
    pallas_call x1, Pallas kernels, analyse(): pl.pallas_call(functools.partial(analyse_kernel, per_device), out_shape=[...  3.21 us
    pallas_call x1, Pallas kernels, spectrum(): pl.pallas_call(functools.partial(spectrum_kernel, local), out_shape=float...  2.42 us
    pallas_call x1, Pallas kernels, restore(): pl.pallas_call(restore_kernel, out_shape=jax.ShapeDtypeStruct((channels,...  2.22 us
    ppermute x11, waiting for transfers between devices, swapped(): return lax.ppermute(value, AXES, [(i, i ^ mask) for i in range(count)])  1.4 us
    pallas_call x1, Pallas kernels, tables_of(): pl.pallas_call(functools.partial(tables_kernel, per_device, local), out_s...  1.3 us
    pallas_call x1, Pallas kernels, prepare(): pl.pallas_call(functools.partial(prepare_kernel, count, local), out_shape...  1.23 us
    pallas_call x1, Pallas kernels, couple(): pl.pallas_call(functools.partial(couple_kernel, local), out_shape=[floats...  1.18 us
  transfers between devices with their start and end apart: 11, of which 1 were waited for; matrix products, arithmetic and copies ran while one was open for 0% of the time, Pallas kernels for 27%

profile of v4, /device:TPU:0, one launch (start us, length us, event | category | flops | bytes accessed | tf_op | source)
XLA Modules:
  0.0 27.2 jit_solution(11491360896547297158)
XLA Ops:
  0.6 3.2 %analyse.1 = (f32[100,128]{1,0:T(8,128)S(1)}, f32[100,128]{1,0:T(8,128)S(1)}, f32[100,128]{1,0:T(8,128)S(1)}, f32[100,128]{1,0:T(8,128)S(1)}, f32[200,128]{1,0:T...) custom-call(s32[16]{0:T(128)} %lengths.13, f32[2,50]{1,0:T(2,128)} %strength_held.1, f32[50,4608]{1,0:T(8,128)} %second.1, ...), custom_call_target="tpu_custom_call" | custom-call | tf_op jit(solution)/shard_map/analyse/pallas_call | solution.py:292
  3.8 0.5 %collective-permute-start = (f32[100,128]{1,0:T(8,128)S(1)}, f32[100,128]{1,0:T(8,128)S(1)}, u32[]{:S(2)}, u32[]{:S(2)}) collective-permute-start(f32[100,128]{1,0:T(8,128)S(1)} %get-tuple-element.29), channel_id=1, source_target_pairs={{0,1},{1,0},{4,5},{5,4},{8,9},{9,8},{12,13},{13,12},{2,3},{3,2},{6... | collective-permute-start | bytes 153608 | tf_op jit(solution)/shard_map/ppermute | solution.py:446
  4.4 2.6 %collective-permute-start.1 = (f32[100,128]{1,0:T(8,128)S(1)}, f32[100,128]{1,0:T(8,128)S(1)}, u32[]{:S(2)}, u32[]{:S(2)}) collective-permute-start(f32[100,128]{1,0:T(8,128)S(1)} %get-tuple-element.30), channel_id=1, source_target_pairs={{0,4},{1,5},{4,0},{5,1},{8,12},{9,13},{12,8},{13,9},{2,6},{3,7},{6... | collective-permute-start | bytes 153608 | tf_op jit(solution)/shard_map/ppermute | solution.py:446
  7.0 0.0 copy-start
  7.0 0.0 copy-start.1
  7.0 0.0 copy-start.2
  7.0 0.1 collective-permute-start.2
  7.2 2.7 %collective-permute-start.7 = (f32[200,128]{1,0:T(8,128)S(1)}, f32[200,128]{1,0:T(8,128)S(1)}, u32[]{:S(2)}, u32[]{:S(2)}) collective-permute-start(f32[200,128]{1,0:T(8,128)S(1)} %get-tuple-element.42), channel_id=1, source_target_pairs={{0,8},{1,9},{4,12},{5,13},{8,0},{9,1},{12,4},{13,5},{2,10},{3,11},... | collective-permute-start | bytes 307208 | tf_op jit(solution)/shard_map/ppermute | solution.py:446
  9.8 0.0 copy-done
  9.8 0.0 copy-done.1
  9.8 0.0 copy-done.2
  9.8 1.2 %prepare.1 = (f32[2,4,16,128]{3,2,1,0:T(8,128)S(1)}, bf16[384,128]{1,0:T(8,128)(2,1)S(1)}, bf16[384,128]{1,0:T(8,128)(2,1)S(1)}) custom-call(s32[16]{0:T(128)S(1)} %copy-done, f32[16]{0:T(128)S(1)} %copy-done.1, f32[16]{0:T(128)S(1)} %copy-done.2), custom_call_target="tpu_custom_call" | custom-call | tf_op jit(solution)/shard_map/prepare/pallas_call | solution.py:627
  11.1 0.0 collective-permute-done.refs_1_
  11.1 0.0 collective-permute-done.1.refs_2_
  11.1 0.0 collective-permute-done.2.refs_3_
  11.1 1.2 %couple.1 = (f32[150,128]{1,0:T(8,128)S(1)}, f32[150,128]{1,0:T(8,128)S(1)}) custom-call(s32[16]{0:T(128)S(1)} %copy-done, f32[50,128]{1,0:T(8,128)S(1)} %get-tuple-element.26.rates, f32[2,4,16,128]{3,2,1,0:T(8,128)S(1)} %get-tuple-element.27.coupling, f32[100,128]{1,0:T(8,128)S(1)} %get-tuple-element.28.refs_0_, ...), custom_call_target="tpu_custom_call" | custom-call | tf_op jit(solution)/shard_map/couple/pallas_call | solution.py:676
  12.3 2.3 %collective-permute-start.3 = (f32[150,128]{1,0:T(8,128)S(1)}, f32[150,128]{1,0:T(8,128)S(1)}, u32[]{:S(2)}, u32[]{:S(2)}) collective-permute-start(f32[150,128]{1,0:T(8,128)S(1)} %get-tuple-element.33), channel_id=1, source_target_pairs={{0,8},{1,9},{4,12},{5,13},{8,0},{9,1},{12,4},{13,5},{2,10},{3,11},... | collective-permute-start | bytes 230408 | tf_op jit(solution)/shard_map/ppermute | solution.py:446
  14.6 1.3 %tables.1 = (bf16[4,256,256]{2,1,0:T(8,128)(2,1)S(1)}, f32[4,24,128]{2,1,0:T(8,128)S(1)}, f32[4,24,128]{2,1,0:T(8,128)S(1)}) custom-call(s32[16]{0:T(128)S(1)} %copy-done, f32[150,128]{1,0:T(8,128)S(1)} %get-tuple-element.32.own.after), custom_call_target="tpu_custom_call" | custom-call | tf_op jit(solution)/shard_map/tables/pallas_call | solution.py:433
  16.0 0.0 collective-permute-done.7.refs_4_
  16.0 0.7 %pack.1 = (f32[200,128]{1,0:T(8,128)S(1)}, f32[50,128]{1,0:T(8,128)S(1)}, f32[50,128]{1,0:T(8,128)S(1)}, f32[50,128]{1,0:T(8,128)S(1)}, f32[50,128]{1,0:T(8,128)S(1)}) custom-call(s32[16]{0:T(128)S(1)} %copy-done, f32[4,24,128]{2,1,0:T(8,128)S(1)} %get-tuple-element.40.refs_6_.after, f32[100,128]{1,0:T(8,128)S(1)} %get-tuple-element.28.refs_0_, ...), custom_call_target="tpu_custom_call" | custom-call | tf_op jit(solution)/shard_map/pack/pallas_call | solution.py:702
  16.7 0.3 %collective-permute-start.8 = (f32[50,128]{1,0:T(8,128)S(1)}, f32[50,128]{1,0:T(8,128)S(1)}, u32[]{:S(2)}, u32[]{:S(2)}) collective-permute-start(f32[50,128]{1,0:T(8,128)S(1)} %get-tuple-element.45), channel_id=1, source_target_pairs={{0,1},{1,0},{4,5},{5,4},{8,9},{9,8},{12,13},{13,12},{2,3},{3,2},{6... | collective-permute-start | bytes 76808 | tf_op jit(solution)/shard_map/ppermute | solution.py:446
  17.0 0.9 %collective-permute-start.9 = (f32[50,128]{1,0:T(8,128)S(1)}, f32[50,128]{1,0:T(8,128)S(1)}, u32[]{:S(2)}, u32[]{:S(2)}) collective-permute-start(f32[50,128]{1,0:T(8,128)S(1)} %get-tuple-element.46), channel_id=1, source_target_pairs={{0,4},{1,5},{4,0},{5,1},{8,12},{9,13},{12,8},{13,9},{2,6},{3,7},{6... | collective-permute-start | bytes 76808 | tf_op jit(solution)/shard_map/ppermute | solution.py:446
  17.9 0.7 %collective-permute-start.10 = (f32[50,128]{1,0:T(8,128)S(1)}, f32[50,128]{1,0:T(8,128)S(1)}, u32[]{:S(2)}, u32[]{:S(2)}) collective-permute-start(f32[50,128]{1,0:T(8,128)S(1)} %get-tuple-element.47), channel_id=1, source_target_pairs={{0,5},{1,4},{4,1},{5,0},{8,13},{9,12},{12,9},{13,8},{2,7},{3,6},{6... | collective-permute-start | bytes 76808 | tf_op jit(solution)/shard_map/ppermute | solution.py:446
  18.6 1.4 %collective-permute-done.3.other = f32[150,128]{1,0:T(8,128)S(1)} collective-permute-done((f32[150,128]{1,0:T(8,128)S(1)}, f32[150,128]{1,0:T(8,128)S(1)}, u32[]{:S(2)}, u32[]{:S(2)}) %collective-permute-start.3) | collective-permute-done | bytes 76832 | tf_op jit(solution)/shard_map/ppermute | solution.py:446
  20.0 0.6 %hand_out.1 = (f32[50,128]{1,0:T(8,128)S(1)}, f32[50,128]{1,0:T(8,128)S(1)}, f32[50,128]{1,0:T(8,128)S(1)}, f32[50,128]{1,0:T(8,128)S(1)}) custom-call(s32[16]{0:T(128)S(1)} %copy-done, f32[150,128]{1,0:T(8,128)S(1)} %get-tuple-element.32.own.after, f32[150,128]{1,0:T(8,128)S(1)} %collective-permute-done.3.other), custom_call_target="tpu_custom_call" | custom-call | tf_op jit(solution)/shard_map/hand_out/pallas_call | solution.py:730
  20.6 0.2 collective-permute-start.4
  20.8 0.0 collective-permute-start.5
  20.8 0.0 collective-permute-done.8.refs_1_
  20.8 1.8 %collective-permute-start.6 = (f32[50,128]{1,0:T(8,128)S(1)}, f32[50,128]{1,0:T(8,128)S(1)}, u32[]{:S(2)}, u32[]{:S(2)}) collective-permute-start(f32[50,128]{1,0:T(8,128)S(1)} %get-tuple-element.37), channel_id=1, source_target_pairs={{0,5},{1,4},{4,1},{5,0},{8,13},{9,12},{12,9},{13,8},{2,7},{3,6},{6... | collective-permute-start | bytes 76808 | tf_op jit(solution)/shard_map/ppermute | solution.py:446
  22.6 0.0 collective-permute-done.9.refs_2_
  22.6 0.0 collective-permute-done.10.refs_3_
  22.6 2.4 %spectrum.1 = f32[2,50,2,8,64]{4,3,2,1,0:T(8,128)} custom-call(s32[16]{0:T(128)S(1)} %copy-done, f32[50,128]{1,0:T(8,128)S(1)} %get-tuple-element.26.rates, f32[200,128]{1,0:T(8,128)S(1)} %get-tuple-element.43.rows, f32[50,128]{1,0:T(8,128)S(1)} %get-tuple-element.44.refs_0_, f32[50,128]{1,0:T(8,128)S(1)} %collective-permute-done.8.refs_1_, ...), custom_call_target="tpu_custom_call" | custom-call | tf_op jit(solution)/shard_map/spectrum/pallas_call | solution.py:784
  25.0 0.0 collective-permute-done.4.refs_1_
  25.0 0.0 collective-permute-done.5.refs_2_
  25.0 0.0 collective-permute-done.6.refs_3_
  25.0 2.2 %restore.1 = f32[50,4608]{1,0:T(8,128)} custom-call(s32[16]{0:T(128)S(1)} %copy-done, f32[50,128]{1,0:T(8,128)S(1)} %get-tuple-element.34.refs_0_, f32[50,128]{1,0:T(8,128)S(1)} %collective-permute-done.4.refs_1_, f32[50,128]{1,0:T(8,128)S(1)} %collective-permute-done.5.refs_2_, f32[50,128]{1,0:T(8,128)S(1)} %collective-permute-done.6.refs_3_, ...), custom_call_target="tpu_custom_call" | custom-call | tf_op jit(solution)/shard_map/restore/pallas_call | solution.py:389
Async XLA Ops:
  3.8 7.2 %collective-permute-start = (f32[100,128]{1,0:T(8,128)S(1)}, f32[100,128]{1,0:T(8,128)S(1)}, u32[]{:S(2)}, u32[]{:S(2)}) collective-permute-start(f32[100,128]{1,0:T(8,128)S(1)} %get-tuple-element.29), channel_id=1, source_target_pairs={{0,1},{1,0},{4,5},{5,4},{8,9},{9,8},{12,13},{13,12},{2,3},{3,2},{6... | collective-permute-start | bytes 153608 | tf_op jit(solution)/shard_map/ppermute | solution.py:446
  4.4 6.7 %collective-permute-start.1 = (f32[100,128]{1,0:T(8,128)S(1)}, f32[100,128]{1,0:T(8,128)S(1)}, u32[]{:S(2)}, u32[]{:S(2)}) collective-permute-start(f32[100,128]{1,0:T(8,128)S(1)} %get-tuple-element.30), channel_id=1, source_target_pairs={{0,4},{1,5},{4,0},{5,1},{8,12},{9,13},{12,8},{13,9},{2,6},{3,7},{6... | collective-permute-start | bytes 153608 | tf_op jit(solution)/shard_map/ppermute | solution.py:446
  7.0 2.8 %copy-start = (s32[16]{0:T(128)S(1)}, s32[16]{0:T(128)}, u32[]{:S(2)}) copy-start(s32[16]{0:T(128)} %lengths.13) | copy-start | bytes 196
  7.0 2.8 %copy-start.1 = (f32[16]{0:T(128)S(1)}, f32[16]{0:T(128)}, u32[]{:S(2)}) copy-start(f32[16]{0:T(128)} %latitude.1) | copy-start | bytes 196
  7.0 2.8 %copy-start.2 = (f32[16]{0:T(128)S(1)}, f32[16]{0:T(128)}, u32[]{:S(2)}) copy-start(f32[16]{0:T(128)} %weights.1) | copy-start | bytes 196
  7.0 4.1 %collective-permute-start.2 = (f32[100,128]{1,0:T(8,128)S(1)}, f32[100,128]{1,0:T(8,128)S(1)}, u32[]{:S(2)}, u32[]{:S(2)}) collective-permute-start(f32[100,128]{1,0:T(8,128)S(1)} %get-tuple-element.31), channel_id=1, source_target_pairs={{0,5},{1,4},{4,1},{5,0},{8,13},{9,12},{12,9},{13,8},{2,7},{3,6},{6... | collective-permute-start | bytes 153608 | tf_op jit(solution)/shard_map/ppermute | solution.py:446
  7.2 8.8 %collective-permute-start.7 = (f32[200,128]{1,0:T(8,128)S(1)}, f32[200,128]{1,0:T(8,128)S(1)}, u32[]{:S(2)}, u32[]{:S(2)}) collective-permute-start(f32[200,128]{1,0:T(8,128)S(1)} %get-tuple-element.42), channel_id=1, source_target_pairs={{0,8},{1,9},{4,12},{5,13},{8,0},{9,1},{12,4},{13,5},{2,10},{3,11},... | collective-permute-start | bytes 307208 | tf_op jit(solution)/shard_map/ppermute | solution.py:446
  12.3 7.7 %collective-permute-start.3 = (f32[150,128]{1,0:T(8,128)S(1)}, f32[150,128]{1,0:T(8,128)S(1)}, u32[]{:S(2)}, u32[]{:S(2)}) collective-permute-start(f32[150,128]{1,0:T(8,128)S(1)} %get-tuple-element.33), channel_id=1, source_target_pairs={{0,8},{1,9},{4,12},{5,13},{8,0},{9,1},{12,4},{13,5},{2,10},{3,11},... | collective-permute-start | bytes 230408 | tf_op jit(solution)/shard_map/ppermute | solution.py:446
  16.7 4.1 %collective-permute-start.8 = (f32[50,128]{1,0:T(8,128)S(1)}, f32[50,128]{1,0:T(8,128)S(1)}, u32[]{:S(2)}, u32[]{:S(2)}) collective-permute-start(f32[50,128]{1,0:T(8,128)S(1)} %get-tuple-element.45), channel_id=1, source_target_pairs={{0,1},{1,0},{4,5},{5,4},{8,9},{9,8},{12,13},{13,12},{2,3},{3,2},{6... | collective-permute-start | bytes 76808 | tf_op jit(solution)/shard_map/ppermute | solution.py:446
  17.0 5.6 %collective-permute-start.9 = (f32[50,128]{1,0:T(8,128)S(1)}, f32[50,128]{1,0:T(8,128)S(1)}, u32[]{:S(2)}, u32[]{:S(2)}) collective-permute-start(f32[50,128]{1,0:T(8,128)S(1)} %get-tuple-element.46), channel_id=1, source_target_pairs={{0,4},{1,5},{4,0},{5,1},{8,12},{9,13},{12,8},{13,9},{2,6},{3,7},{6... | collective-permute-start | bytes 76808 | tf_op jit(solution)/shard_map/ppermute | solution.py:446
  17.9 4.7 %collective-permute-start.10 = (f32[50,128]{1,0:T(8,128)S(1)}, f32[50,128]{1,0:T(8,128)S(1)}, u32[]{:S(2)}, u32[]{:S(2)}) collective-permute-start(f32[50,128]{1,0:T(8,128)S(1)} %get-tuple-element.47), channel_id=1, source_target_pairs={{0,5},{1,4},{4,1},{5,0},{8,13},{9,12},{12,9},{13,8},{2,7},{3,6},{6... | collective-permute-start | bytes 76808 | tf_op jit(solution)/shard_map/ppermute | solution.py:446
  20.6 4.4 %collective-permute-start.4 = (f32[50,128]{1,0:T(8,128)S(1)}, f32[50,128]{1,0:T(8,128)S(1)}, u32[]{:S(2)}, u32[]{:S(2)}) collective-permute-start(f32[50,128]{1,0:T(8,128)S(1)} %get-tuple-element.35), channel_id=1, source_target_pairs={{0,1},{1,0},{4,5},{5,4},{8,9},{9,8},{12,13},{13,12},{2,3},{3,2},{6... | collective-permute-start | bytes 76808 | tf_op jit(solution)/shard_map/ppermute | solution.py:446
  20.8 4.2 %collective-permute-start.5 = (f32[50,128]{1,0:T(8,128)S(1)}, f32[50,128]{1,0:T(8,128)S(1)}, u32[]{:S(2)}, u32[]{:S(2)}) collective-permute-start(f32[50,128]{1,0:T(8,128)S(1)} %get-tuple-element.36), channel_id=1, source_target_pairs={{0,4},{1,5},{4,0},{5,1},{8,12},{9,13},{12,8},{13,9},{2,6},{3,7},{6... | collective-permute-start | bytes 76808 | tf_op jit(solution)/shard_map/ppermute | solution.py:446
  20.8 4.2 %collective-permute-start.6 = (f32[50,128]{1,0:T(8,128)S(1)}, f32[50,128]{1,0:T(8,128)S(1)}, u32[]{:S(2)}, u32[]{:S(2)}) collective-permute-start(f32[50,128]{1,0:T(8,128)S(1)} %get-tuple-element.37), channel_id=1, source_target_pairs={{0,5},{1,4},{4,1},{5,0},{8,13},{9,12},{12,9},{13,8},{2,7},{3,6},{6... | collective-permute-start | bytes 76808 | tf_op jit(solution)/shard_map/ppermute | solution.py:446

commit v5 on v4

--- a/solution.py
+++ b/solution.py
@@ -15,6 +15,7 @@
 LANES = 128
 SHARES = 4
 GROUP = WAVES // SHARES
+ORDER = (0, 2, 3, 1)
 PAD = 64
 FULL = 60 * 1024 * 1024
 WINDOW = 3
@@ -142,7 +143,7 @@
 
 
 def near(me):
-    return [me ^ share for share in range(SHARES)]
+    return [me ^ share for share in ORDER]
 
 
 def row_arrays(first):
@@ -275,10 +276,9 @@
                 if slot != share:
                     moved = pltpu.roll(moved, ((slot - share) * GROUP) % LANES, 1)
                 value = jnp.where(chunk == slot, moved, value)
-            messages[share][pl.ds(which * channels, channels), :] = value
-        across[pl.ds(share * channels, channels), :] = interleaved(
-            messages[share][...], me < SHARES
-        )
+            message = messages[ORDER.index(share)]
+            message[pl.ds(which * channels, channels), :] = value
+        across[pl.ds(share * channels, channels), :] = interleaved(message[...], me < SHARES)
 
 
 def in_hbm(*values):
@@ -319,10 +319,13 @@
 
 
 def restore_kernel(lengths, *refs):
-    messages, (kept, basis, cosine, sine, out, held, coeff, ends, table, sems) = (
+    messages, (kept, basis, cosine, sine, spectra, out, spectra_out, held, coeff, ends, table) = (
         refs[:SHARES],
-        refs[SHARES:],
+        refs[SHARES:-2],
     )
+    sems, spectra_sem = refs[-2:]
+    spectra_copy = pltpu.make_async_copy(spectra, spectra_out, spectra_sem)
+    spectra_copy.start()
     channels, local = kept.shape
     blocks = local // BLOCK
     pieces = sems.shape[0]
@@ -335,7 +338,7 @@
     for slot in range(SHARES):
         value = jnp.zeros((channels, LANES), jnp.float32)
         for share in range(SHARES):
-            moved = messages[share][...]
+            moved = messages[ORDER.index(share)][...]
             if slot != share:
                 moved = pltpu.roll(moved, ((share - slot) * GROUP) % LANES, 1)
             value = jnp.where(chunk == share, moved, value)
@@ -381,27 +384,32 @@
             copies[-1].start()
     for copy in copies:
         copy.wait()
-
-
-def restore(lengths, messages, kept, tables):
+    spectra_copy.wait()
+
+
+def restore(lengths, messages, kept, tables, spectra):
     channels, local = kept.shape
     pieces = math.gcd(local // BLOCK, 6)
     return pl.pallas_call(
         restore_kernel,
-        out_shape=jax.ShapeDtypeStruct((channels, local), jnp.float32),
+        out_shape=[
+            jax.ShapeDtypeStruct((channels, local), jnp.float32),
+            jax.ShapeDtypeStruct(spectra.shape, jnp.float32),
+        ],
         in_specs=[pl.BlockSpec(memory_space=pltpu.SMEM)]
-        + [pl.BlockSpec(memory_space=pltpu.VMEM)] * (SHARES + 4),
-        out_specs=pl.BlockSpec(memory_space=pl.ANY),
+        + [pl.BlockSpec(memory_space=pltpu.VMEM)] * (SHARES + 5),
+        out_specs=[pl.BlockSpec(memory_space=pl.ANY)] * 2,
         scratch_shapes=[
             pltpu.VMEM((channels, local), jnp.float32),
             pltpu.VMEM((SHARES, PAD, LANES), jnp.float32),
             pltpu.VMEM((SHARES, channels, BLOCK), jnp.float32),
             pltpu.SMEM((16,), jnp.int32),
             pltpu.SemaphoreType.DMA((pieces,)),
+            pltpu.SemaphoreType.DMA,
         ],
         compiler_params=pltpu.CompilerParams(vmem_limit_bytes=32 * 1024 * 1024),
         name="restore",
-    )(lengths, *messages, kept, *tables)
+    )(lengths, *messages, kept, *tables, spectra)
 
 
 def fill_tables(table, me, per_device, basis, cosine, sine, blocks):
@@ -444,6 +452,10 @@
 def swapped(value, mask):
     count = lax.axis_size(AXES)
     return lax.ppermute(value, AXES, [(i, i ^ mask) for i in range(count)])
+
+
+def exchanged(values):
+    return [swapped(value, share) if share else value for value, share in zip(values, ORDER)]
 
 
 def legendre(latitude, waves):
@@ -479,7 +491,7 @@
     row_ids = jnp.arange(rows, dtype=jnp.int32)
     slots = jnp.arange(SHARES, dtype=jnp.int32)
     picks = []
-    for share in range(SHARES):
+    for share in ORDER:
         first = jnp.sum((stops <= (me ^ share) * local).astype(jnp.int32))
         held = first + ((slots - first) & 3)
         picks.append((held[:, None] == row_ids[None, :]).astype(jnp.float32))
@@ -688,7 +700,7 @@
     channels = messages[0].shape[0] // 2
     me = device_id()
     for share in range(SHARES):
-        chunks[share][...] = across[pl.ds(share * channels, channels), :]
+        chunks[ORDER.index(share)][...] = across[pl.ds(share * channels, channels), :]
     arrays = by_row(
         [interleaved(message, me >= SHARES) for message in messages],
         first_rows(lengths, near(me), local),
@@ -783,7 +795,7 @@
     channels = rates.shape[0]
     return pl.pallas_call(
         functools.partial(spectrum_kernel, local),
-        out_shape=floats(2, channels, 2, 8, WAVES),
+        out_shape=pltpu.VMEM((2, channels, 2, 8, WAVES), jnp.float32),
         in_specs=[SMEM] + [VMEM] * (SHARES + 4),
         out_specs=VMEM,
         compiler_params=pltpu.CompilerParams(vmem_limit_bytes=SMALL),
@@ -800,7 +812,7 @@
     other_part = swapped(sent_part, SHARES)
     tables = tables_of(lengths, part, local, per_device)
     rows, *chunks = pack(lengths, tables[1], received, across, local)
-    chunks = [chunks[0]] + [swapped(chunks[i], i) for i in range(1, SHARES)]
+    chunks = exchanged(chunks)
     replies = hand_out(lengths, part, other_part, local)
     return replies, tables, (lengths, rates, rows, chunks, poly, gram, local)
 
@@ -810,7 +822,7 @@
     count = lax.axis_size(AXES)
     per_device = WAVES // count
     *messages, across, rates, kept = analyse(lengths, strength, cot_second, cot_first, per_device)
-    received = [messages[0]] + [swapped(messages[i], i) for i in range(1, SHARES)]
+    received = exchanged(messages)
     arguments = (lengths, latitude, weights, local, per_device)
     small = count == 2 * SHARES and lengths.shape[0] == GROUP
     if small:
@@ -818,10 +830,10 @@
     else:
         replies, grad_target = middle_general(received, strength, *arguments)
         tables = tables_of(lengths, replies[0], local, per_device)
-    answers = [replies[0]] + [swapped(replies[i], i) for i in range(1, SHARES)]
-    grad_state = restore(lengths, answers, kept, tables)
+    answers = exchanged(replies)
     if small:
         grad_target = spectrum(*pieces)
+    grad_state, grad_target = restore(lengths, answers, kept, tables, grad_target)
     return (grad_state, grad_target)
 
 

time: 27.4 us -> 26.5 us (0.967)
  Pallas kernels: 12.9 us -> 12 us
  waiting for transfers between devices: 1.4 us -> 0.87 us
  starting transfers between devices: 12.2 us -> 12.7 us
    pallas_call x2, Pallas kernels: 4.65 us -> 3.75 us  [the longest x1 2.23 us: restore(): pl.pallas_call(restore_kernel, out_shape=[jax.ShapeDtypeStruct((channels,...]
    ppermute x11, starting transfers between devices: 12.2 us -> 12.7 us  [swapped(): return lax.ppermute(value, AXES, [(i, i ^ mask) for i in range(count)])]
    ppermute x11, waiting for transfers between devices: 1.4 us -> 0.87 us  [swapped(): return lax.ppermute(value, AXES, [(i, i ^ mask) for i in range(count)])]
  transfers between devices with their start and end apart: 11 -> 11, of which waited for: 1 -> 2; matrix products, arithmetic and copies ran while one was open for 0% -> 0% of each run, Pallas kernels for 27% -> 25%
where the time goes in v5:
time: 26.5 us; the launch traced here: 26.4 us
  starting transfers between devices  12.7 us (48%)
  Pallas kernels  12 us (45%)
  waiting for transfers between devices  0.87 us (3%)
  between operations  0.73 us (3%)
    ppermute x11, starting transfers between devices, swapped(): return lax.ppermute(value, AXES, [(i, i ^ mask) for i in range(count)])  12.7 us
    pallas_call x1, Pallas kernels, analyse(): pl.pallas_call(functools.partial(analyse_kernel, per_device), out_shape=[...  3.21 us
    pallas_call x1, Pallas kernels, restore(): pl.pallas_call(restore_kernel, out_shape=[jax.ShapeDtypeStruct((channels,...  2.23 us
    pallas_call x1, Pallas kernels, spectrum(): pl.pallas_call(functools.partial(spectrum_kernel, local), out_shape=pltpu...  1.52 us
    pallas_call x1, Pallas kernels, tables_of(): pl.pallas_call(functools.partial(tables_kernel, per_device, local), out_s...  1.3 us
    pallas_call x1, Pallas kernels, prepare(): pl.pallas_call(functools.partial(prepare_kernel, count, local), out_shape...  1.23 us
    pallas_call x1, Pallas kernels, couple(): pl.pallas_call(functools.partial(couple_kernel, local), out_shape=[floats...  1.18 us
    ppermute x11, waiting for transfers between devices, swapped(): return lax.ppermute(value, AXES, [(i, i ^ mask) for i in range(count)])  0.87 us
  transfers between devices with their start and end apart: 11, of which 2 were waited for; matrix products, arithmetic and copies ran while one was open for 0% of the time, Pallas kernels for 25%

profile of v5, /device:TPU:0, one launch (start us, length us, event | category | flops | bytes accessed | tf_op | source)
XLA Modules:
  0.0 26.4 jit_solution(11304833837268849664)
XLA Ops:
  0.6 3.2 %analyse.1 = (f32[100,128]{1,0:T(8,128)S(1)}, f32[100,128]{1,0:T(8,128)S(1)}, f32[100,128]{1,0:T(8,128)S(1)}, f32[100,128]{1,0:T(8,128)S(1)}, f32[200,128]{1,0:T...) custom-call(s32[16]{0:T(128)} %lengths.13, f32[2,50]{1,0:T(2,128)} %strength_held.1, f32[50,4608]{1,0:T(8,128)} %second.1, ...), custom_call_target="tpu_custom_call" | custom-call | tf_op jit(solution)/shard_map/analyse/pallas_call | solution.py:292
  3.8 3.1 %collective-permute-start = (f32[100,128]{1,0:T(8,128)S(1)}, f32[100,128]{1,0:T(8,128)S(1)}, u32[]{:S(2)}, u32[]{:S(2)}) collective-permute-start(f32[100,128]{1,0:T(8,128)S(1)} %get-tuple-element.29), channel_id=1, source_target_pairs={{0,4},{1,5},{4,0},{5,1},{8,12},{9,13},{12,8},{13,9},{2,6},{3,7},{6... | collective-permute-start | bytes 153608 | tf_op jit(solution)/shard_map/ppermute | solution.py:454
  6.9 0.0 collective-permute-start.1
  6.9 0.0 copy-start
  6.9 0.0 copy-start.1
  6.9 0.0 copy-start.2
  6.9 0.2 collective-permute-start.2
  7.1 3.0 %collective-permute-start.7 = (f32[200,128]{1,0:T(8,128)S(1)}, f32[200,128]{1,0:T(8,128)S(1)}, u32[]{:S(2)}, u32[]{:S(2)}) collective-permute-start(f32[200,128]{1,0:T(8,128)S(1)} %get-tuple-element.42), channel_id=1, source_target_pairs={{0,8},{1,9},{4,12},{5,13},{8,0},{9,1},{12,4},{13,5},{2,10},{3,11},... | collective-permute-start | bytes 307208 | tf_op jit(solution)/shard_map/ppermute | solution.py:454
  10.1 0.0 copy-done
  10.1 0.0 copy-done.1
  10.1 0.0 copy-done.2
  10.1 1.2 %prepare.1 = (f32[2,4,16,128]{3,2,1,0:T(8,128)S(1)}, bf16[384,128]{1,0:T(8,128)(2,1)S(1)}, bf16[384,128]{1,0:T(8,128)(2,1)S(1)}) custom-call(s32[16]{0:T(128)S(1)} %copy-done, f32[16]{0:T(128)S(1)} %copy-done.1, f32[16]{0:T(128)S(1)} %copy-done.2), custom_call_target="tpu_custom_call" | custom-call | tf_op jit(solution)/shard_map/prepare/pallas_call | solution.py:639
  11.3 0.0 collective-permute-done.refs_1_
  11.3 0.0 collective-permute-done.1.refs_2_
  11.4 0.0 collective-permute-done.2.refs_3_
  11.4 1.2 %couple.1 = (f32[150,128]{1,0:T(8,128)S(1)}, f32[150,128]{1,0:T(8,128)S(1)}) custom-call(s32[16]{0:T(128)S(1)} %copy-done, f32[50,128]{1,0:T(8,128)S(1)} %get-tuple-element.26.rates, f32[2,4,16,128]{3,2,1,0:T(8,128)S(1)} %get-tuple-element.27.coupling, f32[100,128]{1,0:T(8,128)S(1)} %get-tuple-element.28.refs_0_, ...), custom_call_target="tpu_custom_call" | custom-call | tf_op jit(solution)/shard_map/couple/pallas_call | solution.py:688
  12.6 2.1 %collective-permute-start.3 = (f32[150,128]{1,0:T(8,128)S(1)}, f32[150,128]{1,0:T(8,128)S(1)}, u32[]{:S(2)}, u32[]{:S(2)}) collective-permute-start(f32[150,128]{1,0:T(8,128)S(1)} %get-tuple-element.33), channel_id=1, source_target_pairs={{0,8},{1,9},{4,12},{5,13},{8,0},{9,1},{12,4},{13,5},{2,10},{3,11},... | collective-permute-start | bytes 230408 | tf_op jit(solution)/shard_map/ppermute | solution.py:454
  14.7 1.3 %tables.1 = (bf16[4,256,256]{2,1,0:T(8,128)(2,1)S(1)}, f32[4,24,128]{2,1,0:T(8,128)S(1)}, f32[4,24,128]{2,1,0:T(8,128)S(1)}) custom-call(s32[16]{0:T(128)S(1)} %copy-done, f32[150,128]{1,0:T(8,128)S(1)} %get-tuple-element.32.own.after), custom_call_target="tpu_custom_call" | custom-call | tf_op jit(solution)/shard_map/tables/pallas_call | solution.py:441
  16.0 0.0 collective-permute-done.7.refs_4_
  16.0 0.7 %pack.1 = (f32[200,128]{1,0:T(8,128)S(1)}, f32[50,128]{1,0:T(8,128)S(1)}, f32[50,128]{1,0:T(8,128)S(1)}, f32[50,128]{1,0:T(8,128)S(1)}, f32[50,128]{1,0:T(8,128)S(1)}) custom-call(s32[16]{0:T(128)S(1)} %copy-done, f32[4,24,128]{2,1,0:T(8,128)S(1)} %get-tuple-element.40.after.refs_6_, f32[100,128]{1,0:T(8,128)S(1)} %get-tuple-element.28.refs_0_, ...), custom_call_target="tpu_custom_call" | custom-call | tf_op jit(solution)/shard_map/pack/pallas_call | solution.py:714
  16.7 0.8 %collective-permute-start.8 = (f32[50,128]{1,0:T(8,128)S(1)}, f32[50,128]{1,0:T(8,128)S(1)}, u32[]{:S(2)}, u32[]{:S(2)}) collective-permute-start(f32[50,128]{1,0:T(8,128)S(1)} %get-tuple-element.45), channel_id=1, source_target_pairs={{0,4},{1,5},{4,0},{5,1},{8,12},{9,13},{12,8},{13,9},{2,6},{3,7},{6... | collective-permute-start | bytes 76808 | tf_op jit(solution)/shard_map/ppermute | solution.py:454
  17.5 0.2 collective-permute-start.9
  17.7 1.2 %collective-permute-start.10 = (f32[50,128]{1,0:T(8,128)S(1)}, f32[50,128]{1,0:T(8,128)S(1)}, u32[]{:S(2)}, u32[]{:S(2)}) collective-permute-start(f32[50,128]{1,0:T(8,128)S(1)} %get-tuple-element.47), channel_id=1, source_target_pairs={{0,1},{1,0},{4,5},{5,4},{8,9},{9,8},{12,13},{13,12},{2,3},{3,2},{6... | collective-permute-start | bytes 76808 | tf_op jit(solution)/shard_map/ppermute | solution.py:454
  18.9 0.7 %collective-permute-done.3.other = f32[150,128]{1,0:T(8,128)S(1)} collective-permute-done((f32[150,128]{1,0:T(8,128)S(1)}, f32[150,128]{1,0:T(8,128)S(1)}, u32[]{:S(2)}, u32[]{:S(2)}) %collective-permute-start.3) | collective-permute-done | bytes 76832 | tf_op jit(solution)/shard_map/ppermute | solution.py:454
  19.5 0.6 %hand_out.1 = (f32[50,128]{1,0:T(8,128)S(1)}, f32[50,128]{1,0:T(8,128)S(1)}, f32[50,128]{1,0:T(8,128)S(1)}, f32[50,128]{1,0:T(8,128)S(1)}) custom-call(s32[16]{0:T(128)S(1)} %copy-done, f32[150,128]{1,0:T(8,128)S(1)} %get-tuple-element.32.own.after, f32[150,128]{1,0:T(8,128)S(1)} %collective-permute-done.3.other), custom_call_target="tpu_custom_call" | custom-call | tf_op jit(solution)/shard_map/hand_out/pallas_call | solution.py:742
  20.2 0.1 collective-permute-start.4
  20.3 0.6 %collective-permute-start.5 = (f32[50,128]{1,0:T(8,128)S(1)}, f32[50,128]{1,0:T(8,128)S(1)}, u32[]{:S(2)}, u32[]{:S(2)}) collective-permute-start(f32[50,128]{1,0:T(8,128)S(1)} %get-tuple-element.36), channel_id=1, source_target_pairs={{0,5},{1,4},{4,1},{5,0},{8,13},{9,12},{12,9},{13,8},{2,7},{3,6},{6... | collective-permute-start | bytes 76808 | tf_op jit(solution)/shard_map/ppermute | solution.py:454
  21.0 0.0 collective-permute-done.8.refs_1_
  21.0 1.4 %collective-permute-start.6 = (f32[50,128]{1,0:T(8,128)S(1)}, f32[50,128]{1,0:T(8,128)S(1)}, u32[]{:S(2)}, u32[]{:S(2)}) collective-permute-start(f32[50,128]{1,0:T(8,128)S(1)} %get-tuple-element.37), channel_id=1, source_target_pairs={{0,1},{1,0},{4,5},{5,4},{8,9},{9,8},{12,13},{13,12},{2,3},{3,2},{6... | collective-permute-start | bytes 76808 | tf_op jit(solution)/shard_map/ppermute | solution.py:454
  22.4 0.0 collective-permute-done.9.refs_2_
  22.4 0.0 collective-permute-done.10.refs_3_
  22.4 1.5 %spectrum.1.refs_8_ = f32[2,50,2,8,64]{4,3,2,1,0:T(8,128)S(1)} custom-call(s32[16]{0:T(128)S(1)} %copy-done, f32[50,128]{1,0:T(8,128)S(1)} %get-tuple-element.26.rates, f32[200,128]{1,0:T(8,128)S(1)} %get-tuple-element.43.rows, f32[50,128]{1,0:T(8,128)S(1)} %get-tuple-element.44.refs_0_, f32[50,128]{1,0:T(8,128)S(1)} %collective-permute-done.8.refs_1_, ...), custom_call_target="tpu_custom_call" | custom-call | tf_op jit(solution)/shard_map/spectrum/pallas_call | solution.py:796
  23.9 0.2 collective-permute-done.4.refs_1_
  24.1 0.0 collective-permute-done.5.refs_2_
  24.1 0.0 collective-permute-done.6.refs_3_
  24.1 2.2 %restore.1 = (f32[50,4608]{1,0:T(8,128)}, f32[2,50,2,8,64]{4,3,2,1,0:T(8,128)}) custom-call(s32[16]{0:T(128)S(1)} %copy-done, f32[50,128]{1,0:T(8,128)S(1)} %get-tuple-element.34.refs_0_, f32[50,128]{1,0:T(8,128)S(1)} %collective-permute-done.4.refs_1_, f32[50,128]{1,0:T(8,128)S(1)} %collective-permute-done.5.refs_2_, ...), custom_call_target="tpu_custom_call" | custom-call | tf_op jit(solution)/shard_map/restore/pallas_call | solution.py:393
Async XLA Ops:
  3.8 7.5 %collective-permute-start = (f32[100,128]{1,0:T(8,128)S(1)}, f32[100,128]{1,0:T(8,128)S(1)}, u32[]{:S(2)}, u32[]{:S(2)}) collective-permute-start(f32[100,128]{1,0:T(8,128)S(1)} %get-tuple-element.29), channel_id=1, source_target_pairs={{0,4},{1,5},{4,0},{5,1},{8,12},{9,13},{12,8},{13,9},{2,6},{3,7},{6... | collective-permute-start | bytes 153608 | tf_op jit(solution)/shard_map/ppermute | solution.py:454
  6.9 4.4 %collective-permute-start.1 = (f32[100,128]{1,0:T(8,128)S(1)}, f32[100,128]{1,0:T(8,128)S(1)}, u32[]{:S(2)}, u32[]{:S(2)}) collective-permute-start(f32[100,128]{1,0:T(8,128)S(1)} %get-tuple-element.30), channel_id=1, source_target_pairs={{0,5},{1,4},{4,1},{5,0},{8,13},{9,12},{12,9},{13,8},{2,7},{3,6},{6... | collective-permute-start | bytes 153608 | tf_op jit(solution)/shard_map/ppermute | solution.py:454
  6.9 3.2 %copy-start = (s32[16]{0:T(128)S(1)}, s32[16]{0:T(128)}, u32[]{:S(2)}) copy-start(s32[16]{0:T(128)} %lengths.13) | copy-start | bytes 196
  6.9 3.2 %copy-start.1 = (f32[16]{0:T(128)S(1)}, f32[16]{0:T(128)}, u32[]{:S(2)}) copy-start(f32[16]{0:T(128)} %latitude.1) | copy-start | bytes 196
  6.9 3.2 %copy-start.2 = (f32[16]{0:T(128)S(1)}, f32[16]{0:T(128)}, u32[]{:S(2)}) copy-start(f32[16]{0:T(128)} %weights.1) | copy-start | bytes 196
  6.9 4.4 %collective-permute-start.2 = (f32[100,128]{1,0:T(8,128)S(1)}, f32[100,128]{1,0:T(8,128)S(1)}, u32[]{:S(2)}, u32[]{:S(2)}) collective-permute-start(f32[100,128]{1,0:T(8,128)S(1)} %get-tuple-element.31), channel_id=1, source_target_pairs={{0,1},{1,0},{4,5},{5,4},{8,9},{9,8},{12,13},{13,12},{2,3},{3,2},{6... | collective-permute-start | bytes 153608 | tf_op jit(solution)/shard_map/ppermute | solution.py:454
  7.1 8.8 %collective-permute-start.7 = (f32[200,128]{1,0:T(8,128)S(1)}, f32[200,128]{1,0:T(8,128)S(1)}, u32[]{:S(2)}, u32[]{:S(2)}) collective-permute-start(f32[200,128]{1,0:T(8,128)S(1)} %get-tuple-element.42), channel_id=1, source_target_pairs={{0,8},{1,9},{4,12},{5,13},{8,0},{9,1},{12,4},{13,5},{2,10},{3,11},... | collective-permute-start | bytes 307208 | tf_op jit(solution)/shard_map/ppermute | solution.py:454
  12.6 7.0 %collective-permute-start.3 = (f32[150,128]{1,0:T(8,128)S(1)}, f32[150,128]{1,0:T(8,128)S(1)}, u32[]{:S(2)}, u32[]{:S(2)}) collective-permute-start(f32[150,128]{1,0:T(8,128)S(1)} %get-tuple-element.33), channel_id=1, source_target_pairs={{0,8},{1,9},{4,12},{5,13},{8,0},{9,1},{12,4},{13,5},{2,10},{3,11},... | collective-permute-start | bytes 230408 | tf_op jit(solution)/shard_map/ppermute | solution.py:454
  16.7 4.3 %collective-permute-start.8 = (f32[50,128]{1,0:T(8,128)S(1)}, f32[50,128]{1,0:T(8,128)S(1)}, u32[]{:S(2)}, u32[]{:S(2)}) collective-permute-start(f32[50,128]{1,0:T(8,128)S(1)} %get-tuple-element.45), channel_id=1, source_target_pairs={{0,4},{1,5},{4,0},{5,1},{8,12},{9,13},{12,8},{13,9},{2,6},{3,7},{6... | collective-permute-start | bytes 76808 | tf_op jit(solution)/shard_map/ppermute | solution.py:454
  17.5 4.9 %collective-permute-start.9 = (f32[50,128]{1,0:T(8,128)S(1)}, f32[50,128]{1,0:T(8,128)S(1)}, u32[]{:S(2)}, u32[]{:S(2)}) collective-permute-start(f32[50,128]{1,0:T(8,128)S(1)} %get-tuple-element.46), channel_id=1, source_target_pairs={{0,5},{1,4},{4,1},{5,0},{8,13},{9,12},{12,9},{13,8},{2,7},{3,6},{6... | collective-permute-start | bytes 76808 | tf_op jit(solution)/shard_map/ppermute | solution.py:454
  17.7 4.7 %collective-permute-start.10 = (f32[50,128]{1,0:T(8,128)S(1)}, f32[50,128]{1,0:T(8,128)S(1)}, u32[]{:S(2)}, u32[]{:S(2)}) collective-permute-start(f32[50,128]{1,0:T(8,128)S(1)} %get-tuple-element.47), channel_id=1, source_target_pairs={{0,1},{1,0},{4,5},{5,4},{8,9},{9,8},{12,13},{13,12},{2,3},{3,2},{6... | collective-permute-start | bytes 76808 | tf_op jit(solution)/shard_map/ppermute | solution.py:454
  20.2 3.9 %collective-permute-start.4 = (f32[50,128]{1,0:T(8,128)S(1)}, f32[50,128]{1,0:T(8,128)S(1)}, u32[]{:S(2)}, u32[]{:S(2)}) collective-permute-start(f32[50,128]{1,0:T(8,128)S(1)} %get-tuple-element.35), channel_id=1, source_target_pairs={{0,4},{1,5},{4,0},{5,1},{8,12},{9,13},{12,8},{13,9},{2,6},{3,7},{6... | collective-permute-start | bytes 76808 | tf_op jit(solution)/shard_map/ppermute | solution.py:454
  20.3 3.8 %collective-permute-start.5 = (f32[50,128]{1,0:T(8,128)S(1)}, f32[50,128]{1,0:T(8,128)S(1)}, u32[]{:S(2)}, u32[]{:S(2)}) collective-permute-start(f32[50,128]{1,0:T(8,128)S(1)} %get-tuple-element.36), channel_id=1, source_target_pairs={{0,5},{1,4},{4,1},{5,0},{8,13},{9,12},{12,9},{13,8},{2,7},{3,6},{6... | collective-permute-start | bytes 76808 | tf_op jit(solution)/shard_map/ppermute | solution.py:454
  21.0 3.2 %collective-permute-start.6 = (f32[50,128]{1,0:T(8,128)S(1)}, f32[50,128]{1,0:T(8,128)S(1)}, u32[]{:S(2)}, u32[]{:S(2)}) collective-permute-start(f32[50,128]{1,0:T(8,128)S(1)} %get-tuple-element.37), channel_id=1, source_target_pairs={{0,1},{1,0},{4,5},{5,4},{8,9},{9,8},{12,13},{13,12},{2,3},{3,2},{6... | collective-permute-start | bytes 76808 | tf_op jit(solution)/shard_map/ppermute | solution.py:454

commit v6 on v5

--- a/solution.py
+++ b/solution.py
@@ -152,8 +152,7 @@
     return (first + ((group - first) & 3)) >> 2
 
 
-def by_row(messages, firsts):
-    held = [row_arrays(first) for first in firsts]
+def by_row(messages, held):
     arrays = []
     for index in range(SHARES):
         value = jnp.zeros(messages[0].shape, jnp.float32)
@@ -190,7 +189,7 @@
 
 
 def analyse_kernel(per_device, lengths_held, strength_held, second, first, *refs):
-    messages, (across, rates, kept, fields, lengths, strength, basis, cosine, sine, lhs, total, table) = (
+    messages, (rates, kept, fields, lengths, strength, basis, cosine, sine, lhs, total, table) = (
         refs[:SHARES],
         refs[SHARES:-3],
     )
@@ -268,17 +267,23 @@
         value_first = total[slot, PAD : PAD + channels, :]
         part_second = rate_second * value_second
         pairs.append((rate_first * (value_first + value_second) + part_second, part_second))
+    moved = []
+    for which in range(2):
+        by_shift = {}
+        for shift in range(1 - SHARES, SHARES):
+            value = jnp.zeros((channels, LANES), jnp.float32)
+            for share in range(SHARES):
+                if 0 <= share + shift < SHARES:
+                    value = jnp.where(chunk == share, pairs[share + shift][which], value)
+            by_shift[shift] = pltpu.roll(value, (shift * GROUP) % LANES, 1) if shift else value
+        moved.append(by_shift)
     for share in range(SHARES):
         for which in range(2):
-            value = jnp.zeros((channels, LANES), jnp.float32)
-            for slot in range(SHARES):
-                moved = pairs[slot][which]
-                if slot != share:
-                    moved = pltpu.roll(moved, ((slot - share) * GROUP) % LANES, 1)
-                value = jnp.where(chunk == slot, moved, value)
+            value = moved[which][-share]
+            for slot in range(1, SHARES):
+                value = jnp.where(chunk == slot, moved[which][slot - share], value)
             message = messages[ORDER.index(share)]
             message[pl.ds(which * channels, channels), :] = value
-        across[pl.ds(share * channels, channels), :] = interleaved(message[...], me < SHARES)
 
 
 def in_hbm(*values):
@@ -293,12 +298,11 @@
         functools.partial(analyse_kernel, per_device),
         out_shape=[pltpu.VMEM((2 * channels, LANES), jnp.float32)] * SHARES
         + [
-            pltpu.VMEM((SHARES * channels, LANES), jnp.float32),
             pltpu.VMEM((channels, LANES), jnp.float32),
             pltpu.VMEM((channels, local), jnp.float32),
         ],
         in_specs=[pl.BlockSpec(memory_space=pltpu.HBM)] * 4,
-        out_specs=[pl.BlockSpec(memory_space=pltpu.VMEM)] * (SHARES + 3),
+        out_specs=[pl.BlockSpec(memory_space=pltpu.VMEM)] * (SHARES + 2),
         scratch_shapes=[
             pltpu.VMEM((2, channels, local), jnp.float32),
             pltpu.SMEM(lengths.shape, jnp.int32),
@@ -318,20 +322,15 @@
     )(*in_hbm(lengths, strength, second, first))
 
 
-def restore_kernel(lengths, *refs):
-    messages, (kept, basis, cosine, sine, spectra, out, spectra_out, held, coeff, ends, table) = (
-        refs[:SHARES],
-        refs[SHARES:-2],
-    )
+def restore_kernel(*refs):
+    messages, refs = refs[:SHARES], refs[SHARES:]
+    kept, bases, cosine, sine, choose, mix, spectra, out, spectra_out, held, coeff = refs[:-2]
     sems, spectra_sem = refs[-2:]
     spectra_copy = pltpu.make_async_copy(spectra, spectra_out, spectra_sem)
     spectra_copy.start()
     channels, local = kept.shape
     blocks = local // BLOCK
-    pieces = sems.shape[0]
-    width = local // pieces
-    me = device_id()
-    row_table(lengths, table, me, local, lengths.shape[0])
+    width = local // sems.shape[0]
     lane = lax.broadcasted_iota(jnp.int32, (1, LANES), 1)
     chunk = (lane >> 4) & 3
     coeff[...] = jnp.zeros_like(coeff)
@@ -343,38 +342,29 @@
                 moved = pltpu.roll(moved, ((share - slot) * GROUP) % LANES, 1)
             value = jnp.where(chunk == share, moved, value)
         coeff[slot, :channels, :] = value
-    within = lax.broadcasted_iota(jnp.int32, (1, BLOCK), 1)
-
-    def block_value(block, slot):
-        value = coeff[slot]
+
+    def part_value(part):
+        value = coeff[0] * choose[pl.ds(SHARES * part, 1), :]
+        for slot in range(1, SHARES):
+            value = value + coeff[slot] * choose[pl.ds(SHARES * part + slot, 1), :]
         turned = (
-            value * cosine[slot, pl.ds(block, 1), :]
-            + pltpu.roll(value, PAD, 1) * sine[slot, pl.ds(block, 1), :]
+            value * cosine[pl.ds(part, 1), :]
+            + pltpu.roll(value, PAD, 1) * sine[pl.ds(part, 1), :]
         )
         high = turned.astype(jnp.bfloat16)
         low = (turned - high.astype(jnp.float32)).astype(jnp.bfloat16)
         left = jnp.concatenate([high, low], axis=0)
         left = jnp.concatenate([left, left], axis=1)
-        product = jnp.dot(left, basis[slot], preferred_element_type=jnp.float32)
+        product = jnp.dot(left, bases[part], preferred_element_type=jnp.float32)
         return product[:channels] + product[PAD : PAD + channels]
 
-    begin_slot = table[3 * SHARES]
-    splits = []
-    for later in range(1, SHARES):
-        block, low_end = split_block(table[2 * SHARES + later], blocks)
-        splits.append(jnp.where(low_end < BLOCK, block, blocks))
-        ends[later] = block_value(block, (begin_slot + later) & 3)
+    ends = [part_value(blocks + index) for index in range(SHARES - 1)]
     copies = []
     for block in range(blocks):
         place = block * BLOCK
-        slot = begin_slot
-        split = jnp.int32(0)
-        for later in range(1, SHARES):
-            slot = slot + jnp.where(table[2 * SHARES + later] <= place, 1, 0)
-            split = jnp.where(splits[later - 1] == block, later, split)
-        slot = slot & 3
-        end = table[slot] + table[SHARES + slot] - place
-        value = jnp.where(within < end, block_value(block, slot), ends[split])
+        value = part_value(block)
+        for index in range(SHARES - 1):
+            value = value + ends[index] * mix[pl.ds((SHARES - 1) * block + index, 1), :]
         held[:, pl.ds(place, BLOCK)] = kept[:, pl.ds(place, BLOCK)] - value
         if (place + BLOCK) % width == 0:
             at = pl.ds(place + BLOCK - width, width)
@@ -387,7 +377,7 @@
     spectra_copy.wait()
 
 
-def restore(lengths, messages, kept, tables, spectra):
+def restore(messages, kept, tables, spectra):
     channels, local = kept.shape
     pieces = math.gcd(local // BLOCK, 6)
     return pl.pallas_call(
@@ -396,20 +386,17 @@
             jax.ShapeDtypeStruct((channels, local), jnp.float32),
             jax.ShapeDtypeStruct(spectra.shape, jnp.float32),
         ],
-        in_specs=[pl.BlockSpec(memory_space=pltpu.SMEM)]
-        + [pl.BlockSpec(memory_space=pltpu.VMEM)] * (SHARES + 5),
+        in_specs=[pl.BlockSpec(memory_space=pltpu.VMEM)] * (SHARES + 7),
         out_specs=[pl.BlockSpec(memory_space=pl.ANY)] * 2,
         scratch_shapes=[
             pltpu.VMEM((channels, local), jnp.float32),
             pltpu.VMEM((SHARES, PAD, LANES), jnp.float32),
-            pltpu.VMEM((SHARES, channels, BLOCK), jnp.float32),
-            pltpu.SMEM((16,), jnp.int32),
             pltpu.SemaphoreType.DMA((pieces,)),
             pltpu.SemaphoreType.DMA,
         ],
         compiler_params=pltpu.CompilerParams(vmem_limit_bytes=32 * 1024 * 1024),
         name="restore",
-    )(lengths, *messages, kept, *tables, spectra)
+    )(*messages, kept, *tables, spectra)
 
 
 def fill_tables(table, me, per_device, basis, cosine, sine, blocks):
@@ -422,31 +409,71 @@
         basis[slot, LANES:, :] = low
 
 
-def tables_kernel(per_device, local, lengths, after, basis, cosine, sine, table):
+def tables_kernel(
+    per_device, local, lengths_held, after, bases, cosine, sine, choose, mix, *scratch
+):
+    basis, cosines, sines, table, lengths, sem = scratch
+    blocks = local // BLOCK
     me = device_id()
+    copy = pltpu.make_async_copy(lengths_held, lengths, sem)
+    copy.start()
+    copy.wait()
     row_table(lengths, table, me, local, lengths.shape[0])
-    fill_tables(table, me, per_device, basis, cosine, sine, local // BLOCK)
-
-
-def table_shapes(local):
-    phase_rows = -(-(local // BLOCK) // 8) * 8
-    return [
-        jax.ShapeDtypeStruct((SHARES, 2 * LANES, BLOCK), jnp.bfloat16),
-        jax.ShapeDtypeStruct((SHARES, phase_rows, LANES), jnp.float32),
-        jax.ShapeDtypeStruct((SHARES, phase_rows, LANES), jnp.float32),
+    fill_tables(table, me, per_device, basis, cosines, sines, blocks)
+    within = lax.broadcasted_iota(jnp.int32, (1, BLOCK), 1)
+    begin_slot = table[3 * SHARES]
+
+    def place_part(part, block, slot, low_end, high_end):
+        keep = jnp.where((within >= low_end) & (within < high_end), 1.0, 0.0)
+        bases[part] = basis[slot] * keep.astype(jnp.bfloat16)
+        cosine[pl.ds(part, 1), :] = cosines[slot, pl.ds(block, 1), :]
+        sine[pl.ds(part, 1), :] = sines[slot, pl.ds(block, 1), :]
+        for other in range(SHARES):
+            mark = jnp.where(slot == other, 1.0, 0.0)
+            choose[pl.ds(SHARES * part + other, 1), :] = jnp.full((1, LANES), mark)
+
+    for block in range(blocks):
+        place = block * BLOCK
+        slot = begin_slot
+        for later in range(1, SHARES):
+            slot = slot + jnp.where(table[2 * SHARES + later] <= place, 1, 0)
+        slot = slot & 3
+        place_part(block, block, slot, 0, table[slot] + table[SHARES + slot] - place)
+    for later in range(1, SHARES):
+        block, low_end = split_block(table[2 * SHARES + later], blocks)
+        place_part(blocks + later - 1, block, (begin_slot + later) & 3, low_end, BLOCK)
+        for other in range(blocks):
+            mark = jnp.where(block == other, 1.0, 0.0)
+            mix[pl.ds((SHARES - 1) * other + later - 1, 1), :] = jnp.full((1, BLOCK), mark)
+
+
+def tables_of(lengths, after, local, per_device):
+    blocks = local // BLOCK
+    parts = blocks + SHARES - 1
+    phase_rows = -(-blocks // 8) * 8
+    shapes = [
+        jax.ShapeDtypeStruct((parts, 2 * LANES, BLOCK), jnp.bfloat16),
+        jax.ShapeDtypeStruct((parts, LANES), jnp.float32),
+        jax.ShapeDtypeStruct((parts, LANES), jnp.float32),
+        jax.ShapeDtypeStruct((SHARES * parts, LANES), jnp.float32),
+        jax.ShapeDtypeStruct(((SHARES - 1) * blocks, BLOCK), jnp.float32),
     ]
-
-
-def tables_of(lengths, after, local, per_device):
     return pl.pallas_call(
         functools.partial(tables_kernel, per_device, local),
-        out_shape=table_shapes(local),
-        in_specs=[pl.BlockSpec(memory_space=pltpu.SMEM), pl.BlockSpec(memory_space=pl.ANY)],
-        out_specs=[pl.BlockSpec(memory_space=pltpu.VMEM)] * 3,
-        scratch_shapes=[pltpu.SMEM((16,), jnp.int32)],
+        out_shape=shapes,
+        in_specs=[pl.BlockSpec(memory_space=pltpu.HBM), pl.BlockSpec(memory_space=pl.ANY)],
+        out_specs=[pl.BlockSpec(memory_space=pltpu.VMEM)] * len(shapes),
+        scratch_shapes=[
+            pltpu.VMEM((SHARES, 2 * LANES, BLOCK), jnp.bfloat16),
+            pltpu.VMEM((SHARES, phase_rows, LANES), jnp.float32),
+            pltpu.VMEM((SHARES, phase_rows, LANES), jnp.float32),
+            pltpu.SMEM((16,), jnp.int32),
+            pltpu.SMEM(lengths.shape, jnp.int32),
+            pltpu.SemaphoreType.DMA,
+        ],
         compiler_params=pltpu.CompilerParams(vmem_limit_bytes=SMALL),
         name="tables",
-    )(lengths, after)
+    )(*in_hbm(lengths), after)
 
 
 def swapped(value, mask):
@@ -540,10 +567,29 @@
     return result
 
 
-def prepare_kernel(
-    count, local, lengths, latitude, weights, coupling, poly, gram, pt, square
-):
+def hold_rows(lengths, me, local, held):
+    firsts = first_rows(lengths, near(me) + near(me ^ SHARES), local)
+    for index, first in enumerate(firsts):
+        held[pl.ds(index, 1), :] = row_arrays(first)
+    for half in range(2):
+        begin = least(firsts[half * SHARES : (half + 1) * SHARES])
+        held[pl.ds(2 * SHARES + half, 1), :] = row_arrays(begin)
+
+
+def prepare_kernel(count, local, lengths_held, latitude_held, weights_held, after, *refs):
+    coupling, poly, gram, held, pt, square, lengths, latitude, weights, sems = refs
+    copies = [
+        pltpu.make_async_copy(source, target, sems.at[index])
+        for index, (source, target) in enumerate(
+            ((lengths_held, lengths), (latitude_held, latitude), (weights_held, weights))
+        )
+    ]
+    for copy in copies:
+        copy.start()
+    for copy in copies:
+        copy.wait()
     me = device_id()
+    hold_rows(lengths, me, local, held)
     down = lax.broadcasted_iota(jnp.int32, (8, LANES), 0)
     lane = lax.broadcasted_iota(jnp.int32, (8, LANES), 1)
     group = (lane >> 4) & 3
@@ -635,31 +681,43 @@
     return jax.ShapeDtypeStruct(shape, jnp.float32)
 
 
-def prepare(lengths, latitude, weights, count, local):
+def prepare(lengths, latitude, weights, after, count, local):
     return pl.pallas_call(
         functools.partial(prepare_kernel, count, local),
         out_shape=[
             floats(2, SHARES, GROUP, LANES),
             jax.ShapeDtypeStruct((3 * LANES, LANES), jnp.bfloat16),
             jax.ShapeDtypeStruct((3 * LANES, LANES), jnp.bfloat16),
+            jax.ShapeDtypeStruct((GROUP, LANES), jnp.int32),
         ],
-        in_specs=[SMEM] * 3,
-        out_specs=[VMEM] * 3,
+        in_specs=[pl.BlockSpec(memory_space=pltpu.HBM)] * 3 + [pl.BlockSpec(memory_space=pl.ANY)],
+        out_specs=[VMEM] * 4,
         scratch_shapes=[
             pltpu.VMEM((SHARES + 1, WAVES, LANES), jnp.float32),
             pltpu.VMEM((SHARES, GROUP, LANES), jnp.float32),
+            pltpu.SMEM(lengths.shape, jnp.int32),
+            pltpu.SMEM(latitude.shape, jnp.float32),
+            pltpu.SMEM(weights.shape, jnp.float32),
+            pltpu.SemaphoreType.DMA((3,)),
         ],
         compiler_params=pltpu.CompilerParams(vmem_limit_bytes=SMALL),
         name="prepare",
-    )(lengths, latitude, weights)
-
-
-def couple_kernel(local, lengths, rates, coupling, *refs):
+    )(*in_hbm(lengths, latitude, weights), after)
+
+
+def fill_window(begin, arrays, out):
+    channels = out.shape[0] // WINDOW
+    for index in range(WINDOW):
+        value = jnp.zeros((channels, LANES), jnp.float32)
+        for target in range(SHARES):
+            value = jnp.where(begin + index == target, arrays[target], value)
+        out[pl.ds(index * channels, channels), :] = value
+
+
+def couple_kernel(held, rates, coupling, *refs):
     messages, (own, other) = [ref[...] for ref in refs[:SHARES]], refs[SHARES:]
     channels = rates.shape[0]
-    me = device_id()
-    *firsts, far = first_rows(lengths, near(me) + [(me ^ SHARES) & SHARES], local)
-    arrays = by_row(messages, firsts)
+    arrays = by_row(messages, [held[pl.ds(index, 1), :] for index in range(SHARES)])
     sums = [jnp.zeros((channels, LANES), jnp.float32)] * SHARES
     for source in range(SHARES):
         both = arrays[source][:channels]
@@ -674,88 +732,84 @@
                     + coupling[0, target, at, :] * moved_both
                     - coupling[1, target, at, :] * moved_second
                 )
-    for first, out in ((least(firsts), own), (far, other)):
-        begin = row_arrays(first)
-        for index in range(WINDOW):
-            value = jnp.zeros((channels, LANES), jnp.float32)
-            for target in range(SHARES):
-                value = jnp.where(begin + index == target, sums[target], value)
-            out[pl.ds(index * channels, channels), :] = value
-
-
-def couple(lengths, rates, coupling, messages, local):
+    for half, out in enumerate((own, other)):
+        begin = held[pl.ds(2 * SHARES + half, 1), :]
+        fill_window(begin, sums, out)
+
+
+def couple(held, rates, coupling, messages):
     channels = rates.shape[0]
     return pl.pallas_call(
-        functools.partial(couple_kernel, local),
+        couple_kernel,
         out_shape=[floats(WINDOW * channels, LANES)] * 2,
-        in_specs=[SMEM] + [VMEM] * (2 + SHARES),
+        in_specs=[VMEM] * (3 + SHARES),
         out_specs=[VMEM] * 2,
         compiler_params=pltpu.CompilerParams(vmem_limit_bytes=SMALL),
         name="couple",
-    )(lengths, rates, coupling, *messages)
-
-
-def pack_kernel(local, lengths, after, *refs):
-    messages, (across, rows, *chunks) = [ref[...] for ref in refs[:SHARES]], refs[SHARES:]
+    )(held, rates, coupling, *messages)
+
+
+def pack_kernel(held, after, *refs):
+    messages, (rows, sent) = [ref[...] for ref in refs[:SHARES]], refs[SHARES:]
     channels = messages[0].shape[0] // 2
     me = device_id()
-    for share in range(SHARES):
-        chunks[ORDER.index(share)][...] = across[pl.ds(share * channels, channels), :]
-    arrays = by_row(
-        [interleaved(message, me >= SHARES) for message in messages],
-        first_rows(lengths, near(me), local),
-    )
+    places = [held[pl.ds(index, 1), :] for index in range(SHARES)]
+    near_half = by_row([interleaved(message, me >= SHARES) for message in messages], places)
+    far_half = by_row([interleaved(message, me < SHARES) for message in messages], places)
     for index in range(SHARES):
-        rows[pl.ds(index * channels, channels), :] = arrays[index]
-
-
-def pack(lengths, after, messages, across, local):
+        rows[pl.ds(index * channels, channels), :] = near_half[index]
+    fill_window(held[pl.ds(2 * SHARES, 1), :], far_half, sent)
+
+
+def pack(held, after, messages):
     channels = messages[0].shape[0] // 2
     return pl.pallas_call(
-        functools.partial(pack_kernel, local),
-        out_shape=[floats(SHARES * channels, LANES)] + [floats(channels, LANES)] * SHARES,
-        in_specs=[SMEM, pl.BlockSpec(memory_space=pl.ANY)] + [VMEM] * (SHARES + 1),
-        out_specs=[VMEM] * (SHARES + 1),
+        pack_kernel,
+        out_shape=[floats(SHARES * channels, LANES), floats(WINDOW * channels, LANES)],
+        in_specs=[VMEM, pl.BlockSpec(memory_space=pl.ANY)] + [VMEM] * SHARES,
+        out_specs=[VMEM] * 2,
         compiler_params=pltpu.CompilerParams(vmem_limit_bytes=SMALL),
         name="pack",
-    )(lengths, after, *messages, across)
-
-
-def hand_out_kernel(local, lengths, own, other, *outs):
+    )(held, after, *messages)
+
+
+def hand_out_kernel(held, own, other, *outs):
     channels = outs[0].shape[0]
-    firsts = first_rows(lengths, near(device_id()), local)
-    begin = row_arrays(least(firsts))
+    begin = held[pl.ds(2 * SHARES, 1), :]
     sums = []
     for index in range(WINDOW):
         at = pl.ds(index * channels, channels)
         sums.append(own[at, :] + other[at, :])
-    for first, out in zip(firsts, outs):
-        array = row_arrays(first) - begin
+    for place, out in enumerate(outs):
+        array = held[pl.ds(place, 1), :] - begin
         value = sums[0]
         for index in range(1, WINDOW):
             value = jnp.where(array == index, sums[index], value)
         out[...] = value
 
 
-def hand_out(lengths, own, other, local):
+def hand_out(held, own, other):
     channels = own.shape[0] // WINDOW
     return pl.pallas_call(
-        functools.partial(hand_out_kernel, local),
+        hand_out_kernel,
         out_shape=[floats(channels, LANES)] * SHARES,
-        in_specs=[SMEM] + [VMEM] * 2,
+        in_specs=[VMEM] * 3,
         out_specs=[VMEM] * SHARES,
         compiler_params=pltpu.CompilerParams(vmem_limit_bytes=SMALL),
         name="hand_out",
-    )(lengths, own, other)
-
-
-def spectrum_kernel(local, lengths, rates, rows, *refs):
-    chunks, (poly, gram, out) = [ref[...] for ref in refs[:SHARES]], refs[SHARES:]
+    )(held, own, other)
+
+
+def spectrum_kernel(held_rows, rates, rows, far, poly, gram, out):
     channels = rates.shape[0]
-    far = [device ^ SHARES for device in near(device_id())]
-    arrays = by_row(chunks, first_rows(lengths, far, local))
+    begin = held_rows[pl.ds(2 * SHARES + 1, 1), :]
+    arrays = []
     for index in range(SHARES):
-        arrays[index] = arrays[index] + rows[pl.ds(index * channels, channels), :]
+        value = rows[pl.ds(index * channels, channels), :]
+        for place in range(WINDOW):
+            piece = far[pl.ds(place * channels, channels), :]
+            value = value + jnp.where(begin + place == index, piece, 0.0)
+        arrays.append(value)
     across = lax.broadcasted_iota(jnp.int32, (1, LANES), 1)
     held = (across >> 6) * 2 + ((across >> 3) & 1)
 
@@ -791,49 +845,46 @@
             out[index, :, part] = product[:, :WAVES].reshape(channels, 8, WAVES)
 
 
-def spectrum(lengths, rates, rows, chunks, poly, gram, local):
+def spectrum(held, rates, rows, far, poly, gram):
     channels = rates.shape[0]
     return pl.pallas_call(
-        functools.partial(spectrum_kernel, local),
+        spectrum_kernel,
         out_shape=pltpu.VMEM((2, channels, 2, 8, WAVES), jnp.float32),
-        in_specs=[SMEM] + [VMEM] * (SHARES + 4),
+        in_specs=[VMEM] * 6,
         out_specs=VMEM,
         compiler_params=pltpu.CompilerParams(vmem_limit_bytes=SMALL),
         name="spectrum",
-    )(lengths, rates, rows, *chunks, poly, gram)
-
-
-def middle_small(
-    received, across, rates, lengths, latitude, weights, local, per_device, count
-):
-    across = swapped(across, SHARES)
-    coupling, poly, gram = prepare(lengths, latitude, weights, count, local)
-    part, sent_part = couple(lengths, rates, coupling, received, local)
+    )(held, rates, rows, far, poly, gram)
+
+
+def middle_small(messages, rates, lengths, latitude, weights, local, per_device, count):
+    coupling, poly, gram, held = prepare(lengths, latitude, weights, rates, count, local)
+    received = exchanged(messages)
+    part, sent_part = couple(held, rates, coupling, received)
     other_part = swapped(sent_part, SHARES)
     tables = tables_of(lengths, part, local, per_device)
-    rows, *chunks = pack(lengths, tables[1], received, across, local)
-    chunks = exchanged(chunks)
-    replies = hand_out(lengths, part, other_part, local)
-    return replies, tables, (lengths, rates, rows, chunks, poly, gram, local)
+    rows, sent_rows = pack(held, tables[1], received)
+    far = swapped(sent_rows, SHARES)
+    replies = hand_out(held, part, other_part)
+    return replies, tables, (held, rates, rows, far, poly, gram)
 
 
 def on_device(cot_first, cot_second, strength, lengths, latitude, weights):
     local = cot_first.shape[1]
     count = lax.axis_size(AXES)
     per_device = WAVES // count
-    *messages, across, rates, kept = analyse(lengths, strength, cot_second, cot_first, per_device)
-    received = exchanged(messages)
+    *messages, rates, kept = analyse(lengths, strength, cot_second, cot_first, per_device)
     arguments = (lengths, latitude, weights, local, per_device)
     small = count == 2 * SHARES and lengths.shape[0] == GROUP
     if small:
-        replies, tables, pieces = middle_small(received, across, rates, *arguments, count)
+        replies, tables, pieces = middle_small(messages, rates, *arguments, count)
     else:
-        replies, grad_target = middle_general(received, strength, *arguments)
+        replies, grad_target = middle_general(exchanged(messages), strength, *arguments)
         tables = tables_of(lengths, replies[0], local, per_device)
     answers = exchanged(replies)
     if small:
         grad_target = spectrum(*pieces)
-    grad_state, grad_target = restore(lengths, answers, kept, tables, grad_target)
+    grad_state, grad_target = restore(answers, kept, tables, grad_target)
     return (grad_state, grad_target)
 
 

time: 26.5 us -> 25.6 us (0.966)
  waiting for transfers between devices: 0.87 us -> 6.22 us
  starting transfers between devices: 12.7 us -> 8.91 us
  Pallas kernels: 12 us -> 9.57 us
    ppermute x11 -> x8, waiting for transfers between devices: 0.87 us -> 6.22 us  [swapped(): return lax.ppermute(value, AXES, [(i, i ^ mask) for i in range(count)])]
    ppermute x11 -> x8, starting transfers between devices: 12.7 us -> 8.91 us  [swapped(): return lax.ppermute(value, AXES, [(i, i ^ mask) for i in range(count)])]
    pallas_call x4, Pallas kernels: 4.03 us -> 1.67 us  [the longest x1 0.89 us: spectrum(): pl.pallas_call(spectrum_kernel, out_shape=pltpu.VMEM((2, channels, 2, 8,...]
    pallas_call x1, Pallas kernels: 2.23 us -> 1.72 us  [restore(): pl.pallas_call(restore_kernel, out_shape=[jax.ShapeDtypeStruct((channels,...]
    pallas_call x1, Pallas kernels: 1.3 us -> 1.71 us  [tables_of(): pl.pallas_call(functools.partial(tables_kernel, per_device, local), out_s...]
  transfers between devices with their start and end apart: 11 -> 8, of which waited for: 2 -> 5; matrix products, arithmetic and copies ran while one was open for 0% -> 0% of each run, Pallas kernels for 25% -> 17%
where the time goes in v6:
time: 25.6 us; the launch traced here: 25.4 us
  Pallas kernels  9.57 us (37%)
  starting transfers between devices  8.91 us (35%)
  waiting for transfers between devices  6.22 us (24%)
  between operations  0.7 us (3%)
    ppermute x8, starting transfers between devices, swapped(): return lax.ppermute(value, AXES, [(i, i ^ mask) for i in range(count)])  8.91 us
    ppermute x8, waiting for transfers between devices, swapped(): return lax.ppermute(value, AXES, [(i, i ^ mask) for i in range(count)])  6.22 us
    pallas_call x1, Pallas kernels, analyse(): pl.pallas_call(functools.partial(analyse_kernel, per_device), out_shape=[...  3.05 us
    pallas_call x1, Pallas kernels, restore(): pl.pallas_call(restore_kernel, out_shape=[jax.ShapeDtypeStruct((channels,...  1.72 us
    pallas_call x1, Pallas kernels, tables_of(): pl.pallas_call(functools.partial(tables_kernel, per_device, local), out_s...  1.71 us
    pallas_call x1, Pallas kernels, prepare(): pl.pallas_call(functools.partial(prepare_kernel, count, local), out_shape...  1.41 us
    pallas_call x1, Pallas kernels, spectrum(): pl.pallas_call(spectrum_kernel, out_shape=pltpu.VMEM((2, channels, 2, 8,...  0.89 us
    pallas_call x1, Pallas kernels, couple(): pl.pallas_call(couple_kernel, out_shape=[floats(WINDOW * channels, LANES)...  0.56 us
  transfers between devices with their start and end apart: 8, of which 5 were waited for; matrix products, arithmetic and copies ran while one was open for 0% of the time, Pallas kernels for 17%

profile of v6, /device:TPU:0, one launch (start us, length us, event | category | flops | bytes accessed | tf_op | source)
XLA Modules:
  0.0 25.4 jit_solution(16055388959868148555)
XLA Ops:
  0.6 3.0 %analyse.1 = (f32[100,128]{1,0:T(8,128)S(1)}, f32[100,128]{1,0:T(8,128)S(1)}, f32[100,128]{1,0:T(8,128)S(1)}, f32[100,128]{1,0:T(8,128)S(1)}, f32[50,128]{1,0:T(8,128)S(1)}, /*index=5*/f32[50,4608]{1,0:T(8,128)S(1)}) custom-call(s32[16]{0:T(128)} %lengths_held.5, f32[2,50]{1,0:T(2,128)} %strength_held.1, f32[50,4608]{1,0:T(8,128)} %second.1, f32[50,4608]{1,0:T(8,128)} %first.1), custom_call_target="tpu_custom_call" | custom-call | tf_op jit(solution)/shard_map/analyse/pallas_call | solution.py:297
  3.7 3.1 %collective-permute-start = (f32[100,128]{1,0:T(8,128)S(1)}, f32[100,128]{1,0:T(8,128)S(1)}, u32[]{:S(2)}, u32[]{:S(2)}) collective-permute-start(f32[100,128]{1,0:T(8,128)S(1)} %get-tuple-element.29), channel_id=1, source_target_pairs={{0,4},{1,5},{4,0},{5,1},{8,12},{9,13},{12,8},{13,9},{2,6},{3,7},{6... | collective-permute-start | bytes 153608 | tf_op jit(solution)/shard_map/ppermute | solution.py:481
  6.8 0.0 collective-permute-start.1
  6.8 0.2 collective-permute-start.2
  7.0 1.4 %prepare.1 = (f32[2,4,16,128]{3,2,1,0:T(8,128)S(1)}, bf16[384,128]{1,0:T(8,128)(2,1)S(1)}, bf16[384,128]{1,0:T(8,128)(2,1)S(1)}, s32[16,128]{1,0:T(8,128)S(1)}) custom-call(s32[16]{0:T(128)} %lengths_held.5, f32[16]{0:T(128)} %latitude_held.1, f32[16]{0:T(128)} %weights_held.1, f32[50,128]{1,0:T(8,128)S(1)} %get-tuple-element.25.after.rates), custom_call_target="tpu_custom_call" | custom-call | tf_op jit(solution)/shard_map/prepare/pallas_call | solution.py:685
  8.4 0.5 %collective-permute-done.refs_1_ = f32[100,128]{1,0:T(8,128)S(1)} collective-permute-done((f32[100,128]{1,0:T(8,128)S(1)}, f32[100,128]{1,0:T(8,128)S(1)}, u32[]{:S(2)}, u32[]{:S(2)}) %collective-permute-start) | collective-permute-done | bytes 51232 | tf_op jit(solution)/shard_map/ppermute | solution.py:481
  8.9 1.8 %collective-permute-done.1.refs_2_ = f32[100,128]{1,0:T(8,128)S(1)} collective-permute-done((f32[100,128]{1,0:T(8,128)S(1)}, f32[100,128]{1,0:T(8,128)S(1)}, u32[]{:S(2)}, u32[]{:S(2)}) %collective-permute-start.1) | collective-permute-done | bytes 51232 | tf_op jit(solution)/shard_map/ppermute | solution.py:481
  10.6 0.0 collective-permute-done.2.refs_3_
  10.7 0.6 %couple.1 = (f32[150,128]{1,0:T(8,128)S(1)}, f32[150,128]{1,0:T(8,128)S(1)}) custom-call(s32[16,128]{1,0:T(8,128)S(1)} %get-tuple-element.26.held.held_rows, f32[50,128]{1,0:T(8,128)S(1)} %get-tuple-element.25.after.rates, f32[2,4,16,128]{3,2,1,0:T(8,128)S(1)} %get-tuple-element.27.coupling, f32[100,128]{1,0:T(8,128)S(1)} %get-tuple-element.28.refs_0_, ...), custom_call_target="tpu_custom_call" | custom-call | tf_op jit(solution)/shard_map/couple/pallas_call | solution.py:742
  11.2 2.7 %collective-permute-start.3 = (f32[150,128]{1,0:T(8,128)S(1)}, f32[150,128]{1,0:T(8,128)S(1)}, u32[]{:S(2)}, u32[]{:S(2)}) collective-permute-start(f32[150,128]{1,0:T(8,128)S(1)} %get-tuple-element.33), channel_id=1, source_target_pairs={{0,8},{1,9},{4,12},{5,13},{8,0},{9,1},{12,4},{13,5},{2,10},{3,11},... | collective-permute-start | bytes 230408 | tf_op jit(solution)/shard_map/ppermute | solution.py:481
  13.9 1.7 %tables.1 = (bf16[21,256,256]{2,1,0:T(8,128)(2,1)S(1)}, f32[21,128]{1,0:T(8,128)S(1)}, f32[21,128]{1,0:T(8,128)S(1)}, f32[84,128]{1,0:T(8,128)S(1)}, f32[54,256]{1,0:T(8,128)S(1)}) custom-call(s32[16]{0:T(128)} %lengths_held.5, f32[150,128]{1,0:T(8,128)S(1)} %get-tuple-element.32.own.after), custom_call_target="tpu_custom_call" | custom-call | tf_op jit(solution)/shard_map/tables/pallas_call | solution.py:461
  15.6 0.2 pack.1
  15.8 0.4 %collective-permute-start.7 = (f32[150,128]{1,0:T(8,128)S(1)}, f32[150,128]{1,0:T(8,128)S(1)}, u32[]{:S(2)}, u32[]{:S(2)}) collective-permute-start(f32[150,128]{1,0:T(8,128)S(1)} %get-tuple-element.45), channel_id=1, source_target_pairs={{0,8},{1,9},{4,12},{5,13},{8,0},{9,1},{12,4},{13,5},{2,10},{3,11},... | collective-permute-start | bytes 230408 | tf_op jit(solution)/shard_map/ppermute | solution.py:481
  16.2 1.8 %collective-permute-done.3.other = f32[150,128]{1,0:T(8,128)S(1)} collective-permute-done((f32[150,128]{1,0:T(8,128)S(1)}, f32[150,128]{1,0:T(8,128)S(1)}, u32[]{:S(2)}, u32[]{:S(2)}) %collective-permute-start.3) | collective-permute-done | bytes 76832 | tf_op jit(solution)/shard_map/ppermute | solution.py:481
  18.0 2.4 %collective-permute-start.4 = (f32[50,128]{1,0:T(8,128)S(1)}, f32[50,128]{1,0:T(8,128)S(1)}, u32[]{:S(2)}, u32[]{:S(2)}) collective-permute-start(f32[50,128]{1,0:T(8,128)S(1)} %get-tuple-element.35), channel_id=1, source_target_pairs={{0,4},{1,5},{4,0},{5,1},{8,12},{9,13},{12,8},{13,9},{2,6},{3,7},{6... | collective-permute-start | bytes 76808 | tf_op jit(solution)/shard_map/ppermute | solution.py:481
  20.4 0.0 collective-permute-start.5
  20.4 0.2 collective-permute-start.6
  20.6 1.8 %collective-permute-done.7.far = f32[150,128]{1,0:T(8,128)S(1)} collective-permute-done((f32[150,128]{1,0:T(8,128)S(1)}, f32[150,128]{1,0:T(8,128)S(1)}, u32[]{:S(2)}, u32[]{:S(2)}) %collective-permute-start.7) | collective-permute-done | bytes 76832 | tf_op jit(solution)/shard_map/ppermute | solution.py:481
  22.3 0.9 %spectrum.1.refs_10_ = f32[2,50,2,8,64]{4,3,2,1,0:T(8,128)S(1)} custom-call(s32[16,128]{1,0:T(8,128)S(1)} %get-tuple-element.26.held.held_rows, f32[50,128]{1,0:T(8,128)S(1)} %get-tuple-element.25.after.rates, f32[200,128]{1,0:T(8,128)S(1)} %get-tuple-element.44.rows, f32[150,128]{1,0:T(8,128)S(1)} %collective-permute-done.7.far, ...), custom_call_target="tpu_custom_call" | custom-call | tf_op jit(solution)/shard_map/spectrum/pallas_call | solution.py:850
  23.2 0.0 collective-permute-done.4.refs_1_
  23.2 0.4 %collective-permute-done.5.refs_2_ = f32[50,128]{1,0:T(8,128)S(1)} collective-permute-done((f32[50,128]{1,0:T(8,128)S(1)}, f32[50,128]{1,0:T(8,128)S(1)}, u32[]{:S(2)}, u32[]{:S(2)}) %collective-permute-start.5) | collective-permute-done | bytes 25632 | tf_op jit(solution)/shard_map/ppermute | solution.py:481
  23.7 0.0 collective-permute-done.6.refs_3_
  23.7 1.7 %restore.1 = (f32[50,4608]{1,0:T(8,128)}, f32[2,50,2,8,64]{4,3,2,1,0:T(8,128)}) custom-call(f32[50,128]{1,0:T(8,128)S(1)} %get-tuple-element.34.refs_0_, f32[50,128]{1,0:T(8,128)S(1)} %collective-permute-done.4.refs_1_, f32[50,128]{1,0:T(8,128)S(1)} %collective-permute-done.5.refs_2_, f32[50,128]{1,0:T(8,128)S(1)} %collective-permute-done.6.refs_3_, ...), custom_call_target="tpu_custom_call" | custom-call | tf_op jit(solution)/shard_map/restore/pallas_call | solution.py:383
  (1 shorter events, 0.0 us)
Async XLA Ops:
  3.7 5.2 %collective-permute-start = (f32[100,128]{1,0:T(8,128)S(1)}, f32[100,128]{1,0:T(8,128)S(1)}, u32[]{:S(2)}, u32[]{:S(2)}) collective-permute-start(f32[100,128]{1,0:T(8,128)S(1)} %get-tuple-element.29), channel_id=1, source_target_pairs={{0,4},{1,5},{4,0},{5,1},{8,12},{9,13},{12,8},{13,9},{2,6},{3,7},{6... | collective-permute-start | bytes 153608 | tf_op jit(solution)/shard_map/ppermute | solution.py:481
  6.8 3.9 %collective-permute-start.1 = (f32[100,128]{1,0:T(8,128)S(1)}, f32[100,128]{1,0:T(8,128)S(1)}, u32[]{:S(2)}, u32[]{:S(2)}) collective-permute-start(f32[100,128]{1,0:T(8,128)S(1)} %get-tuple-element.30), channel_id=1, source_target_pairs={{0,5},{1,4},{4,1},{5,0},{8,13},{9,12},{12,9},{13,8},{2,7},{3,6},{6... | collective-permute-start | bytes 153608 | tf_op jit(solution)/shard_map/ppermute | solution.py:481
  6.8 3.9 %collective-permute-start.2 = (f32[100,128]{1,0:T(8,128)S(1)}, f32[100,128]{1,0:T(8,128)S(1)}, u32[]{:S(2)}, u32[]{:S(2)}) collective-permute-start(f32[100,128]{1,0:T(8,128)S(1)} %get-tuple-element.31), channel_id=1, source_target_pairs={{0,1},{1,0},{4,5},{5,4},{8,9},{9,8},{12,13},{13,12},{2,3},{3,2},{6... | collective-permute-start | bytes 153608 | tf_op jit(solution)/shard_map/ppermute | solution.py:481
  11.2 6.7 %collective-permute-start.3 = (f32[150,128]{1,0:T(8,128)S(1)}, f32[150,128]{1,0:T(8,128)S(1)}, u32[]{:S(2)}, u32[]{:S(2)}) collective-permute-start(f32[150,128]{1,0:T(8,128)S(1)} %get-tuple-element.33), channel_id=1, source_target_pairs={{0,8},{1,9},{4,12},{5,13},{8,0},{9,1},{12,4},{13,5},{2,10},{3,11},... | collective-permute-start | bytes 230408 | tf_op jit(solution)/shard_map/ppermute | solution.py:481
  15.8 6.5 %collective-permute-start.7 = (f32[150,128]{1,0:T(8,128)S(1)}, f32[150,128]{1,0:T(8,128)S(1)}, u32[]{:S(2)}, u32[]{:S(2)}) collective-permute-start(f32[150,128]{1,0:T(8,128)S(1)} %get-tuple-element.45), channel_id=1, source_target_pairs={{0,8},{1,9},{4,12},{5,13},{8,0},{9,1},{12,4},{13,5},{2,10},{3,11},... | collective-permute-start | bytes 230408 | tf_op jit(solution)/shard_map/ppermute | solution.py:481
  18.0 5.2 %collective-permute-start.4 = (f32[50,128]{1,0:T(8,128)S(1)}, f32[50,128]{1,0:T(8,128)S(1)}, u32[]{:S(2)}, u32[]{:S(2)}) collective-permute-start(f32[50,128]{1,0:T(8,128)S(1)} %get-tuple-element.35), channel_id=1, source_target_pairs={{0,4},{1,5},{4,0},{5,1},{8,12},{9,13},{12,8},{13,9},{2,6},{3,7},{6... | collective-permute-start | bytes 76808 | tf_op jit(solution)/shard_map/ppermute | solution.py:481
  20.4 3.3 %collective-permute-start.5 = (f32[50,128]{1,0:T(8,128)S(1)}, f32[50,128]{1,0:T(8,128)S(1)}, u32[]{:S(2)}, u32[]{:S(2)}) collective-permute-start(f32[50,128]{1,0:T(8,128)S(1)} %get-tuple-element.36), channel_id=1, source_target_pairs={{0,5},{1,4},{4,1},{5,0},{8,13},{9,12},{12,9},{13,8},{2,7},{3,6},{6... | collective-permute-start | bytes 76808 | tf_op jit(solution)/shard_map/ppermute | solution.py:481
  20.4 3.3 %collective-permute-start.6 = (f32[50,128]{1,0:T(8,128)S(1)}, f32[50,128]{1,0:T(8,128)S(1)}, u32[]{:S(2)}, u32[]{:S(2)}) collective-permute-start(f32[50,128]{1,0:T(8,128)S(1)} %get-tuple-element.37), channel_id=1, source_target_pairs={{0,1},{1,0},{4,5},{5,4},{8,9},{9,8},{12,13},{13,12},{2,3},{3,2},{6... | collective-permute-start | bytes 76808 | tf_op jit(solution)/shard_map/ppermute | solution.py:481

commit v7 on v6

--- a/solution.py
+++ b/solution.py
@@ -16,6 +16,7 @@
 SHARES = 4
 GROUP = WAVES // SHARES
 ORDER = (0, 2, 3, 1)
+RETURN = (0, 3, 2, 1)
 PAD = 64
 FULL = 60 * 1024 * 1024
 WINDOW = 3
@@ -178,6 +179,10 @@
     )
 
 
+def padded(value):
+    return jnp.pad(value, ((0, -value.shape[0] % 8), (0, 0)))
+
+
 def load_fields(second, first, fields, sems):
     copies = [
         pltpu.make_async_copy(source, fields.at[index], sems.at[index])
@@ -189,7 +194,7 @@
 
 
 def analyse_kernel(per_device, lengths_held, strength_held, second, first, *refs):
-    messages, (rates, kept, fields, lengths, strength, basis, cosine, sine, lhs, total, table) = (
+    messages, (rates, kept, fields, lengths, strength, basis, cosine, sine, total, table) = (
         refs[:SHARES],
         refs[SHARES:-3],
     )
@@ -213,23 +218,23 @@
         basis[slot, :, :LANES] = high
         basis[slot, :, LANES:] = low
     total[...] = jnp.zeros_like(total)
-    lhs[...] = jnp.zeros_like(lhs)
     within = lax.broadcasted_iota(jnp.int32, (1, BLOCK), 1)
 
-    def add_block(block, place, slot, low_end, high_end, buffer):
+    def add_block(block, place, slot, low_end, high_end):
         keep = (within >= low_end) & (within < high_end)
+        highs, lows = [], []
         for index in range(2):
             piece = jnp.where(keep, fields[index, :, pl.ds(place, BLOCK)], 0.0)
-            high = piece.astype(jnp.bfloat16)
-            low = (piece - high.astype(jnp.float32)).astype(jnp.bfloat16)
-            lhs[buffer, pl.ds(index * PAD, channels), :] = high
-            lhs[buffer, pl.ds((2 + index) * PAD, channels), :] = low
-        product = jnp.dot(
-            lhs[buffer, : 2 * PAD, :], basis[slot], preferred_element_type=jnp.float32
-        )
+            high = piece.astype(jnp.bfloat16).astype(jnp.float32)
+            highs.append(padded(high))
+            lows.append(padded(piece - high))
+        highs, lows = [
+            jnp.concatenate(sides, axis=0).astype(jnp.bfloat16) for sides in (highs, lows)
+        ]
+        product = jnp.dot(highs, basis[slot], preferred_element_type=jnp.float32)
         value = product[:, :LANES] + product[:, LANES:]
         value = value + jnp.dot(
-            lhs[buffer, 2 * PAD :, :], basis[slot, :, :LANES], preferred_element_type=jnp.float32
+            lows, basis[slot, :, :LANES], preferred_element_type=jnp.float32
         )
         turned = (
             value * cosine[slot, pl.ds(block, 1), :]
@@ -246,15 +251,13 @@
         for later in range(1, SHARES):
             slot = slot + jnp.where(table[2 * SHARES + later] <= place, 1, 0)
         slot = slot & 3
-        add_block(
-            block, place, slot, 0, table[slot] + table[SHARES + slot] - place, block % lhs.shape[0]
-        )
+        add_block(block, place, slot, 0, table[slot] + table[SHARES + slot] - place)
         at = pl.ds(place, BLOCK)
         kept[:, at] = fields[0, :, at] + fields[1, :, at]
     for later in range(1, SHARES):
         block, low_end = split_block(table[2 * SHARES + later], blocks)
         place = pl.multiple_of(block * BLOCK, BLOCK)
-        add_block(block, place, (begin_slot + later) & 3, low_end, BLOCK, later)
+        add_block(block, place, (begin_slot + later) & 3, low_end, BLOCK)
 
     rate_first = column(strength[0:1, :])
     rate_second = column(strength[1:2, :])
@@ -264,7 +267,7 @@
     pairs = []
     for slot in range(SHARES):
         value_second = total[slot, :channels, :]
-        value_first = total[slot, PAD : PAD + channels, :]
+        value_first = total[slot, total.shape[1] // 2 :, :][:channels]
         part_second = rate_second * value_second
         pairs.append((rate_first * (value_first + value_second) + part_second, part_second))
     moved = []
@@ -310,8 +313,7 @@
             pltpu.VMEM((SHARES, BLOCK, 2 * LANES), jnp.bfloat16),
             pltpu.VMEM((SHARES, phase_rows, LANES), jnp.float32),
             pltpu.VMEM((SHARES, phase_rows, LANES), jnp.float32),
-            pltpu.VMEM((4, 4 * PAD, BLOCK), jnp.bfloat16),
-            pltpu.VMEM((SHARES, 2 * PAD, LANES), jnp.float32),
+            pltpu.VMEM((SHARES, 2 * (channels + -channels % 8), LANES), jnp.float32),
             pltpu.SMEM((16,), jnp.int32),
             pltpu.SemaphoreType.DMA((2,)),
             pltpu.SemaphoreType.DMA,
@@ -337,7 +339,7 @@
     for slot in range(SHARES):
         value = jnp.zeros((channels, LANES), jnp.float32)
         for share in range(SHARES):
-            moved = messages[ORDER.index(share)][...]
+            moved = messages[RETURN.index(share)][...]
             if slot != share:
                 moved = pltpu.roll(moved, ((share - slot) * GROUP) % LANES, 1)
             value = jnp.where(chunk == share, moved, value)
@@ -409,17 +411,46 @@
         basis[slot, LANES:, :] = low
 
 
+def waves_kernel(per_device, local, lengths_held, after, basis, cosine, sine, table, lengths, sem):
+    me = device_id()
+    copy = pltpu.make_async_copy(lengths_held, lengths, sem)
+    copy.start()
+    copy.wait()
+    row_table(lengths, table, me, local, lengths.shape[0])
+    fill_tables(table, me, per_device, basis, cosine, sine, local // BLOCK)
+
+
+def waves_of(lengths, after, local, per_device):
+    phase_rows = -(-(local // BLOCK) // 8) * 8
+    return pl.pallas_call(
+        functools.partial(waves_kernel, per_device, local),
+        out_shape=[
+            jax.ShapeDtypeStruct((SHARES, 2 * LANES, BLOCK), jnp.bfloat16),
+            jax.ShapeDtypeStruct((SHARES, phase_rows, LANES), jnp.float32),
+            jax.ShapeDtypeStruct((SHARES, phase_rows, LANES), jnp.float32),
+        ],
+        in_specs=[pl.BlockSpec(memory_space=pltpu.HBM), pl.BlockSpec(memory_space=pl.ANY)],
+        out_specs=[pl.BlockSpec(memory_space=pltpu.VMEM)] * 3,
+        scratch_shapes=[
+            pltpu.SMEM((16,), jnp.int32),
+            pltpu.SMEM(lengths.shape, jnp.int32),
+            pltpu.SemaphoreType.DMA,
+        ],
+        compiler_params=pltpu.CompilerParams(vmem_limit_bytes=SMALL),
+        name="waves",
+    )(*in_hbm(lengths), after)
+
+
 def tables_kernel(
-    per_device, local, lengths_held, after, bases, cosine, sine, choose, mix, *scratch
+    local, lengths_held, basis, cosines, sines, bases, cosine, sine, choose, mix, *scratch
 ):
-    basis, cosines, sines, table, lengths, sem = scratch
+    table, lengths, sem = scratch
     blocks = local // BLOCK
     me = device_id()
     copy = pltpu.make_async_copy(lengths_held, lengths, sem)
     copy.start()
     copy.wait()
     row_table(lengths, table, me, local, lengths.shape[0])
-    fill_tables(table, me, per_device, basis, cosines, sines, blocks)
     within = lax.broadcasted_iota(jnp.int32, (1, BLOCK), 1)
     begin_slot = table[3 * SHARES]
 
@@ -447,10 +478,9 @@
             mix[pl.ds((SHARES - 1) * other + later - 1, 1), :] = jnp.full((1, BLOCK), mark)
 
 
-def tables_of(lengths, after, local, per_device):
+def tables_of(lengths, waves, local):
     blocks = local // BLOCK
     parts = blocks + SHARES - 1
-    phase_rows = -(-blocks // 8) * 8
     shapes = [
         jax.ShapeDtypeStruct((parts, 2 * LANES, BLOCK), jnp.bfloat16),
         jax.ShapeDtypeStruct((parts, LANES), jnp.float32),
@@ -459,21 +489,18 @@
         jax.ShapeDtypeStruct(((SHARES - 1) * blocks, BLOCK), jnp.float32),
     ]
     return pl.pallas_call(
-        functools.partial(tables_kernel, per_device, local),
+        functools.partial(tables_kernel, local),
         out_shape=shapes,
-        in_specs=[pl.BlockSpec(memory_space=pltpu.HBM), pl.BlockSpec(memory_space=pl.ANY)],
+        in_specs=[pl.BlockSpec(memory_space=pltpu.HBM)] + [pl.BlockSpec(memory_space=pltpu.VMEM)] * 3,
         out_specs=[pl.BlockSpec(memory_space=pltpu.VMEM)] * len(shapes),
         scratch_shapes=[
-            pltpu.VMEM((SHARES, 2 * LANES, BLOCK), jnp.bfloat16),
-            pltpu.VMEM((SHARES, phase_rows, LANES), jnp.float32),
-            pltpu.VMEM((SHARES, phase_rows, LANES), jnp.float32),
             pltpu.SMEM((16,), jnp.int32),
             pltpu.SMEM(lengths.shape, jnp.int32),
             pltpu.SemaphoreType.DMA,
         ],
         compiler_params=pltpu.CompilerParams(vmem_limit_bytes=SMALL),
         name="tables",
-    )(*in_hbm(lengths), after)
+    )(*in_hbm(lengths), *waves)
 
 
 def swapped(value, mask):
@@ -481,8 +508,8 @@
     return lax.ppermute(value, AXES, [(i, i ^ mask) for i in range(count)])
 
 
-def exchanged(values):
-    return [swapped(value, share) if share else value for value, share in zip(values, ORDER)]
+def exchanged(values, order):
+    return [swapped(value, share) if share else value for value, share in zip(values, order)]
 
 
 def legendre(latitude, waves):
@@ -577,7 +604,7 @@
 
 
 def prepare_kernel(count, local, lengths_held, latitude_held, weights_held, after, *refs):
-    coupling, poly, gram, held, pt, square, lengths, latitude, weights, sems = refs
+    coupling, mine, factors, held, pt, square, lengths, latitude, weights, sems = refs
     copies = [
         pltpu.make_async_copy(source, target, sems.at[index])
         for index, (source, target) in enumerate(
@@ -652,16 +679,20 @@
     for target in range(SHARES):
         coupling[0, target] = square[target] * scale[target : target + 1, :]
         coupling[1, target] = twice[target] * scale[target : target + 1, :]
-    mine = pt[SHARES]
-    factor = doubling[SHARES : SHARES + 1, :] * (float(local * count) ** -0.5)
+    mine[...] = pt[SHARES]
+    factors[0:1, :] = weight[SHARES : SHARES + 1, :]
+    factors[1:2, :] = doubling[SHARES : SHARES + 1, :] * (float(local * count) ** -0.5)
+
+
+def spectral_factors(mine, factors, poly, gram):
     products = lax.dot_general(
         mine, mine, (((0,), (0,)), ((), ())), precision=HIGHEST, preferred_element_type=jnp.float32
     )
     same = (lax.broadcasted_iota(jnp.int32, (LANES, LANES), 0) & 7) == (
         lax.broadcasted_iota(jnp.int32, (LANES, LANES), 1) & 7
     )
-    products = jnp.where(same, products * weight[SHARES : SHARES + 1, :], 0.0)
-    turned = jnp.concatenate([mine * factor, jnp.zeros_like(mine)], axis=0).T
+    products = jnp.where(same, products * factors[0:1, :], 0.0)
+    turned = jnp.concatenate([mine * factors[1:2, :], jnp.zeros_like(mine)], axis=0).T
     for value, out in ((turned, poly), (products, gram)):
         high = value.astype(jnp.bfloat16)
         low = (value - high.astype(jnp.float32)).astype(jnp.bfloat16)
@@ -686,8 +717,8 @@
         functools.partial(prepare_kernel, count, local),
         out_shape=[
             floats(2, SHARES, GROUP, LANES),
-            jax.ShapeDtypeStruct((3 * LANES, LANES), jnp.bfloat16),
-            jax.ShapeDtypeStruct((3 * LANES, LANES), jnp.bfloat16),
+            floats(WAVES, LANES),
+            floats(8, LANES),
             jax.ShapeDtypeStruct((GROUP, LANES), jnp.int32),
         ],
         in_specs=[pl.BlockSpec(memory_space=pltpu.HBM)] * 3 + [pl.BlockSpec(memory_space=pl.ANY)],
@@ -749,8 +780,8 @@
     )(held, rates, coupling, *messages)
 
 
-def pack_kernel(held, after, *refs):
-    messages, (rows, sent) = [ref[...] for ref in refs[:SHARES]], refs[SHARES:]
+def pack_kernel(held, mine, factors, after, *refs):
+    messages, (rows, sent, poly, gram) = [ref[...] for ref in refs[:SHARES]], refs[SHARES:]
     channels = messages[0].shape[0] // 2
     me = device_id()
     places = [held[pl.ds(index, 1), :] for index in range(SHARES)]
@@ -759,18 +790,20 @@
     for index in range(SHARES):
         rows[pl.ds(index * channels, channels), :] = near_half[index]
     fill_window(held[pl.ds(2 * SHARES, 1), :], far_half, sent)
-
-
-def pack(held, after, messages):
+    spectral_factors(mine[...], factors[...], poly, gram)
+
+
+def pack(held, mine, factors, after, messages):
     channels = messages[0].shape[0] // 2
     return pl.pallas_call(
         pack_kernel,
-        out_shape=[floats(SHARES * channels, LANES), floats(WINDOW * channels, LANES)],
-        in_specs=[VMEM, pl.BlockSpec(memory_space=pl.ANY)] + [VMEM] * SHARES,
-        out_specs=[VMEM] * 2,
+        out_shape=[floats(SHARES * channels, LANES), floats(WINDOW * channels, LANES)]
+        + [jax.ShapeDtypeStruct((3 * LANES, LANES), jnp.bfloat16)] * 2,
+        in_specs=[VMEM] * 3 + [pl.BlockSpec(memory_space=pl.ANY)] + [VMEM] * SHARES,
+        out_specs=[VMEM] * 4,
         compiler_params=pltpu.CompilerParams(vmem_limit_bytes=SMALL),
         name="pack",
-    )(held, after, *messages)
+    )(held, mine, factors, after, *messages)
 
 
 def hand_out_kernel(held, own, other, *outs):
@@ -780,8 +813,8 @@
     for index in range(WINDOW):
         at = pl.ds(index * channels, channels)
         sums.append(own[at, :] + other[at, :])
-    for place, out in enumerate(outs):
-        array = held[pl.ds(place, 1), :] - begin
+    for share, out in zip(RETURN, outs):
+        array = held[pl.ds(ORDER.index(share), 1), :] - begin
         value = sums[0]
         for index in range(1, WINDOW):
             value = jnp.where(array == index, sums[index], value)
@@ -858,12 +891,13 @@
 
 
 def middle_small(messages, rates, lengths, latitude, weights, local, per_device, count):
-    coupling, poly, gram, held = prepare(lengths, latitude, weights, rates, count, local)
-    received = exchanged(messages)
+    coupling, mine, factors, held = prepare(lengths, latitude, weights, rates, count, local)
+    received = exchanged(messages, ORDER)
     part, sent_part = couple(held, rates, coupling, received)
     other_part = swapped(sent_part, SHARES)
-    tables = tables_of(lengths, part, local, per_device)
-    rows, sent_rows = pack(held, tables[1], received)
+    waves = waves_of(lengths, part, local, per_device)
+    rows, sent_rows, poly, gram = pack(held, mine, factors, waves[1], received)
+    tables = tables_of(lengths, waves, local)
     far = swapped(sent_rows, SHARES)
     replies = hand_out(held, part, other_part)
     return replies, tables, (held, rates, rows, far, poly, gram)
@@ -879,9 +913,10 @@
     if small:
         replies, tables, pieces = middle_small(messages, rates, *arguments, count)
     else:
-        replies, grad_target = middle_general(exchanged(messages), strength, *arguments)
-        tables = tables_of(lengths, replies[0], local, per_device)
-    answers = exchanged(replies)
+        replies, grad_target = middle_general(exchanged(messages, ORDER), strength, *arguments)
+        replies = [replies[ORDER.index(share)] for share in RETURN]
+        tables = tables_of(lengths, waves_of(lengths, replies[0], local, per_device), local)
+    answers = exchanged(replies, RETURN)
     if small:
         grad_target = spectrum(*pieces)
     grad_state, grad_target = restore(answers, kept, tables, grad_target)

time: 25.6 us -> 25.2 us (0.984)
  waiting for transfers between devices: 6.22 us -> 5.02 us
  Pallas kernels: 9.57 us -> 10.3 us
    ppermute x8, waiting for transfers between devices: 6.22 us -> 5.02 us  [swapped(): return lax.ppermute(value, AXES, [(i, i ^ mask) for i in range(count)])]
    pallas_call x1 -> x2, Pallas kernels: 1.71 us -> 2.53 us  [the longest x1 1.43 us: waves_of(): pl.pallas_call(functools.partial(waves_kernel, per_device, local), out_sh...]
  transfers between devices with their start and end apart: 8 -> 8, of which waited for: 5 -> 5; matrix products, arithmetic and copies ran while one was open for 0% -> 0% of each run, Pallas kernels for 17% -> 20%
where the time goes in v7:
time: 25.2 us; the launch traced here: 25 us
  Pallas kernels  10.3 us (41%)
  starting transfers between devices  8.99 us (36%)
  waiting for transfers between devices  5.02 us (20%)
  between operations  0.7 us (3%)
    ppermute x8, starting transfers between devices, swapped(): return lax.ppermute(value, AXES, [(i, i ^ mask) for i in range(count)])  8.99 us
    ppermute x8, waiting for transfers between devices, swapped(): return lax.ppermute(value, AXES, [(i, i ^ mask) for i in range(count)])  5.02 us
    pallas_call x1, Pallas kernels, analyse(): pl.pallas_call(functools.partial(analyse_kernel, per_device), out_shape=[...  2.94 us
    pallas_call x1, Pallas kernels, restore(): pl.pallas_call(restore_kernel, out_shape=[jax.ShapeDtypeStruct((channels,...  1.72 us
    pallas_call x1, Pallas kernels, waves_of(): pl.pallas_call(functools.partial(waves_kernel, per_device, local), out_sh...  1.43 us
    pallas_call x1, Pallas kernels, prepare(): pl.pallas_call(functools.partial(prepare_kernel, count, local), out_shape...  1.35 us
    pallas_call x1, Pallas kernels, tables_of(): pl.pallas_call(functools.partial(tables_kernel, local), out_shape=shapes,...  1.1 us
    pallas_call x1, Pallas kernels, spectrum(): pl.pallas_call(spectrum_kernel, out_shape=pltpu.VMEM((2, channels, 2, 8,...  0.89 us
  transfers between devices with their start and end apart: 8, of which 5 were waited for; matrix products, arithmetic and copies ran while one was open for 0% of the time, Pallas kernels for 20%

profile of v7, /device:TPU:0, one launch (start us, length us, event | category | flops | bytes accessed | tf_op | source)
XLA Modules:
  0.0 25.0 jit_solution(14117134257258399685)
XLA Ops:
  0.6 2.9 %analyse.1 = (f32[100,128]{1,0:T(8,128)S(1)}, f32[100,128]{1,0:T(8,128)S(1)}, f32[100,128]{1,0:T(8,128)S(1)}, f32[100,128]{1,0:T(8,128)S(1)}, f32[50,128]{1,0:T(8,128)S(1)}, /*index=5*/f32[50,4608]{1,0:T(8,128)S(1)}) custom-call(s32[16]{0:T(128)} %lengths_held.7, f32[2,50]{1,0:T(2,128)} %strength_held.1, f32[50,4608]{1,0:T(8,128)} %second.1, f32[50,4608]{1,0:T(8,128)} %first.1), custom_call_target="tpu_custom_call" | custom-call | tf_op jit(solution)/shard_map/analyse/pallas_call | solution.py:300
  3.6 3.1 %collective-permute-start = (f32[100,128]{1,0:T(8,128)S(1)}, f32[100,128]{1,0:T(8,128)S(1)}, u32[]{:S(2)}, u32[]{:S(2)}) collective-permute-start(f32[100,128]{1,0:T(8,128)S(1)} %get-tuple-element.34), channel_id=1, source_target_pairs={{0,4},{1,5},{4,0},{5,1},{8,12},{9,13},{12,8},{13,9},{2,6},{3,7},{6... | collective-permute-start | bytes 153608 | tf_op jit(solution)/shard_map/ppermute | solution.py:508
  6.7 0.0 collective-permute-start.1
  6.7 0.2 collective-permute-start.2
  6.9 1.3 %prepare.1 = (f32[2,4,16,128]{3,2,1,0:T(8,128)S(1)}, f32[64,128]{1,0:T(8,128)S(1)}, f32[8,128]{1,0:T(8,128)S(1)}, s32[16,128]{1,0:T(8,128)S(1)}) custom-call(s32[16]{0:T(128)} %lengths_held.7, f32[16]{0:T(128)} %latitude_held.1, f32[16]{0:T(128)} %weights_held.1, f32[50,128]{1,0:T(8,128)S(1)} %get-tuple-element.30.after.rates), custom_call_target="tpu_custom_call" | custom-call | tf_op jit(solution)/shard_map/prepare/pallas_call | solution.py:716
  8.2 0.6 %collective-permute-done.refs_1_ = f32[100,128]{1,0:T(8,128)S(1)} collective-permute-done((f32[100,128]{1,0:T(8,128)S(1)}, f32[100,128]{1,0:T(8,128)S(1)}, u32[]{:S(2)}, u32[]{:S(2)}) %collective-permute-start) | collective-permute-done | bytes 51232 | tf_op jit(solution)/shard_map/ppermute | solution.py:508
  8.8 1.7 %collective-permute-done.1.refs_2_ = f32[100,128]{1,0:T(8,128)S(1)} collective-permute-done((f32[100,128]{1,0:T(8,128)S(1)}, f32[100,128]{1,0:T(8,128)S(1)}, u32[]{:S(2)}, u32[]{:S(2)}) %collective-permute-start.1) | collective-permute-done | bytes 51232 | tf_op jit(solution)/shard_map/ppermute | solution.py:508
  10.5 0.0 collective-permute-done.2.refs_3_
  10.5 0.5 %couple.1 = (f32[150,128]{1,0:T(8,128)S(1)}, f32[150,128]{1,0:T(8,128)S(1)}) custom-call(s32[16,128]{1,0:T(8,128)S(1)} %get-tuple-element.31.held.held_rows, f32[50,128]{1,0:T(8,128)S(1)} %get-tuple-element.30.after.rates, f32[2,4,16,128]{3,2,1,0:T(8,128)S(1)} %get-tuple-element.32.coupling, f32[100,128]{1,0:T(8,128)S(1)} %get-tuple-element.33.refs_0_, ...), custom_call_target="tpu_custom_call" | custom-call | tf_op jit(solution)/shard_map/couple/pallas_call | solution.py:773
  11.1 2.7 %collective-permute-start.3 = (f32[150,128]{1,0:T(8,128)S(1)}, f32[150,128]{1,0:T(8,128)S(1)}, u32[]{:S(2)}, u32[]{:S(2)}) collective-permute-start(f32[150,128]{1,0:T(8,128)S(1)} %get-tuple-element.38), channel_id=1, source_target_pairs={{0,8},{1,9},{4,12},{5,13},{8,0},{9,1},{12,4},{13,5},{2,10},{3,11},... | collective-permute-start | bytes 230408 | tf_op jit(solution)/shard_map/ppermute | solution.py:508
  13.8 1.4 %waves.1 = (bf16[4,256,256]{2,1,0:T(8,128)(2,1)S(1)}, f32[4,24,128]{2,1,0:T(8,128)S(1)}, f32[4,24,128]{2,1,0:T(8,128)S(1)}) custom-call(s32[16]{0:T(128)} %lengths_held.7, f32[150,128]{1,0:T(8,128)S(1)} %get-tuple-element.37.own.after), custom_call_target="tpu_custom_call" | custom-call | tf_op jit(solution)/shard_map/waves/pallas_call | solution.py:425
  15.2 0.3 %pack.1 = (f32[200,128]{1,0:T(8,128)S(1)}, f32[150,128]{1,0:T(8,128)S(1)}, bf16[384,128]{1,0:T(8,128)(2,1)S(1)}, bf16[384,128]{1,0:T(8,128)(2,1)S(1)}) custom-call(s32[16,128]{1,0:T(8,128)S(1)} %get-tuple-element.31.held.held_rows, f32[64,128]{1,0:T(8,128)S(1)} %get-tuple-element.52.mine, f32[8,128]{1,0:T(8,128)S(1)} %get-tuple-element.53.factors, ...), custom_call_target="tpu_custom_call" | custom-call | tf_op jit(solution)/shard_map/pack/pallas_call | solution.py:798
  15.5 0.4 %collective-permute-start.7 = (f32[150,128]{1,0:T(8,128)S(1)}, f32[150,128]{1,0:T(8,128)S(1)}, u32[]{:S(2)}, u32[]{:S(2)}) collective-permute-start(f32[150,128]{1,0:T(8,128)S(1)} %get-tuple-element.55), channel_id=1, source_target_pairs={{0,8},{1,9},{4,12},{5,13},{8,0},{9,1},{12,4},{13,5},{2,10},{3,11},... | collective-permute-start | bytes 230408 | tf_op jit(solution)/shard_map/ppermute | solution.py:508
  15.9 2.0 %collective-permute-done.3.other = f32[150,128]{1,0:T(8,128)S(1)} collective-permute-done((f32[150,128]{1,0:T(8,128)S(1)}, f32[150,128]{1,0:T(8,128)S(1)}, u32[]{:S(2)}, u32[]{:S(2)}) %collective-permute-start.3) | collective-permute-done | bytes 76832 | tf_op jit(solution)/shard_map/ppermute | solution.py:508
  17.8 1.5 %collective-permute-start.4 = (f32[50,128]{1,0:T(8,128)S(1)}, f32[50,128]{1,0:T(8,128)S(1)}, u32[]{:S(2)}, u32[]{:S(2)}) collective-permute-start(f32[50,128]{1,0:T(8,128)S(1)} %get-tuple-element.40), channel_id=1, source_target_pairs={{0,5},{1,4},{4,1},{5,0},{8,13},{9,12},{12,9},{13,8},{2,7},{3,6},{6... | collective-permute-start | bytes 76808 | tf_op jit(solution)/shard_map/ppermute | solution.py:508
  19.3 1.2 %collective-permute-start.5 = (f32[50,128]{1,0:T(8,128)S(1)}, f32[50,128]{1,0:T(8,128)S(1)}, u32[]{:S(2)}, u32[]{:S(2)}) collective-permute-start(f32[50,128]{1,0:T(8,128)S(1)} %get-tuple-element.41), channel_id=1, source_target_pairs={{0,4},{1,5},{4,0},{5,1},{8,12},{9,13},{12,8},{13,9},{2,6},{3,7},{6... | collective-permute-start | bytes 76808 | tf_op jit(solution)/shard_map/ppermute | solution.py:508
  20.5 0.0 collective-permute-start.6
  20.5 1.1 %tables.1 = (bf16[21,256,256]{2,1,0:T(8,128)(2,1)S(1)}, f32[21,128]{1,0:T(8,128)S(1)}, f32[21,128]{1,0:T(8,128)S(1)}, f32[84,128]{1,0:T(8,128)S(1)}, f32[54,256]{1,0:T(8,128)S(1)}) custom-call(s32[16]{0:T(128)} %lengths_held.7, bf16[4,256,256]{2,1,0:T(8,128)(2,1)S(1)} %get-tuple-element.44.basis, f32[4,24,128]{2,1,0:T(8,128)S(1)} %get-tuple-element.45.cosines.after, ...), custom_call_target="tpu_custom_call" | custom-call | tf_op jit(solution)/shard_map/tables/pallas_call | solution.py:491
  21.6 0.4 %collective-permute-done.7.far = f32[150,128]{1,0:T(8,128)S(1)} collective-permute-done((f32[150,128]{1,0:T(8,128)S(1)}, f32[150,128]{1,0:T(8,128)S(1)}, u32[]{:S(2)}, u32[]{:S(2)}) %collective-permute-start.7) | collective-permute-done | bytes 76832 | tf_op jit(solution)/shard_map/ppermute | solution.py:508
  22.1 0.9 %spectrum.1.refs_10_ = f32[2,50,2,8,64]{4,3,2,1,0:T(8,128)S(1)} custom-call(s32[16,128]{1,0:T(8,128)S(1)} %get-tuple-element.31.held.held_rows, f32[50,128]{1,0:T(8,128)S(1)} %get-tuple-element.30.after.rates, f32[200,128]{1,0:T(8,128)S(1)} %get-tuple-element.54.rows, f32[150,128]{1,0:T(8,128)S(1)} %collective-permute-done.7.far, ...), custom_call_target="tpu_custom_call" | custom-call | tf_op jit(solution)/shard_map/spectrum/pallas_call | solution.py:883
  23.0 0.0 collective-permute-done.4.refs_1_
  23.0 0.3 %collective-permute-done.5.refs_2_ = f32[50,128]{1,0:T(8,128)S(1)} collective-permute-done((f32[50,128]{1,0:T(8,128)S(1)}, f32[50,128]{1,0:T(8,128)S(1)}, u32[]{:S(2)}, u32[]{:S(2)}) %collective-permute-start.5) | collective-permute-done | bytes 25632 | tf_op jit(solution)/shard_map/ppermute | solution.py:508
  23.3 0.0 collective-permute-done.6.refs_3_
  23.3 1.7 %restore.1 = (f32[50,4608]{1,0:T(8,128)}, f32[2,50,2,8,64]{4,3,2,1,0:T(8,128)}) custom-call(f32[50,128]{1,0:T(8,128)S(1)} %get-tuple-element.39.refs_0_, f32[50,128]{1,0:T(8,128)S(1)} %collective-permute-done.4.refs_1_, f32[50,128]{1,0:T(8,128)S(1)} %collective-permute-done.5.refs_2_, f32[50,128]{1,0:T(8,128)S(1)} %collective-permute-done.6.refs_3_, ...), custom_call_target="tpu_custom_call" | custom-call | tf_op jit(solution)/shard_map/restore/pallas_call | solution.py:385
  (1 shorter events, 0.0 us)
Async XLA Ops:
  3.6 5.2 %collective-permute-start = (f32[100,128]{1,0:T(8,128)S(1)}, f32[100,128]{1,0:T(8,128)S(1)}, u32[]{:S(2)}, u32[]{:S(2)}) collective-permute-start(f32[100,128]{1,0:T(8,128)S(1)} %get-tuple-element.34), channel_id=1, source_target_pairs={{0,4},{1,5},{4,0},{5,1},{8,12},{9,13},{12,8},{13,9},{2,6},{3,7},{6... | collective-permute-start | bytes 153608 | tf_op jit(solution)/shard_map/ppermute | solution.py:508
  6.7 3.9 %collective-permute-start.1 = (f32[100,128]{1,0:T(8,128)S(1)}, f32[100,128]{1,0:T(8,128)S(1)}, u32[]{:S(2)}, u32[]{:S(2)}) collective-permute-start(f32[100,128]{1,0:T(8,128)S(1)} %get-tuple-element.35), channel_id=1, source_target_pairs={{0,5},{1,4},{4,1},{5,0},{8,13},{9,12},{12,9},{13,8},{2,7},{3,6},{6... | collective-permute-start | bytes 153608 | tf_op jit(solution)/shard_map/ppermute | solution.py:508
  6.7 3.9 %collective-permute-start.2 = (f32[100,128]{1,0:T(8,128)S(1)}, f32[100,128]{1,0:T(8,128)S(1)}, u32[]{:S(2)}, u32[]{:S(2)}) collective-permute-start(f32[100,128]{1,0:T(8,128)S(1)} %get-tuple-element.36), channel_id=1, source_target_pairs={{0,1},{1,0},{4,5},{5,4},{8,9},{9,8},{12,13},{13,12},{2,3},{3,2},{6... | collective-permute-start | bytes 153608 | tf_op jit(solution)/shard_map/ppermute | solution.py:508
  11.1 6.7 %collective-permute-start.3 = (f32[150,128]{1,0:T(8,128)S(1)}, f32[150,128]{1,0:T(8,128)S(1)}, u32[]{:S(2)}, u32[]{:S(2)}) collective-permute-start(f32[150,128]{1,0:T(8,128)S(1)} %get-tuple-element.38), channel_id=1, source_target_pairs={{0,8},{1,9},{4,12},{5,13},{8,0},{9,1},{12,4},{13,5},{2,10},{3,11},... | collective-permute-start | bytes 230408 | tf_op jit(solution)/shard_map/ppermute | solution.py:508
  15.5 6.6 %collective-permute-start.7 = (f32[150,128]{1,0:T(8,128)S(1)}, f32[150,128]{1,0:T(8,128)S(1)}, u32[]{:S(2)}, u32[]{:S(2)}) collective-permute-start(f32[150,128]{1,0:T(8,128)S(1)} %get-tuple-element.55), channel_id=1, source_target_pairs={{0,8},{1,9},{4,12},{5,13},{8,0},{9,1},{12,4},{13,5},{2,10},{3,11},... | collective-permute-start | bytes 230408 | tf_op jit(solution)/shard_map/ppermute | solution.py:508
  17.8 5.1 %collective-permute-start.4 = (f32[50,128]{1,0:T(8,128)S(1)}, f32[50,128]{1,0:T(8,128)S(1)}, u32[]{:S(2)}, u32[]{:S(2)}) collective-permute-start(f32[50,128]{1,0:T(8,128)S(1)} %get-tuple-element.40), channel_id=1, source_target_pairs={{0,5},{1,4},{4,1},{5,0},{8,13},{9,12},{12,9},{13,8},{2,7},{3,6},{6... | collective-permute-start | bytes 76808 | tf_op jit(solution)/shard_map/ppermute | solution.py:508
  19.3 4.0 %collective-permute-start.5 = (f32[50,128]{1,0:T(8,128)S(1)}, f32[50,128]{1,0:T(8,128)S(1)}, u32[]{:S(2)}, u32[]{:S(2)}) collective-permute-start(f32[50,128]{1,0:T(8,128)S(1)} %get-tuple-element.41), channel_id=1, source_target_pairs={{0,4},{1,5},{4,0},{5,1},{8,12},{9,13},{12,8},{13,9},{2,6},{3,7},{6... | collective-permute-start | bytes 76808 | tf_op jit(solution)/shard_map/ppermute | solution.py:508
  20.5 2.8 %collective-permute-start.6 = (f32[50,128]{1,0:T(8,128)S(1)}, f32[50,128]{1,0:T(8,128)S(1)}, u32[]{:S(2)}, u32[]{:S(2)}) collective-permute-start(f32[50,128]{1,0:T(8,128)S(1)} %get-tuple-element.42), channel_id=1, source_target_pairs={{0,1},{1,0},{4,5},{5,4},{8,9},{9,8},{12,13},{13,12},{2,3},{3,2},{6... | collective-permute-start | bytes 76808 | tf_op jit(solution)/shard_map/ppermute | solution.py:508

commit v8 on v7

--- a/solution.py
+++ b/solution.py
@@ -806,7 +806,7 @@
     )(held, mine, factors, after, *messages)
 
 
-def hand_out_kernel(held, own, other, *outs):
+def hand_out_kernel(held, own, other, after, *outs):
     channels = outs[0].shape[0]
     begin = held[pl.ds(2 * SHARES, 1), :]
     sums = []
@@ -821,16 +821,16 @@
         out[...] = value
 
 
-def hand_out(held, own, other):
+def hand_out(held, own, other, after):
     channels = own.shape[0] // WINDOW
     return pl.pallas_call(
         hand_out_kernel,
         out_shape=[floats(channels, LANES)] * SHARES,
-        in_specs=[VMEM] * 3,
+        in_specs=[VMEM] * 3 + [pl.BlockSpec(memory_space=pl.ANY)],
         out_specs=[VMEM] * SHARES,
         compiler_params=pltpu.CompilerParams(vmem_limit_bytes=SMALL),
         name="hand_out",
-    )(held, own, other)
+    )(held, own, other, after)
 
 
 def spectrum_kernel(held_rows, rates, rows, far, poly, gram, out):
@@ -899,7 +899,7 @@
     rows, sent_rows, poly, gram = pack(held, mine, factors, waves[1], received)
     tables = tables_of(lengths, waves, local)
     far = swapped(sent_rows, SHARES)
-    replies = hand_out(held, part, other_part)
+    replies = hand_out(held, part, other_part, tables[1])
     return replies, tables, (held, rates, rows, far, poly, gram)
 
 

time: 25.2 us -> 25.1 us (level); the launches traced: 25 us -> 24.6 us
  waiting for transfers between devices: 5.02 us -> 4.75 us
    ppermute x8, waiting for transfers between devices: 5.02 us -> 4.75 us  [swapped(): return lax.ppermute(value, AXES, [(i, i ^ mask) for i in range(count)])]
  transfers between devices with their start and end apart: 8 -> 8, of which waited for: 5 -> 4; matrix products, arithmetic and copies ran while one was open for 0% -> 0% of each run, Pallas kernels for 20% -> 21%
where the time goes in v8:
time: 25.1 us; the launch traced here: 24.6 us
  Pallas kernels  10.2 us (41%)
  starting transfers between devices  8.96 us (36%)
  waiting for transfers between devices  4.75 us (19%)
  between operations  0.72 us (3%)
    ppermute x8, starting transfers between devices, swapped(): return lax.ppermute(value, AXES, [(i, i ^ mask) for i in range(count)])  8.96 us
    ppermute x8, waiting for transfers between devices, swapped(): return lax.ppermute(value, AXES, [(i, i ^ mask) for i in range(count)])  4.75 us
    pallas_call x1, Pallas kernels, analyse(): pl.pallas_call(functools.partial(analyse_kernel, per_device), out_shape=[...  2.92 us
    pallas_call x1, Pallas kernels, restore(): pl.pallas_call(restore_kernel, out_shape=[jax.ShapeDtypeStruct((channels,...  1.66 us
    pallas_call x1, Pallas kernels, waves_of(): pl.pallas_call(functools.partial(waves_kernel, per_device, local), out_sh...  1.43 us
    pallas_call x1, Pallas kernels, prepare(): pl.pallas_call(functools.partial(prepare_kernel, count, local), out_shape...  1.35 us
    pallas_call x1, Pallas kernels, tables_of(): pl.pallas_call(functools.partial(tables_kernel, local), out_shape=shapes,...  1.1 us
    pallas_call x1, Pallas kernels, spectrum(): pl.pallas_call(spectrum_kernel, out_shape=pltpu.VMEM((2, channels, 2, 8,...  0.9 us
  transfers between devices with their start and end apart: 8, of which 4 were waited for; matrix products, arithmetic and copies ran while one was open for 0% of the time, Pallas kernels for 21%

profile of v8, /device:TPU:0, one launch (start us, length us, event | category | flops | bytes accessed | tf_op | source)
XLA Modules:
  0.0 24.6 jit_solution(402926599665035535)
XLA Ops:
  0.6 2.9 %analyse.1 = (f32[100,128]{1,0:T(8,128)S(1)}, f32[100,128]{1,0:T(8,128)S(1)}, f32[100,128]{1,0:T(8,128)S(1)}, f32[100,128]{1,0:T(8,128)S(1)}, f32[50,128]{1,0:T(8,128)S(1)}, /*index=5*/f32[50,4608]{1,0:T(8,128)S(1)}) custom-call(s32[16]{0:T(128)} %lengths_held.7, f32[2,50]{1,0:T(2,128)} %strength_held.1, f32[50,4608]{1,0:T(8,128)} %second.1, f32[50,4608]{1,0:T(8,128)} %first.1), custom_call_target="tpu_custom_call" | custom-call | tf_op jit(solution)/shard_map/analyse/pallas_call | solution.py:300
  3.6 3.1 %collective-permute-start = (f32[100,128]{1,0:T(8,128)S(1)}, f32[100,128]{1,0:T(8,128)S(1)}, u32[]{:S(2)}, u32[]{:S(2)}) collective-permute-start(f32[100,128]{1,0:T(8,128)S(1)} %get-tuple-element.34), channel_id=1, source_target_pairs={{0,4},{1,5},{4,0},{5,1},{8,12},{9,13},{12,8},{13,9},{2,6},{3,7},{6... | collective-permute-start | bytes 153608 | tf_op jit(solution)/shard_map/ppermute | solution.py:508
  6.7 0.0 collective-permute-start.1
  6.7 0.2 collective-permute-start.2
  6.9 1.3 %prepare.1 = (f32[2,4,16,128]{3,2,1,0:T(8,128)S(1)}, f32[64,128]{1,0:T(8,128)S(1)}, f32[8,128]{1,0:T(8,128)S(1)}, s32[16,128]{1,0:T(8,128)S(1)}) custom-call(s32[16]{0:T(128)} %lengths_held.7, f32[16]{0:T(128)} %latitude_held.1, f32[16]{0:T(128)} %weights_held.1, f32[50,128]{1,0:T(8,128)S(1)} %get-tuple-element.30.after.rates), custom_call_target="tpu_custom_call" | custom-call | tf_op jit(solution)/shard_map/prepare/pallas_call | solution.py:716
  8.2 0.6 %collective-permute-done.refs_1_ = f32[100,128]{1,0:T(8,128)S(1)} collective-permute-done((f32[100,128]{1,0:T(8,128)S(1)}, f32[100,128]{1,0:T(8,128)S(1)}, u32[]{:S(2)}, u32[]{:S(2)}) %collective-permute-start) | collective-permute-done | bytes 51232 | tf_op jit(solution)/shard_map/ppermute | solution.py:508
  8.8 1.8 %collective-permute-done.1.refs_2_ = f32[100,128]{1,0:T(8,128)S(1)} collective-permute-done((f32[100,128]{1,0:T(8,128)S(1)}, f32[100,128]{1,0:T(8,128)S(1)}, u32[]{:S(2)}, u32[]{:S(2)}) %collective-permute-start.1) | collective-permute-done | bytes 51232 | tf_op jit(solution)/shard_map/ppermute | solution.py:508
  10.5 0.0 collective-permute-done.2.refs_3_
  10.5 0.5 %couple.1 = (f32[150,128]{1,0:T(8,128)S(1)}, f32[150,128]{1,0:T(8,128)S(1)}) custom-call(s32[16,128]{1,0:T(8,128)S(1)} %get-tuple-element.31.held.held_rows, f32[50,128]{1,0:T(8,128)S(1)} %get-tuple-element.30.after.rates, f32[2,4,16,128]{3,2,1,0:T(8,128)S(1)} %get-tuple-element.32.coupling, f32[100,128]{1,0:T(8,128)S(1)} %get-tuple-element.33.refs_0_, ...), custom_call_target="tpu_custom_call" | custom-call | tf_op jit(solution)/shard_map/couple/pallas_call | solution.py:773
  11.1 2.7 %collective-permute-start.3 = (f32[150,128]{1,0:T(8,128)S(1)}, f32[150,128]{1,0:T(8,128)S(1)}, u32[]{:S(2)}, u32[]{:S(2)}) collective-permute-start(f32[150,128]{1,0:T(8,128)S(1)} %get-tuple-element.38), channel_id=1, source_target_pairs={{0,8},{1,9},{4,12},{5,13},{8,0},{9,1},{12,4},{13,5},{2,10},{3,11},... | collective-permute-start | bytes 230408 | tf_op jit(solution)/shard_map/ppermute | solution.py:508
  13.7 1.4 %waves.1 = (bf16[4,256,256]{2,1,0:T(8,128)(2,1)S(1)}, f32[4,24,128]{2,1,0:T(8,128)S(1)}, f32[4,24,128]{2,1,0:T(8,128)S(1)}) custom-call(s32[16]{0:T(128)} %lengths_held.7, f32[150,128]{1,0:T(8,128)S(1)} %get-tuple-element.37.after.own), custom_call_target="tpu_custom_call" | custom-call | tf_op jit(solution)/shard_map/waves/pallas_call | solution.py:425
  15.2 0.3 %pack.1 = (f32[200,128]{1,0:T(8,128)S(1)}, f32[150,128]{1,0:T(8,128)S(1)}, bf16[384,128]{1,0:T(8,128)(2,1)S(1)}, bf16[384,128]{1,0:T(8,128)(2,1)S(1)}) custom-call(s32[16,128]{1,0:T(8,128)S(1)} %get-tuple-element.31.held.held_rows, f32[64,128]{1,0:T(8,128)S(1)} %get-tuple-element.52.mine, f32[8,128]{1,0:T(8,128)S(1)} %get-tuple-element.53.factors, ...), custom_call_target="tpu_custom_call" | custom-call | tf_op jit(solution)/shard_map/pack/pallas_call | solution.py:798
  15.5 0.4 %collective-permute-start.7 = (f32[150,128]{1,0:T(8,128)S(1)}, f32[150,128]{1,0:T(8,128)S(1)}, u32[]{:S(2)}, u32[]{:S(2)}) collective-permute-start(f32[150,128]{1,0:T(8,128)S(1)} %get-tuple-element.55), channel_id=1, source_target_pairs={{0,8},{1,9},{4,12},{5,13},{8,0},{9,1},{12,4},{13,5},{2,10},{3,11},... | collective-permute-start | bytes 230408 | tf_op jit(solution)/shard_map/ppermute | solution.py:508
  15.9 1.1 %tables.1 = (bf16[21,256,256]{2,1,0:T(8,128)(2,1)S(1)}, f32[21,128]{1,0:T(8,128)S(1)}, f32[21,128]{1,0:T(8,128)S(1)}, f32[84,128]{1,0:T(8,128)S(1)}, f32[54,256]{1,0:T(8,128)S(1)}) custom-call(s32[16]{0:T(128)} %lengths_held.7, bf16[4,256,256]{2,1,0:T(8,128)(2,1)S(1)} %get-tuple-element.39.basis, f32[4,24,128]{2,1,0:T(8,128)S(1)} %get-tuple-element.40.cosines.after, ...), custom_call_target="tpu_custom_call" | custom-call | tf_op jit(solution)/shard_map/tables/pallas_call | solution.py:491
  17.0 0.9 %collective-permute-done.3.other = f32[150,128]{1,0:T(8,128)S(1)} collective-permute-done((f32[150,128]{1,0:T(8,128)S(1)}, f32[150,128]{1,0:T(8,128)S(1)}, u32[]{:S(2)}, u32[]{:S(2)}) %collective-permute-start.3) | collective-permute-done | bytes 76832 | tf_op jit(solution)/shard_map/ppermute | solution.py:508
  17.9 0.6 %collective-permute-start.4 = (f32[50,128]{1,0:T(8,128)S(1)}, f32[50,128]{1,0:T(8,128)S(1)}, u32[]{:S(2)}, u32[]{:S(2)}) collective-permute-start(f32[50,128]{1,0:T(8,128)S(1)} %get-tuple-element.44), channel_id=1, source_target_pairs={{0,5},{1,4},{4,1},{5,0},{8,13},{9,12},{12,9},{13,8},{2,7},{3,6},{6... | collective-permute-start | bytes 76808 | tf_op jit(solution)/shard_map/ppermute | solution.py:508
  18.5 2.0 %collective-permute-start.5 = (f32[50,128]{1,0:T(8,128)S(1)}, f32[50,128]{1,0:T(8,128)S(1)}, u32[]{:S(2)}, u32[]{:S(2)}) collective-permute-start(f32[50,128]{1,0:T(8,128)S(1)} %get-tuple-element.45), channel_id=1, source_target_pairs={{0,4},{1,5},{4,0},{5,1},{8,12},{9,13},{12,8},{13,9},{2,6},{3,7},{6... | collective-permute-start | bytes 76808 | tf_op jit(solution)/shard_map/ppermute | solution.py:508
  20.4 0.0 collective-permute-start.6
  20.5 1.6 %collective-permute-done.7.far = f32[150,128]{1,0:T(8,128)S(1)} collective-permute-done((f32[150,128]{1,0:T(8,128)S(1)}, f32[150,128]{1,0:T(8,128)S(1)}, u32[]{:S(2)}, u32[]{:S(2)}) %collective-permute-start.7) | collective-permute-done | bytes 76832 | tf_op jit(solution)/shard_map/ppermute | solution.py:508
  22.0 0.9 %spectrum.1.refs_10_ = f32[2,50,2,8,64]{4,3,2,1,0:T(8,128)S(1)} custom-call(s32[16,128]{1,0:T(8,128)S(1)} %get-tuple-element.31.held.held_rows, f32[50,128]{1,0:T(8,128)S(1)} %get-tuple-element.30.after.rates, f32[200,128]{1,0:T(8,128)S(1)} %get-tuple-element.54.rows, f32[150,128]{1,0:T(8,128)S(1)} %collective-permute-done.7.far, ...), custom_call_target="tpu_custom_call" | custom-call | tf_op jit(solution)/shard_map/spectrum/pallas_call | solution.py:883
  22.9 0.0 collective-permute-done.4.refs_1_
  22.9 0.0 collective-permute-done.5.refs_2_
  23.0 0.0 collective-permute-done.6.refs_3_
  23.0 1.7 %restore.1 = (f32[50,4608]{1,0:T(8,128)}, f32[2,50,2,8,64]{4,3,2,1,0:T(8,128)}) custom-call(f32[50,128]{1,0:T(8,128)S(1)} %get-tuple-element.43.refs_0_, f32[50,128]{1,0:T(8,128)S(1)} %collective-permute-done.4.refs_1_, f32[50,128]{1,0:T(8,128)S(1)} %collective-permute-done.5.refs_2_, f32[50,128]{1,0:T(8,128)S(1)} %collective-permute-done.6.refs_3_, ...), custom_call_target="tpu_custom_call" | custom-call | tf_op jit(solution)/shard_map/restore/pallas_call | solution.py:385
  (1 shorter events, 0.0 us)
Async XLA Ops:
  3.6 5.2 %collective-permute-start = (f32[100,128]{1,0:T(8,128)S(1)}, f32[100,128]{1,0:T(8,128)S(1)}, u32[]{:S(2)}, u32[]{:S(2)}) collective-permute-start(f32[100,128]{1,0:T(8,128)S(1)} %get-tuple-element.34), channel_id=1, source_target_pairs={{0,4},{1,5},{4,0},{5,1},{8,12},{9,13},{12,8},{13,9},{2,6},{3,7},{6... | collective-permute-start | bytes 153608 | tf_op jit(solution)/shard_map/ppermute | solution.py:508
  6.7 3.9 %collective-permute-start.1 = (f32[100,128]{1,0:T(8,128)S(1)}, f32[100,128]{1,0:T(8,128)S(1)}, u32[]{:S(2)}, u32[]{:S(2)}) collective-permute-start(f32[100,128]{1,0:T(8,128)S(1)} %get-tuple-element.35), channel_id=1, source_target_pairs={{0,5},{1,4},{4,1},{5,0},{8,13},{9,12},{12,9},{13,8},{2,7},{3,6},{6... | collective-permute-start | bytes 153608 | tf_op jit(solution)/shard_map/ppermute | solution.py:508
  6.7 3.9 %collective-permute-start.2 = (f32[100,128]{1,0:T(8,128)S(1)}, f32[100,128]{1,0:T(8,128)S(1)}, u32[]{:S(2)}, u32[]{:S(2)}) collective-permute-start(f32[100,128]{1,0:T(8,128)S(1)} %get-tuple-element.36), channel_id=1, source_target_pairs={{0,1},{1,0},{4,5},{5,4},{8,9},{9,8},{12,13},{13,12},{2,3},{3,2},{6... | collective-permute-start | bytes 153608 | tf_op jit(solution)/shard_map/ppermute | solution.py:508
  11.1 6.7 %collective-permute-start.3 = (f32[150,128]{1,0:T(8,128)S(1)}, f32[150,128]{1,0:T(8,128)S(1)}, u32[]{:S(2)}, u32[]{:S(2)}) collective-permute-start(f32[150,128]{1,0:T(8,128)S(1)} %get-tuple-element.38), channel_id=1, source_target_pairs={{0,8},{1,9},{4,12},{5,13},{8,0},{9,1},{12,4},{13,5},{2,10},{3,11},... | collective-permute-start | bytes 230408 | tf_op jit(solution)/shard_map/ppermute | solution.py:508
  15.5 6.6 %collective-permute-start.7 = (f32[150,128]{1,0:T(8,128)S(1)}, f32[150,128]{1,0:T(8,128)S(1)}, u32[]{:S(2)}, u32[]{:S(2)}) collective-permute-start(f32[150,128]{1,0:T(8,128)S(1)} %get-tuple-element.55), channel_id=1, source_target_pairs={{0,8},{1,9},{4,12},{5,13},{8,0},{9,1},{12,4},{13,5},{2,10},{3,11},... | collective-permute-start | bytes 230408 | tf_op jit(solution)/shard_map/ppermute | solution.py:508
  17.9 5.1 %collective-permute-start.4 = (f32[50,128]{1,0:T(8,128)S(1)}, f32[50,128]{1,0:T(8,128)S(1)}, u32[]{:S(2)}, u32[]{:S(2)}) collective-permute-start(f32[50,128]{1,0:T(8,128)S(1)} %get-tuple-element.44), channel_id=1, source_target_pairs={{0,5},{1,4},{4,1},{5,0},{8,13},{9,12},{12,9},{13,8},{2,7},{3,6},{6... | collective-permute-start | bytes 76808 | tf_op jit(solution)/shard_map/ppermute | solution.py:508
  18.5 4.5 %collective-permute-start.5 = (f32[50,128]{1,0:T(8,128)S(1)}, f32[50,128]{1,0:T(8,128)S(1)}, u32[]{:S(2)}, u32[]{:S(2)}) collective-permute-start(f32[50,128]{1,0:T(8,128)S(1)} %get-tuple-element.45), channel_id=1, source_target_pairs={{0,4},{1,5},{4,0},{5,1},{8,12},{9,13},{12,8},{13,9},{2,6},{3,7},{6... | collective-permute-start | bytes 76808 | tf_op jit(solution)/shard_map/ppermute | solution.py:508
  20.4 2.5 %collective-permute-start.6 = (f32[50,128]{1,0:T(8,128)S(1)}, f32[50,128]{1,0:T(8,128)S(1)}, u32[]{:S(2)}, u32[]{:S(2)}) collective-permute-start(f32[50,128]{1,0:T(8,128)S(1)} %get-tuple-element.46), channel_id=1, source_target_pairs={{0,1},{1,0},{4,5},{5,4},{8,9},{9,8},{12,13},{13,12},{2,3},{3,2},{6... | collective-permute-start | bytes 76808 | tf_op jit(solution)/shard_map/ppermute | solution.py:508

commit v9 on v8

--- a/solution.py
+++ b/solution.py
@@ -745,11 +745,19 @@
         out[pl.ds(index * channels, channels), :] = value
 
 
-def couple_kernel(held, rates, coupling, *refs):
-    messages, (own, other) = [ref[...] for ref in refs[:SHARES]], refs[SHARES:]
+def couple_kernel(half, held, rates, coupling, *refs):
+    messages, out = [ref[...] for ref in refs[:SHARES]], refs[-1]
     channels = rates.shape[0]
     arrays = by_row(messages, [held[pl.ds(index, 1), :] for index in range(SHARES)])
-    sums = [jnp.zeros((channels, LANES), jnp.float32)] * SHARES
+    begin = held[pl.ds(2 * SHARES + half, 1), :]
+
+    def factor(which, place, at):
+        value = jnp.zeros((1, LANES), jnp.float32)
+        for target in range(SHARES):
+            value = jnp.where(begin + place == target, coupling[which, target, at, :], value)
+        return value
+
+    sums = [jnp.zeros((channels, LANES), jnp.float32)] * WINDOW
     for source in range(SHARES):
         both = arrays[source][:channels]
         second = rates[...] * arrays[source][channels:]
@@ -757,27 +765,26 @@
             moved_both = group_roll(both, step)
             moved_second = group_roll(second, step)
             at = pl.ds(step * SHARES + source, 1)
-            for target in range(SHARES):
-                sums[target] = (
-                    sums[target]
-                    + coupling[0, target, at, :] * moved_both
-                    - coupling[1, target, at, :] * moved_second
+            for place in range(WINDOW):
+                sums[place] = (
+                    sums[place]
+                    + factor(0, place, at) * moved_both
+                    - factor(1, place, at) * moved_second
                 )
-    for half, out in enumerate((own, other)):
-        begin = held[pl.ds(2 * SHARES + half, 1), :]
-        fill_window(begin, sums, out)
-
-
-def couple(held, rates, coupling, messages):
+    for place in range(WINDOW):
+        out[pl.ds(place * channels, channels), :] = sums[place]
+
+
+def couple(half, held, rates, coupling, messages, after=()):
     channels = rates.shape[0]
     return pl.pallas_call(
-        couple_kernel,
-        out_shape=[floats(WINDOW * channels, LANES)] * 2,
-        in_specs=[VMEM] * (3 + SHARES),
-        out_specs=[VMEM] * 2,
+        functools.partial(couple_kernel, half),
+        out_shape=floats(WINDOW * channels, LANES),
+        in_specs=[VMEM] * (3 + SHARES) + [pl.BlockSpec(memory_space=pl.ANY)] * len(after),
+        out_specs=VMEM,
         compiler_params=pltpu.CompilerParams(vmem_limit_bytes=SMALL),
-        name="couple",
-    )(held, rates, coupling, *messages)
+        name=("couple", "couple_across")[half],
+    )(held, rates, coupling, *messages, *after)
 
 
 def pack_kernel(held, mine, factors, after, *refs):
@@ -893,12 +900,13 @@
 def middle_small(messages, rates, lengths, latitude, weights, local, per_device, count):
     coupling, mine, factors, held = prepare(lengths, latitude, weights, rates, count, local)
     received = exchanged(messages, ORDER)
-    part, sent_part = couple(held, rates, coupling, received)
+    sent_part = couple(1, held, rates, coupling, received)
     other_part = swapped(sent_part, SHARES)
-    waves = waves_of(lengths, part, local, per_device)
+    waves = waves_of(lengths, sent_part, local, per_device)
     rows, sent_rows, poly, gram = pack(held, mine, factors, waves[1], received)
     tables = tables_of(lengths, waves, local)
     far = swapped(sent_rows, SHARES)
+    part = couple(0, held, rates, coupling, received, (sent_rows,))
     replies = hand_out(held, part, other_part, tables[1])
     return replies, tables, (held, rates, rows, far, poly, gram)
 

time: 25.1 us -> 25.1 us (level)
  the two profiles are of different devices: /device:TPU:0 before, /device:TPU:19 now
where the time goes in v9:
time: 25.1 us; the launch traced here: 24.9 us
  Pallas kernels  10.7 us (43%)
  starting transfers between devices  9.8 us (39%)
  waiting for transfers between devices  3.68 us (15%)
  between operations  0.72 us (3%)
    ppermute x8, starting transfers between devices, swapped(): return lax.ppermute(value, AXES, [(i, i ^ mask) for i in range(count)])  9.8 us
    ppermute x8, waiting for transfers between devices, swapped(): return lax.ppermute(value, AXES, [(i, i ^ mask) for i in range(count)])  3.68 us
    pallas_call x1, Pallas kernels, analyse(): pl.pallas_call(functools.partial(analyse_kernel, per_device), out_shape=[...  2.93 us
    pallas_call x1, Pallas kernels, restore(): pl.pallas_call(restore_kernel, out_shape=[jax.ShapeDtypeStruct((channels,...  1.66 us
    pallas_call x1, Pallas kernels, waves_of(): pl.pallas_call(functools.partial(waves_kernel, per_device, local), out_sh...  1.43 us
    pallas_call x1, Pallas kernels, prepare(): pl.pallas_call(functools.partial(prepare_kernel, count, local), out_shape...  1.35 us
    pallas_call x1, Pallas kernels, tables_of(): pl.pallas_call(functools.partial(tables_kernel, local), out_shape=shapes,...  1.1 us
    pallas_call x2, Pallas kernels, couple(): pl.pallas_call(functools.partial(couple_kernel, half), out_shape=floats(W...  1 us
  transfers between devices with their start and end apart: 8, of which 3 were waited for; matrix products, arithmetic and copies ran while one was open for 0% of the time, Pallas kernels for 22%

profile of v9, /device:TPU:19, one launch (start us, length us, event | category | flops | bytes accessed | tf_op | source)
XLA Modules:
  0.0 24.9 jit_solution(15291443365502620927)
XLA Ops:
  0.6 2.9 %analyse.1 = (f32[100,128]{1,0:T(8,128)S(1)}, f32[100,128]{1,0:T(8,128)S(1)}, f32[100,128]{1,0:T(8,128)S(1)}, f32[100,128]{1,0:T(8,128)S(1)}, f32[50,128]{1,0:T(8,128)S(1)}, /*index=5*/f32[50,4608]{1,0:T(8,128)S(1)}) custom-call(s32[16]{0:T(128)} %lengths_held.7, f32[2,50]{1,0:T(2,128)} %strength_held.1, f32[50,4608]{1,0:T(8,128)} %second.1, f32[50,4608]{1,0:T(8,128)} %first.1), custom_call_target="tpu_custom_call" | custom-call | tf_op jit(solution)/shard_map/analyse/pallas_call | solution.py:300
  3.6 1.4 %collective-permute-start = (f32[100,128]{1,0:T(8,128)S(1)}, f32[100,128]{1,0:T(8,128)S(1)}, u32[]{:S(2)}, u32[]{:S(2)}) collective-permute-start(f32[100,128]{1,0:T(8,128)S(1)} %get-tuple-element.32), channel_id=1, source_target_pairs={{0,4},{1,5},{4,0},{5,1},{8,12},{9,13},{12,8},{13,9},{2,6},{3,7},{6... | collective-permute-start | bytes 153608 | tf_op jit(solution)/shard_map/ppermute | solution.py:508
  4.9 1.0 %collective-permute-start.1 = (f32[100,128]{1,0:T(8,128)S(1)}, f32[100,128]{1,0:T(8,128)S(1)}, u32[]{:S(2)}, u32[]{:S(2)}) collective-permute-start(f32[100,128]{1,0:T(8,128)S(1)} %get-tuple-element.33), channel_id=1, source_target_pairs={{0,5},{1,4},{4,1},{5,0},{8,13},{9,12},{12,9},{13,8},{2,7},{3,6},{6... | collective-permute-start | bytes 153608 | tf_op jit(solution)/shard_map/ppermute | solution.py:508
  5.9 0.0 collective-permute-start.2
  5.9 1.3 %prepare.1 = (f32[2,4,16,128]{3,2,1,0:T(8,128)S(1)}, f32[64,128]{1,0:T(8,128)S(1)}, f32[8,128]{1,0:T(8,128)S(1)}, s32[16,128]{1,0:T(8,128)S(1)}) custom-call(s32[16]{0:T(128)} %lengths_held.7, f32[16]{0:T(128)} %latitude_held.1, f32[16]{0:T(128)} %weights_held.1, f32[50,128]{1,0:T(8,128)S(1)} %get-tuple-element.28.after.rates), custom_call_target="tpu_custom_call" | custom-call | tf_op jit(solution)/shard_map/prepare/pallas_call | solution.py:716
  7.3 0.0 collective-permute-done.refs_1_
  7.3 1.8 %collective-permute-done.1.refs_2_ = f32[100,128]{1,0:T(8,128)S(1)} collective-permute-done((f32[100,128]{1,0:T(8,128)S(1)}, f32[100,128]{1,0:T(8,128)S(1)}, u32[]{:S(2)}, u32[]{:S(2)}) %collective-permute-start.1) | collective-permute-done | bytes 51232 | tf_op jit(solution)/shard_map/ppermute | solution.py:508
  9.1 0.0 collective-permute-done.2.refs_3_
  9.1 0.5 %couple_across.1.after = f32[150,128]{1,0:T(8,128)S(1)} custom-call(s32[16,128]{1,0:T(8,128)S(1)} %get-tuple-element.29.held.held_rows, f32[50,128]{1,0:T(8,128)S(1)} %get-tuple-element.28.after.rates, f32[2,4,16,128]{3,2,1,0:T(8,128)S(1)} %get-tuple-element.30.coupling, f32[100,128]{1,0:T(8,128)S(1)} %get-tuple-element.31.refs_0_, ...), custom_call_target="tpu_custom_call" | custom-call | tf_op jit(solution)/shard_map/couple_across/pallas_call | solution.py:780
  9.6 0.1 collective-permute-start.3
  9.7 1.4 %waves.1 = (bf16[4,256,256]{2,1,0:T(8,128)(2,1)S(1)}, f32[4,24,128]{2,1,0:T(8,128)S(1)}, f32[4,24,128]{2,1,0:T(8,128)S(1)}) custom-call(s32[16]{0:T(128)} %lengths_held.7, f32[150,128]{1,0:T(8,128)S(1)} %couple_across.1.after), custom_call_target="tpu_custom_call" | custom-call | tf_op jit(solution)/shard_map/waves/pallas_call | solution.py:425
  11.2 0.3 %pack.1 = (f32[200,128]{1,0:T(8,128)S(1)}, f32[150,128]{1,0:T(8,128)S(1)}, bf16[384,128]{1,0:T(8,128)(2,1)S(1)}, bf16[384,128]{1,0:T(8,128)(2,1)S(1)}) custom-call(s32[16,128]{1,0:T(8,128)S(1)} %get-tuple-element.29.held.held_rows, f32[64,128]{1,0:T(8,128)S(1)} %get-tuple-element.35.mine, f32[8,128]{1,0:T(8,128)S(1)} %get-tuple-element.36.factors, ...), custom_call_target="tpu_custom_call" | custom-call | tf_op jit(solution)/shard_map/pack/pallas_call | solution.py:805
  11.5 2.4 %collective-permute-start.7 = (f32[150,128]{1,0:T(8,128)S(1)}, f32[150,128]{1,0:T(8,128)S(1)}, u32[]{:S(2)}, u32[]{:S(2)}) collective-permute-start(f32[150,128]{1,0:T(8,128)S(1)} %get-tuple-element.38.refs_4_), channel_id=1, source_target_pairs={{0,8},{1,9},{4,12},{5,13},{8,0},{9,1},{12,4},{13,5},{2,10},{3,11},... | collective-permute-start | bytes 230408 | tf_op jit(solution)/shard_map/ppermute | solution.py:508
  13.8 1.1 %tables.1 = (bf16[21,256,256]{2,1,0:T(8,128)(2,1)S(1)}, f32[21,128]{1,0:T(8,128)S(1)}, f32[21,128]{1,0:T(8,128)S(1)}, f32[84,128]{1,0:T(8,128)S(1)}, f32[54,256]{1,0:T(8,128)S(1)}) custom-call(s32[16]{0:T(128)} %lengths_held.7, bf16[4,256,256]{2,1,0:T(8,128)(2,1)S(1)} %get-tuple-element.39.basis, f32[4,24,128]{2,1,0:T(8,128)S(1)} %get-tuple-element.37.after.cosines, ...), custom_call_target="tpu_custom_call" | custom-call | tf_op jit(solution)/shard_map/tables/pallas_call | solution.py:491
  14.9 0.5 %couple.1.own = f32[150,128]{1,0:T(8,128)S(1)} custom-call(s32[16,128]{1,0:T(8,128)S(1)} %get-tuple-element.29.held.held_rows, f32[50,128]{1,0:T(8,128)S(1)} %get-tuple-element.28.after.rates, f32[2,4,16,128]{3,2,1,0:T(8,128)S(1)} %get-tuple-element.30.coupling, f32[100,128]{1,0:T(8,128)S(1)} %get-tuple-element.31.refs_0_, ...), custom_call_target="tpu_custom_call" | custom-call | tf_op jit(solution)/shard_map/couple/pallas_call | solution.py:780
  15.4 0.0 collective-permute-done.3.other
  15.5 4.5 %collective-permute-start.4 = (f32[50,128]{1,0:T(8,128)S(1)}, f32[50,128]{1,0:T(8,128)S(1)}, u32[]{:S(2)}, u32[]{:S(2)}) collective-permute-start(f32[50,128]{1,0:T(8,128)S(1)} %get-tuple-element.43), channel_id=1, source_target_pairs={{0,5},{1,4},{4,1},{5,0},{8,13},{9,12},{12,9},{13,8},{2,7},{3,6},{6... | collective-permute-start | bytes 76808 | tf_op jit(solution)/shard_map/ppermute | solution.py:508
  19.9 0.0 collective-permute-start.5
  19.9 0.5 %collective-permute-start.6 = (f32[50,128]{1,0:T(8,128)S(1)}, f32[50,128]{1,0:T(8,128)S(1)}, u32[]{:S(2)}, u32[]{:S(2)}) collective-permute-start(f32[50,128]{1,0:T(8,128)S(1)} %get-tuple-element.45), channel_id=1, source_target_pairs={{0,1},{1,0},{4,5},{5,4},{8,9},{9,8},{12,13},{13,12},{2,3},{3,2},{6... | collective-permute-start | bytes 76808 | tf_op jit(solution)/shard_map/ppermute | solution.py:508
  20.4 0.0 collective-permute-done.7.far
  20.4 0.9 %spectrum.1.refs_10_ = f32[2,50,2,8,64]{4,3,2,1,0:T(8,128)S(1)} custom-call(s32[16,128]{1,0:T(8,128)S(1)} %get-tuple-element.29.held.held_rows, f32[50,128]{1,0:T(8,128)S(1)} %get-tuple-element.28.after.rates, f32[200,128]{1,0:T(8,128)S(1)} %get-tuple-element.51.rows, f32[150,128]{1,0:T(8,128)S(1)} %collective-permute-done.7.far, ...), custom_call_target="tpu_custom_call" | custom-call | tf_op jit(solution)/shard_map/spectrum/pallas_call | solution.py:890
  21.3 0.2 collective-permute-done.4.refs_1_
  21.5 1.7 %collective-permute-done.5.refs_2_ = f32[50,128]{1,0:T(8,128)S(1)} collective-permute-done((f32[50,128]{1,0:T(8,128)S(1)}, f32[50,128]{1,0:T(8,128)S(1)}, u32[]{:S(2)}, u32[]{:S(2)}) %collective-permute-start.5) | collective-permute-done | bytes 25632 | tf_op jit(solution)/shard_map/ppermute | solution.py:508
  23.2 0.0 collective-permute-done.6.refs_3_
  23.2 1.7 %restore.1 = (f32[50,4608]{1,0:T(8,128)}, f32[2,50,2,8,64]{4,3,2,1,0:T(8,128)}) custom-call(f32[50,128]{1,0:T(8,128)S(1)} %get-tuple-element.42.refs_0_, f32[50,128]{1,0:T(8,128)S(1)} %collective-permute-done.4.refs_1_, f32[50,128]{1,0:T(8,128)S(1)} %collective-permute-done.5.refs_2_, f32[50,128]{1,0:T(8,128)S(1)} %collective-permute-done.6.refs_3_, ...), custom_call_target="tpu_custom_call" | custom-call | tf_op jit(solution)/shard_map/restore/pallas_call | solution.py:385
  (1 shorter events, 0.0 us)
Async XLA Ops:
  3.6 3.7 %collective-permute-start = (f32[100,128]{1,0:T(8,128)S(1)}, f32[100,128]{1,0:T(8,128)S(1)}, u32[]{:S(2)}, u32[]{:S(2)}) collective-permute-start(f32[100,128]{1,0:T(8,128)S(1)} %get-tuple-element.32), channel_id=1, source_target_pairs={{0,4},{1,5},{4,0},{5,1},{8,12},{9,13},{12,8},{13,9},{2,6},{3,7},{6... | collective-permute-start | bytes 153608 | tf_op jit(solution)/shard_map/ppermute | solution.py:508
  4.9 4.2 %collective-permute-start.1 = (f32[100,128]{1,0:T(8,128)S(1)}, f32[100,128]{1,0:T(8,128)S(1)}, u32[]{:S(2)}, u32[]{:S(2)}) collective-permute-start(f32[100,128]{1,0:T(8,128)S(1)} %get-tuple-element.33), channel_id=1, source_target_pairs={{0,5},{1,4},{4,1},{5,0},{8,13},{9,12},{12,9},{13,8},{2,7},{3,6},{6... | collective-permute-start | bytes 153608 | tf_op jit(solution)/shard_map/ppermute | solution.py:508
  5.9 3.1 %collective-permute-start.2 = (f32[100,128]{1,0:T(8,128)S(1)}, f32[100,128]{1,0:T(8,128)S(1)}, u32[]{:S(2)}, u32[]{:S(2)}) collective-permute-start(f32[100,128]{1,0:T(8,128)S(1)} %get-tuple-element.34), channel_id=1, source_target_pairs={{0,1},{1,0},{4,5},{5,4},{8,9},{9,8},{12,13},{13,12},{2,3},{3,2},{6... | collective-permute-start | bytes 153608 | tf_op jit(solution)/shard_map/ppermute | solution.py:508
  9.6 5.8 %collective-permute-start.3 = (f32[150,128]{1,0:T(8,128)S(1)}, f32[150,128]{1,0:T(8,128)S(1)}, u32[]{:S(2)}, u32[]{:S(2)}) collective-permute-start(f32[150,128]{1,0:T(8,128)S(1)} %couple_across.1.after), channel_id=1, source_target_pairs={{0,8},{1,9},{4,12},{5,13},{8,0},{9,1},{12,4},{13,5},{2,10},{3,11},... | collective-permute-start | bytes 230408 | tf_op jit(solution)/shard_map/ppermute | solution.py:508
  11.5 8.9 %collective-permute-start.7 = (f32[150,128]{1,0:T(8,128)S(1)}, f32[150,128]{1,0:T(8,128)S(1)}, u32[]{:S(2)}, u32[]{:S(2)}) collective-permute-start(f32[150,128]{1,0:T(8,128)S(1)} %get-tuple-element.38.refs_4_), channel_id=1, source_target_pairs={{0,8},{1,9},{4,12},{5,13},{8,0},{9,1},{12,4},{13,5},{2,10},{3,11},... | collective-permute-start | bytes 230408 | tf_op jit(solution)/shard_map/ppermute | solution.py:508
  15.5 6.0 %collective-permute-start.4 = (f32[50,128]{1,0:T(8,128)S(1)}, f32[50,128]{1,0:T(8,128)S(1)}, u32[]{:S(2)}, u32[]{:S(2)}) collective-permute-start(f32[50,128]{1,0:T(8,128)S(1)} %get-tuple-element.43), channel_id=1, source_target_pairs={{0,5},{1,4},{4,1},{5,0},{8,13},{9,12},{12,9},{13,8},{2,7},{3,6},{6... | collective-permute-start | bytes 76808 | tf_op jit(solution)/shard_map/ppermute | solution.py:508
  19.9 3.3 %collective-permute-start.5 = (f32[50,128]{1,0:T(8,128)S(1)}, f32[50,128]{1,0:T(8,128)S(1)}, u32[]{:S(2)}, u32[]{:S(2)}) collective-permute-start(f32[50,128]{1,0:T(8,128)S(1)} %get-tuple-element.44), channel_id=1, source_target_pairs={{0,4},{1,5},{4,0},{5,1},{8,12},{9,13},{12,8},{13,9},{2,6},{3,7},{6... | collective-permute-start | bytes 76808 | tf_op jit(solution)/shard_map/ppermute | solution.py:508
  19.9 3.3 %collective-permute-start.6 = (f32[50,128]{1,0:T(8,128)S(1)}, f32[50,128]{1,0:T(8,128)S(1)}, u32[]{:S(2)}, u32[]{:S(2)}) collective-permute-start(f32[50,128]{1,0:T(8,128)S(1)} %get-tuple-element.45), channel_id=1, source_target_pairs={{0,1},{1,0},{4,5},{5,4},{8,9},{9,8},{12,13},{13,12},{2,3},{3,2},{6... | collective-permute-start | bytes 76808 | tf_op jit(solution)/shard_map/ppermute | solution.py:508
